TPU v7x, 32 devices: a whole 2x2x4 slice. The times are simulated.
32 devices in a mesh: dp: 8 (over z, y), mp: 4 (over x, core).
Axes of the slice: x: 2, y: 2, z: 4, core: 2. Of those that a mesh axis runs over, the one named last changes fastest.
Arguments:
- tokens: bfloat16 [64, 512, 768], P('dp', 'mp'), may hold values from -6 to 6
- cotangent: bfloat16 [64, 512, 768], P('dp', 'mp'), may hold values from -6 to 6
- lengths: int32 [64], P('dp'), may hold values from 256 to 512, as said below
- gain_attn: float32 [768], replicated, may hold values from 0.5 to 1.5
- gain_ff: float32 [768], replicated, may hold values from 0.5 to 1.5
- bias_table: float32 [32, 12], P(None, 'mp'), may hold values from -4 to 4
- w_query: float32 [768, 768], P('dp', 'mp'), may hold values from -0.109375 to 0.109375
- w_key: float32 [768, 768], P('dp', 'mp'), may hold values from -0.109375 to 0.109375
- w_value: float32 [768, 768], P('dp', 'mp'), may hold values from -0.21875 to 0.21875
- w_out_attn: float32 [768, 768], P('mp', 'dp'), may hold values from -0.875 to 0.875
- w_in_ff: float32 [768, 3072], P('dp', 'mp'), may hold values from -0.21875 to 0.21875
- w_out_ff: float32 [3072, 768], P('mp', 'dp'), may hold values from -0.109375 to 0.109375
Outputs:
- layer_out: bfloat16 [64, 512, 768], P('dp', 'mp')
- input_grad: bfloat16 [64, 512, 768], P('dp', 'mp')
- grad_gain_attn: float32 [768], replicated
- grad_gain_ff: float32 [768], replicated
- grad_bias_table: float32 [32, 12], P(None, 'mp')
- grad_query: float32 [768, 768], P('dp', 'mp')
- grad_key: float32 [768, 768], P('dp', 'mp')
- grad_value: float32 [768, 768], P('dp', 'mp')
- grad_out_attn: float32 [768, 768], P('mp', 'dp')
- grad_in_ff: float32 [768, 3072], P('dp', 'mp')
- grad_out_ff: float32 [3072, 768], P('mp', 'dp')
Inputs may be any that keep to these rules, and one draw needn't show every extreme that they name: `lengths`: each length is 256 or 512; among the 8 pairs of each aligned block at least one has 512 and one has 256.
All inputs are finite; a program needn't handle non-finite values.
Results may differ from a plain program's by a relative error of at most 0.018.
Values may be sent and summed in bfloat16 or wider, within the bound.
A program may use at most 256 MiB of HBM per device.

v0:
```python
import jax
import jax.numpy as jnp
import numpy as np
from jax import lax
from jax.sharding import PartitionSpec as P

epsilon = 1e-06
far_reach = 128
largest_bucket = lax.Precision.HIGHEST


def in_blocks(array, dim, length):
    lengths = array.shape
    tiles = array.reshape(*lengths[:dim], length, lengths[dim] // length, *lengths[dim + 1 :])
    return jnp.moveaxis(tiles, dim, 0)


def sent_and_summed(array, axis, dim):
    length = lax.axis_size(axis)
    tiles = lax.all_to_all(in_blocks(array, dim, length), axis, 0, 0, tiled=True)
    return jnp.sum(tiles.astype(jnp.float32), axis=0)


def bucket_table(pair_length, element_count):
    places = np.arange(pair_length)
    offset = places[None, :] - places[:, None]
    half_count = element_count // 2
    upper = (offset > 0).astype(np.int64) * half_count
    distance = np.abs(offset)
    exact_span = half_count // 2
    scaled = (
        np.log(np.maximum(distance, 1) / exact_span)
        / np.log(far_reach / exact_span)
        * (half_count - exact_span)
    )
    larger = np.minimum(exact_span + scaled.astype(np.int64), half_count - 1)
    return (upper + np.where(distance < exact_span, distance, larger)).astype(np.int32)


def bucket_onehot_matrix(pair_length, element_count):
    codes = jnp.asarray(bucket_table(pair_length, element_count))
    return (codes[None, :, :] == jnp.arange(element_count, dtype=jnp.int32)[:, None, None]).astype(
        jnp.float32
    )


def lookup(position_bias_grid, pair_length):
    return jnp.einsum(
        "tlj,td->dlj",
        bucket_onehot_matrix(pair_length, position_bias_grid.shape[0]),
        position_bias_grid,
        precision=largest_bucket,
    )


def lookup_back(attention_score_totals, pair_length, element_count):
    return jnp.einsum(
        "wds,vds->wv",
        bucket_onehot_matrix(pair_length, element_count),
        attention_score_totals,
        precision=largest_bucket,
    )


def rms_norm(x, gain):
    scale = lax.rsqrt(jnp.mean(x * x, axis=-1, keepdims=True) + epsilon)
    return (x * scale * gain, scale)


def norm_back(x, scale, gain, upward):
    normed = x * scale
    gain_part = jnp.sum(upward * normed, axis=(0, 1))
    inner = upward * gain
    return (scale * (inner - normed * jnp.mean(inner * normed, axis=-1, keepdims=True)), gain_part)


def gather_rows(x):
    return lax.all_gather(x, "mp", axis=1, tiled=True)


def gather_grads(x):
    return lax.all_gather(x, "mp", axis=1, tiled=True)


def sum_rows(x):
    return lax.psum_scatter(x.astype(jnp.bfloat16), "mp", scatter_dimension=1, tiled=True).astype(
        jnp.float32
    )


def sum_grads(x):
    return lax.psum_scatter(x.astype(jnp.bfloat16), "mp", scatter_dimension=1, tiled=True).astype(
        jnp.float32
    )


def masked_scores(query, keys, biases, pair_length):
    scores = jnp.einsum("qhd,khd->hqk", query, keys, preferred_element_type=jnp.float32) + biases
    usable = jnp.arange(keys.shape[0]) < pair_length
    return jnp.where(usable[None, None, :], scores, -1e30)


def attention_forward(seen_one, w_joint, out_w, biases, lengths, pairs, seq_len, heads, head_dim):
    bfloat = jnp.bfloat16
    inner_width = heads * head_dim
    joint = jnp.dot(seen_one, w_joint, preferred_element_type=jnp.float32).astype(bfloat)
    query = joint[:, :inner_width].reshape(pairs, seq_len, heads, head_dim)
    keys = joint[:, inner_width : 2 * inner_width].reshape(pairs, seq_len, heads, head_dim)
    values = joint[:, 2 * inner_width :].reshape(pairs, seq_len, heads, head_dim)

    def attend(carry, element):
        query_seq, key_seq, value_seq, pair_length = element
        scores = masked_scores(query_seq, key_seq, biases, pair_length)
        top_score = jnp.max(scores, axis=-1, keepdims=True)
        expo = jnp.exp(scores - top_score)
        denom = jnp.sum(expo, axis=-1, keepdims=True)
        probs = expo / denom
        result = jnp.einsum(
            "hqk,khd->qhd", probs.astype(bfloat), value_seq, preferred_element_type=jnp.float32
        ).astype(bfloat)
        return (carry, (result, top_score[..., 0] + jnp.log(denom[..., 0])))

    unused, (attended, log_norm) = lax.scan(attend, 0, (query, keys, values, lengths))
    attended_flat = attended.reshape(pairs * seq_len, inner_width)
    attn_term = jnp.dot(attended_flat, out_w, preferred_element_type=jnp.float32).reshape(
        pairs, seq_len, out_w.shape[1]
    )
    return ((query, keys, values, attended_flat, log_norm), attn_term)


def attention_backward(
    seen_one, seen_grad, w_joint, out_w, saved, biases, lengths, pairs, seq_len, heads, head_dim
):
    bfloat = jnp.bfloat16
    query, keys, values, attended_flat, log_norm = saved
    rows = pairs * seq_len
    inner_width = heads * head_dim
    grad_out_w = jnp.dot(attended_flat.T, seen_grad, preferred_element_type=jnp.float32)
    grad_attended = (
        jnp.dot(seen_grad, out_w.T, preferred_element_type=jnp.float32)
        .astype(bfloat)
        .reshape(pairs, seq_len, heads, head_dim)
    )

    def attend_back(score_sum, element):
        query_seq, key_seq, value_seq, grad_seq, norm_seq, pair_length = element
        scores = masked_scores(query_seq, key_seq, biases, pair_length)
        probs = jnp.exp(scores - norm_seq[:, :, None])
        grad_probs = jnp.einsum(
            "qhd,khd->hqk", grad_seq, value_seq, preferred_element_type=jnp.float32
        )
        grad_val = jnp.einsum(
            "hqk,qhd->khd", probs.astype(bfloat), grad_seq, preferred_element_type=jnp.float32
        ).astype(bfloat)
        grad_scores = (
            probs * (grad_probs - jnp.sum(probs * grad_probs, axis=-1, keepdims=True))
        ).astype(bfloat)
        grad_que = jnp.einsum(
            "hqk,khd->qhd", grad_scores, key_seq, preferred_element_type=jnp.float32
        ).astype(bfloat)
        grad_keys = jnp.einsum(
            "hqk,qhd->khd", grad_scores, query_seq, preferred_element_type=jnp.float32
        ).astype(bfloat)
        return (score_sum + grad_scores.astype(jnp.float32), (grad_que, grad_keys, grad_val))

    score_start = jnp.zeros((heads, seq_len, seq_len), jnp.float32)
    attention_score_totals, (grad_que, grad_keys, grad_val) = lax.scan(
        attend_back, score_start, (query, keys, values, grad_attended, log_norm, lengths)
    )
    grad_joint = jnp.concatenate(
        [
            grad_que.reshape(rows, inner_width),
            grad_keys.reshape(rows, inner_width),
            grad_val.reshape(rows, inner_width),
        ],
        axis=1,
    )
    grad_w_joint = jnp.dot(seen_one.T, grad_joint, preferred_element_type=jnp.float32)
    normed_term = jnp.dot(grad_joint, w_joint.T, preferred_element_type=jnp.float32).reshape(
        pairs, seq_len, w_joint.shape[0]
    )
    return (grad_out_w, grad_w_joint, normed_term, attention_score_totals)


def body(
    tokens,
    cotangent,
    lengths,
    gain_attn,
    gain_ff,
    bias_table,
    w_query,
    w_key,
    w_value,
    w_out_attn,
    w_in_ff,
    w_out_ff,
):
    bfloat = jnp.bfloat16
    pairs, rows_local, width = tokens.shape
    parts_mp = lax.axis_size("mp")
    seq_len = rows_local * parts_mp
    heads_local = bias_table.shape[1]
    head_dim = w_query.shape[1] // heads_local
    rows_all = pairs * seq_len
    x = tokens.astype(jnp.float32)
    normed_one, scale_one = rms_norm(x, gain_attn)
    normed_one_low = normed_one.astype(bfloat)
    query_w, key_w, value_w, out_w = (
        lax.all_gather(w_query.astype(bfloat), "dp", axis=0, tiled=True),
        lax.all_gather(w_key.astype(bfloat), "dp", axis=0, tiled=True),
        lax.all_gather(w_value.astype(bfloat), "dp", axis=0, tiled=True),
        lax.all_gather(w_out_attn.astype(bfloat), "dp", axis=1, tiled=True),
    )
    seen_one = gather_rows(normed_one_low).reshape(rows_all, width)
    heads_here = bias_table.shape[1]
    w_joint = jnp.concatenate([query_w, key_w, value_w], axis=1)
    biases = lookup(bias_table, seq_len)
    saved, attn_term = attention_forward(
        seen_one, w_joint, out_w, biases, lengths, pairs, seq_len, heads_here, head_dim
    )
    hidden = x + sum_rows(attn_term)
    normed_two, scale_two = rms_norm(hidden, gain_ff)
    normed_two_low = normed_two.astype(bfloat)
    upstream = cotangent.astype(jnp.float32)
    in_w, feedforward_output = (
        lax.all_gather(w_in_ff.astype(bfloat), "dp", axis=0, tiled=True),
        lax.all_gather(w_out_ff.astype(bfloat), "dp", axis=1, tiled=True),
    )
    seen_two = gather_rows(normed_two_low).reshape(rows_all, width)
    pre_act = jnp.dot(seen_two, in_w, preferred_element_type=jnp.float32)
    acted = jax.nn.gelu(pre_act).astype(bfloat)
    ff_term = jnp.dot(acted, feedforward_output, preferred_element_type=jnp.float32).reshape(
        pairs, seq_len, width
    )
    layer = hidden + sum_rows(ff_term)
    seen_upstream = gather_grads(cotangent).reshape(rows_all, width)
    grad_wout = jnp.dot(acted.T, seen_upstream, preferred_element_type=jnp.float32)
    grad_acted = jnp.dot(seen_upstream, feedforward_output.T, preferred_element_type=jnp.float32)
    grad_pre = jax.vjp(jax.nn.gelu, pre_act)[1](grad_acted)[0].astype(bfloat)
    grad_win = jnp.dot(seen_two.T, grad_pre, preferred_element_type=jnp.float32)
    grad_normed_two = sum_grads(
        jnp.dot(grad_pre, in_w.T, preferred_element_type=jnp.float32).reshape(pairs, seq_len, width)
    )
    grad_in_ff, grad_out_ff = (
        sent_and_summed(grad_win.astype(jnp.bfloat16), "dp", 0),
        sent_and_summed(grad_wout.astype(jnp.bfloat16), "dp", 1),
    )
    grad_norm_two, gain_ff_part = norm_back(hidden, scale_two, gain_ff, grad_normed_two)
    grad_hidden = upstream + grad_norm_two
    grad_hidden_low = grad_hidden.astype(bfloat)
    seen_grad = gather_grads(grad_hidden_low).reshape(rows_all, width)
    grad_out_w, grad_w_joint, normed_term, attention_score_totals = attention_backward(
        seen_one,
        seen_grad,
        w_joint,
        out_w,
        saved,
        biases,
        lengths,
        pairs,
        seq_len,
        heads_here,
        head_dim,
    )
    inner_here = heads_here * head_dim
    grad_q_full = grad_w_joint[:, :inner_here]
    grad_k_full = grad_w_joint[:, inner_here : 2 * inner_here]
    grad_v_full = grad_w_joint[:, 2 * inner_here :]
    table_grad = lookup_back(attention_score_totals, seq_len, bias_table.shape[0])
    head_start = lax.axis_index("mp") * heads_local
    gradient_first_normed = sum_grads(normed_term)
    grad_query, grad_key, grad_value, grad_out_attn = (
        lax.psum_scatter(grad_q_full, "dp", scatter_dimension=0, tiled=True),
        lax.psum_scatter(grad_k_full, "dp", scatter_dimension=0, tiled=True),
        lax.psum_scatter(grad_v_full, "dp", scatter_dimension=0, tiled=True),
        lax.psum_scatter(grad_out_w, "dp", scatter_dimension=1, tiled=True),
    )
    every_head = jnp.zeros((bias_table.shape[0], heads_local * parts_mp), jnp.float32)
    every_head = lax.dynamic_update_slice_in_dim(every_head, table_grad, head_start, 1)
    grad_norm_one, gain_attn_part = norm_back(x, scale_one, gain_attn, gradient_first_normed)
    input_grad = (grad_hidden + grad_norm_one).astype(bfloat)
    grad_gain_attn, grad_gain_ff, table_all = lax.psum(
        (gain_attn_part, gain_ff_part, every_head), ("dp", "mp")
    )
    grad_bias_table = lax.dynamic_slice_in_dim(table_all, head_start, heads_local, 1)
    return (
        layer.astype(bfloat),
        input_grad,
        grad_gain_attn,
        grad_gain_ff,
        grad_bias_table,
        grad_query,
        grad_key,
        grad_value,
        grad_out_attn,
        grad_in_ff,
        grad_out_ff,
    )


def solution(mesh):
    placed = (
        P("dp", "mp", None),
        P("dp", "mp", None),
        P("dp"),
        P(),
        P(),
        P(None, "mp"),
        P("dp", "mp"),
        P("dp", "mp"),
        P("dp", "mp"),
        P("mp", "dp"),
        P("dp", "mp"),
        P("mp", "dp"),
    )
    return jax.shard_map(
        body,
        mesh=mesh,
        in_specs=placed,
        out_specs=(
            P("dp", "mp", None),
            P("dp", "mp", None),
            P(),
            P(),
            P(None, "mp"),
            P("dp", "mp"),
            P("dp", "mp"),
            P("dp", "mp"),
            P("mp", "dp"),
            P("dp", "mp"),
            P("mp", "dp"),
        ),
        check_vma=False,
    )
```

profile of v0, /device:TPU:1, one launch (start us, length us, event | category | flops | bytes accessed | tf_op | source)
XLA Modules:
  0.0 1094.8 jit_solution(6340226721429164682)
XLA Ops:
  16.3 11.5 %fusion.78 = f32[3,512,512]{2,0,1:T(4,128)} fusion(s32[512,512]{1,0:T(8,128)S(1)} %copy-done.34, f32[32,3]{0,1:T(4,128)S(1)} %copy-done), kind=kOutput, calls=%fused_computation.106 | convolution fusion | flops 310378496 | bytes 4194688 | tf_op jit(solution)/shard_map/tlj,td->dlj/dot_general | solution.py:48
  31.2 26.4 %all_gather.34 = bf16[192,768]{0,1:T(8,128)(2,1)S(1)} all-gather(bf16[192,96]{0,1:T(8,128)(2,1)} %copy.71), channel_id=1, replica_groups=mesh['dp'=8,'mp'=4] {'dp'}, dimensions={1}, use_global_device_ids=true | all-gather | bytes 331776 | tf_op jit(solution)/shard_map/all_gather | solution.py:213
  57.7 27.6 %all_gather.33 = bf16[768,192]{1,0:T(8,128)(2,1)} all-gather(bf16[96,192]{1,0:T(8,128)(2,1)} %convert_element_type.138), channel_id=1, replica_groups=mesh['dp'=8,'mp'=4] {'dp'}, dimensions={0}, use_global_device_ids=true | all-gather | bytes 331776 | tf_op jit(solution)/shard_map/all_gather | solution.py:212
  85.3 27.3 %all_gather.32 = bf16[768,192]{1,0:T(8,128)(2,1)} all-gather(bf16[96,192]{1,0:T(8,128)(2,1)} %convert_element_type.137), channel_id=1, replica_groups=mesh['dp'=8,'mp'=4] {'dp'}, dimensions={0}, use_global_device_ids=true | all-gather | bytes 331776 | tf_op jit(solution)/shard_map/all_gather | solution.py:211
  112.6 27.0 %all_gather.31 = bf16[768,192]{1,0:T(8,128)(2,1)} all-gather(bf16[96,192]{1,0:T(8,128)(2,1)} %convert_element_type.136), channel_id=1, replica_groups=mesh['dp'=8,'mp'=4] {'dp'}, dimensions={0}, use_global_device_ids=true | all-gather | bytes 331776 | tf_op jit(solution)/shard_map/all_gather | solution.py:210
  139.6 7.1 convolution_convert_fusion.5
  155.2 51.3 %while.29 = (s32[]{:T(128)}, bf16[8,512,3,64]{1,3,2,0:T(8,128)(2,1)}, f32[8,3,512]{2,1,0:T(4,128)}, bf16[8,512,3,64]{1,3,2,0:T(8,128)(2,1)}, s32[8]{0:T(128)S(1)...) while((s32[]{:T(128)}, ...), condition=%wide.region_4.5_spmd, body=%wide.region_1.4_spmd.sunk | while | flops 207715328 | bytes 13423737 | solution.py:123
  206.5 5.9 convolution_convert_fusion.7
  216.7 79.6 %reduce-scatter.17.cloned.1.call-done = bf16[8,128,768]{2,1,0:T(8,128)(2,1)} async-done(((bf16[8,512,768]{2,1,0:T(8,128)(2,1)}), bf16[8,128,768]{2,1,0:T(8,128)(2,1)}) %reduce-scatter.17.cloned.1.call-update) | async-done | bytes 1572880 | tf_op jit(solution)/shard_map/reduce_scatter | solution.py:86
  301.0 29.4 %all-gather.15.cloned.1.call-done = bf16[8,512,768]{2,1,0:T(8,128)(2,1)} async-done(((bf16[8,128,768]{2,1,0:T(8,128)(2,1)}), bf16[8,512,768]{2,1,0:T(8,128)(2,1)}) %all-gather.15.cloned.1.call-update) | async-done | bytes 6291472 | tf_op jit(solution)/shard_map/all_gather | solution.py:82
  330.4 10.1 fusion.88
  340.5 32.2 %all-gather.11.cloned.1.call-done = bf16[768,768]{1,0:T(8,128)(2,1)} async-done(((bf16[96,768]{1,0:T(8,128)(2,1)}), bf16[768,768]{1,0:T(8,128)(2,1)}) %all-gather.11.cloned.1.call-update) | async-done | bytes 1179664 | tf_op jit(solution)/shard_map/all_gather | solution.py:227
  372.7 48.9 %all-gather.9.cloned.1.call-done = bf16[8,512,768]{2,1,0:T(8,128)(2,1)} async-done(((bf16[8,128,768]{2,1,0:T(8,128)(2,1)}), bf16[8,512,768]{2,1,0:T(8,128)(2,1)}) %all-gather.9.cloned.1.call-update) | async-done | bytes 6291472 | tf_op jit(solution)/shard_map/all_gather | solution.py:78
  421.6 20.9 %fusion.58 = (bf16[4096,768]{1,0:T(8,128)(2,1)S(1)}, f32[4096,768]{1,0:T(8,128)}) fusion(f32[4096,768]{1,0:T(8,128)} %fusion.88, bf16[4096,768]{1,0:T(8,128)(2,1)} %bitcast.222, bf16[768,768]{1,0:T(8,128)(2,1)} %all-gather.11.cloned.1.call-done), kind=kOutput, calls=%fused_computation.68 | convolution fusion | flops 4894752768 | bytes 38928384 | tf_op jit(solution)/shard_map/dot_general | solution.py:231
  442.4 7.1 convolution_convert_fusion.3
  450.0 57.7 %reduce-scatter.21.cloned.1.call-done = bf16[8,128,768]{2,1,0:T(8,128)(2,1)} async-done(((bf16[8,512,768]{2,1,0:T(8,128)(2,1)}), bf16[8,128,768]{2,1,0:T(8,128)(2,1)}) %reduce-scatter.21.cloned.1.call-update) | async-done | bytes 1572880 | tf_op jit(solution)/shard_map/reduce_scatter | solution.py:92
  520.1 42.6 %all-gather.17.cloned.1.call-done = bf16[8,512,768]{2,1,0:T(8,128)(2,1)} async-done(((bf16[8,128,768]{2,1,0:T(8,128)(2,1)}), bf16[8,512,768]{2,1,0:T(8,128)(2,1)}) %all-gather.17.cloned.1.call-update) | async-done | bytes 6291472 | tf_op jit(solution)/shard_map/all_gather | solution.py:82
  562.7 6.3 convolution_convert_fusion.6
  580.2 116.5 %while.30 = (s32[]{:T(128)}, f32[3,512,512]{1,2,0:T(8,128)}, bf16[8,512,3,64]{1,3,2,0:T(8,128)(2,1)}, bf16[8,512,3,64]{1,3,2,0:T(8,128)(2,1)}, bf16[8,512,3,64]{...) while((s32[]{:T(128)}, f32[3,512,512]{1,2,0:T(8,128)}, ...), condition=%wide.region_12.13_spmd.clone, body=%wide.region_10.12_spmd.clone.sunk | while | flops 513047552 | bytes 60199136 | solution.py:167
  704.2 7.6 convolution_convert_fusion.2
  713.0 12.2 %convolution_convert_fusion.4 = bf16[4096,768]{1,0:T(8,128)(2,1)} fusion(bf16[768,768]{0,1:T(8,128)(2,1)S(1)} %copy-done.30, f32[4096,768]{1,0:T(8,128)} %get-tuple-element.319), kind=kOutput, calls=%fused_computation.72 | convolution fusion | flops 4863295488 | bytes 20054016 | tf_op jit(solution)/shard_map/dot_general | solution.py:233
  725.3 12.6 %convolution_convert_fusion.8 = bf16[768,768]{0,1:T(8,128)(2,1)} fusion(bf16[4096,768]{1,0:T(8,128)(2,1)} %bitcast.221, f32[4096,768]{1,0:T(8,128)} %get-tuple-element.319), kind=kOutput, calls=%fused_computation.107 | convolution fusion | flops 4860739584 | bytes 20054016 | tf_op jit(solution)/shard_map/dot_general | solution.py:238
  743.4 9.9 convolution_convert_fusion.9
  753.3 21.4 %all-to-all-done.1 = bf16[8,768,96]{1,2,0:T(8,128)(2,1)S(1)} async-done(((bf16[8,768,96]{1,2,0:T(8,128)(2,1)}), bf16[8,768,96]{1,2,0:T(8,128)(2,1)S(1)}, u32[]{:S(2)}, u32[]{:S(2)}) %all-to-all-start.1) | async-done | bytes 1179680 | tf_op jit(solution)/shard_map/all_to_all | solution.py:20
  779.1 9.0 fusion.89
  795.3 10.9 all-to-all-done
  814.1 17.6 %fusion.79 = f32[32,3]{0,1:T(4,128)S(1)} fusion(f32[3,512,512]{2,0,1:T(4,128)} %copy.81, s32[512,512]{1,0:T(8,128)} %constant.76.clone), kind=kOutput, calls=%fused_computation.110 | convolution fusion | flops 310378496 | bytes 4194688 | tf_op jit(solution)/shard_map/wds,vds->wv/dot_general | solution.py:57
  836.4 39.8 %all-reduce = (f32[768]{0:T(1024)}, f32[768]{0:T(1024)}, f32[32,12]{0,1:T(8,128)S(1)}) all-reduce(f32[768]{0:T(1024)S(1)} %get-tuple-element.259, f32[768]{0:T(1024)S(1)} %copy-done.29, f32[32,12]{0,1:T(8,128)S(1)} %dynamic_update_slice.20), channel_id=1, replica_groups=mesh['dp'=8,'mp'=4] {'dp','mp'}, use_global_device_ids=true, to_apply=%region_16.17 | all-reduce | flops 1920 | bytes 15360 | tf_op jit(solution)/shard_map/psum | solution.py:283
  876.8 13.8 %reduce-scatter.19.cloned.1.call-done = bf16[8,128,768]{2,1,0:T(8,128)(2,1)} async-done(((bf16[8,512,768]{2,1,0:T(8,128)(2,1)}), bf16[8,128,768]{2,1,0:T(8,128)(2,1)}) %reduce-scatter.19.cloned.1.call-update) | async-done | bytes 1572880 | tf_op jit(solution)/shard_map/reduce_scatter | solution.py:86
  896.4 59.3 %reduce-scatter.29.cloned.1.call-done = f32[96,192]{1,0:T(8,128)} async-done(((f32[768,192]{1,0:T(8,128)}), f32[96,192]{1,0:T(8,128)}) %reduce-scatter.29.cloned.1.call-update) | async-done | bytes 73744
  955.7 65.5 %reduce-scatter.27.cloned.1.call-done = f32[96,192]{1,0:T(8,128)} async-done(((f32[768,192]{1,0:T(8,128)}), f32[96,192]{1,0:T(8,128)}) %reduce-scatter.27.cloned.1.call-update) | async-done | bytes 73744
  1021.2 65.8 %reduce-scatter.25.cloned.1.call-done = f32[96,192]{1,0:T(8,128)} async-done(((f32[768,192]{1,0:T(8,128)}), f32[96,192]{1,0:T(8,128)}) %reduce-scatter.25.cloned.1.call-update) | async-done | bytes 73744
  (311 shorter events, 264.8 us)
Async XLA Ops:
  8.0 8.3 copy-start
  8.0 6.9 copy-start.23
  8.1 7.5 copy-start.24
  8.1 8.2 copy-start.34
  8.1 131.5 %all-gather.7.cloned.1.call-start = ((), (), s32[]{:S(2)}) async-start(), calls=%async_computation.10 | async-start | bytes 7864320 | tf_op jit(solution)/shard_map/all_gather | solution.py:78
  13.6 282.7 %reduce-scatter.17.cloned.1.call-start = ((), (), s32[]{:S(2)}) async-start(), calls=%async_computation.11 | async-start | bytes 7864320 | tf_op jit(solution)/shard_map/reduce_scatter | solution.py:86
  212.4 86.5 %copy-start.25 = (f32[768]{0:T(1024)S(1)}, f32[768]{0:T(1024)}, u32[]{:S(2)}) copy-start(f32[768]{0:T(1024)} %param.22) | copy-start | bytes 9220
  212.4 88.5 %all-gather.13.cloned.1.call-start = ((), (), s32[]{:S(2)}) async-start(), calls=%async_computation.14 | async-start | bytes 1327104 | tf_op jit(solution)/shard_map/all_gather | solution.py:228
  214.2 116.2 %all-gather.15.cloned.1.call-start = ((), (), s32[]{:S(2)}) async-start(), calls=%async_computation.16 | async-start | bytes 7864320 | tf_op jit(solution)/shard_map/all_gather | solution.py:82
  214.7 157.9 %all-gather.11.cloned.1.call-start = ((), (), s32[]{:S(2)}) async-start(), calls=%async_computation.13 | async-start | bytes 1327104 | tf_op jit(solution)/shard_map/all_gather | solution.py:227
  216.5 205.1 %all-gather.9.cloned.1.call-start = ((), (), s32[]{:S(2)}) async-start(), calls=%async_computation.12 | async-start | bytes 7864320 | tf_op jit(solution)/shard_map/all_gather | solution.py:78
  300.9 206.8 %reduce-scatter.21.cloned.1.call-start = ((), (), s32[]{:S(2)}) async-start(), calls=%async_computation.17 | async-start | bytes 7864320 | tf_op jit(solution)/shard_map/reduce_scatter | solution.py:92
  421.6 20.9 %copy-start.31 = (bf16[768,768]{1,0:T(8,128)(2,1)S(1)}, bf16[768,768]{1,0:T(8,128)(2,1)}, u32[]{:S(2)}) copy-start(bf16[768,768]{1,0:T(8,128)(2,1)} %all-gather.11.cloned.1.call-done) | copy-start | bytes 3538948
  442.4 7.1 copy-start.35
  449.6 113.1 %all-gather.17.cloned.1.call-start = ((), (), s32[]{:S(2)}) async-start(), calls=%async_computation.18 | async-start | bytes 7864320 | tf_op jit(solution)/shard_map/all_gather | solution.py:82
  515.9 316.1 %reduce-scatter.31.cloned.1.call-start = ((), (), s32[]{:S(2)}) async-start(), calls=%async_computation.23 | async-start | bytes 884736
  602.8 6.7 copy-start.3
  699.7 134.0 %reduce-scatter.23.cloned.1.call-start = ((), (), s32[]{:S(2)}) async-start(), calls=%async_computation.19 | async-start | bytes 7864320 | tf_op jit(solution)/shard_map/reduce_scatter | solution.py:92
  704.2 7.6 copy-start.17
  711.8 178.9 %reduce-scatter.19.cloned.1.call-start = ((), (), s32[]{:S(2)}) async-start(), calls=%async_computation.15 | async-start | bytes 7864320 | tf_op jit(solution)/shard_map/reduce_scatter | solution.py:86
  737.8 36.8 %all-to-all-start.1 = ((bf16[8,768,96]{1,2,0:T(8,128)(2,1)}), bf16[8,768,96]{1,2,0:T(8,128)(2,1)S(1)}, u32[]{:S(2)}, u32[]{:S(2)}) async-start(bf16[8,768,96]{1,2,0:T(8,128)(2,1)} %bitcast.21), calls=%async_computation.5 | async-start | bytes 2359296 | tf_op jit(solution)/shard_map/all_to_all | solution.py:20
  774.7 13.4 %copy-start.15 = (bf16[8,768,96]{1,2,0:T(8,128)(2,1)}, bf16[8,768,96]{1,2,0:T(8,128)(2,1)S(1)}, u32[]{:S(2)}) copy-start(bf16[8,768,96]{1,2,0:T(8,128)(2,1)S(1)} %all-to-all-done.1) | copy-start | bytes 3538948
  774.7 31.5 %all-to-all-start = ((bf16[8,96,768]{2,1,0:T(8,128)(2,1)}), bf16[8,96,768]{2,1,0:T(8,128)(2,1)}, u32[]{:S(2)}, u32[]{:S(2)}) async-start(bf16[8,96,768]{2,1,0:T(8,128)(2,1)} %bitcast.19), calls=%async_computation.4 | async-start | bytes 2359296 | tf_op jit(solution)/shard_map/all_to_all | solution.py:20
  779.0 176.7 %reduce-scatter.29.cloned.1.call-start = ((), (), s32[]{:S(2)}) async-start(), calls=%async_computation.22 | async-start | bytes 884736
  790.5 230.8 %reduce-scatter.27.cloned.1.call-start = ((), (), s32[]{:S(2)}) async-start(), calls=%async_computation.21 | async-start | bytes 884736
  790.5 20.1 %copy-start.4 = (f32[3,512,512]{1,2,0:T(8,128)S(1)}, f32[3,512,512]{1,2,0:T(8,128)}, u32[]{:S(2)}) copy-start(f32[3,512,512]{1,2,0:T(8,128)} %get-tuple-element.124) | copy-start | bytes 9437188
  792.9 294.0 %reduce-scatter.25.cloned.1.call-start = ((), (), s32[]{:S(2)}) async-start(), calls=%async_computation.20 | async-start | bytes 884736
  814.1 19.6 %copy-start.7 = (bf16[8,128,768]{2,1,0:T(8,128)(2,1)S(1)}, bf16[8,128,768]{2,1,0:T(8,128)(2,1)}, u32[]{:S(2)}) copy-start(bf16[8,128,768]{2,1,0:T(8,128)(2,1)} %param.18) | copy-start | bytes 4718596
  814.1 19.6 %copy-start.27 = (f32[8,128]{1,0:T(8,128)S(1)}, f32[8,128]{1,0:T(8,128)}, u32[]{:S(2)}) copy-start(f32[8,128]{1,0:T(8,128)} %copy-done.26) | copy-start | bytes 12292
  814.1 19.6 %copy-start.28 = (f32[768]{0:T(1024)S(1)}, f32[768]{0:T(1024)}, u32[]{:S(2)}) copy-start(f32[768]{0:T(1024)} %param.21) | copy-start | bytes 9220
  831.8 58.9 %copy-start.10 = (bf16[8,128,768]{2,1,0:T(8,128)(2,1)S(1)}, bf16[8,128,768]{2,1,0:T(8,128)(2,1)}, u32[]{:S(2)}) copy-start(bf16[8,128,768]{2,1,0:T(8,128)(2,1)} %reduce-scatter.17.cloned.1.call-done) | copy-start | bytes 4718596
  890.7 196.3 %copy-start.1 = (f32[32,3]{0,1:T(4,128)S(1)}, f32[32,3]{0,1:T(4,128)}, u32[]{:S(2)}) copy-start(f32[32,3]{0,1:T(4,128)} %param.23) | copy-start | bytes 1156
  (34 other events, 130.8 us)
Sparse Core Ops, SparseCore 0:
  13.7 48.8 all-gather.6
  212.5 83.7 reduce-scatter.16
  449.7 57.9 reduce-scatter.20
Sparse Core Ops, SparseCore 1:
  215.7 65.4 all-gather.12
  282.5 47.8 all-gather.14
  333.0 39.6 all-gather.10
  374.9 46.6 all-gather.8
  516.0 46.6 all-gather.16
  699.8 71.5 reduce-scatter.30
  773.9 55.2 reduce-scatter.22
  831.6 59.0 reduce-scatter.18
  894.8 60.9 reduce-scatter.28
  959.6 61.6 reduce-scatter.26
  1025.3 61.6 reduce-scatter.24
where the time goes:
time: 1100 us; the launch traced here: 1090 us
  waiting for transfers between devices  528 us (48%)
  matrix products  260 us (24%)
  blocking collectives  148 us (13%)
  other arithmetic  68.9 us (6%)
  local copies, waits for them, and re-layouts  61.8 us (6%)
  between operations  16.4 us (1%)
  starting transfers between devices  11.1 us (1%)
    unnamed x18, waiting for transfers between devices  191 us
    reduce_scatter x2, waiting for transfers between devices, sum_rows(): lax.psum_scatter(x.astype(jnp.bfloat16), 'mp', scatter_dimension=1, tiled...  93.5 us
    all_gather x2, waiting for transfers between devices, gather_grads(): return lax.all_gather(x, 'mp', axis=1, tiled=True)  72 us
    reduce_scatter x2, waiting for transfers between devices, sum_grads(): lax.psum_scatter(x.astype(jnp.bfloat16), 'mp', scatter_dimension=1, tiled...  57.7 us
    all_gather x2, waiting for transfers between devices, gather_rows(): return lax.all_gather(x, 'mp', axis=1, tiled=True)  48.9 us
    psum x1, blocking collectives, body(): lax.psum((gain_attn_part, gain_ff_part, every_head), ('dp', 'mp'))  39.8 us
    dot_general x16, matrix products, masked_scores(): jnp.einsum('qhd,khd->hqk', query, keys, preferred_element_type=jnp.float32)  34.1 us
    all_to_all x2, waiting for transfers between devices, sent_and_summed(): lax.all_to_all(in_blocks(array, dim, length), axis, 0, 0, tiled=True)  32.3 us
  transfers between devices with their start and end apart: 16, of which 12 were waited for; matrix products, arithmetic and copies ran while one was open for 13% of the time, Pallas kernels for 0%

commit v1 on v0

v1 whole, which is shorter than its diff:
```python
import functools

import jax
import jax.numpy as jnp
import numpy as np
from jax import lax
from jax.experimental import pallas as pl
from jax.experimental.pallas import tpu as pltpu
from jax.sharding import PartitionSpec as P

BF = jnp.bfloat16
F32 = jnp.float32
MESH = pl.DeviceIdType.MESH
EPS = 1e-06
FAR = 128
HIGHEST = lax.Precision.HIGHEST
MIB = 2**20


def bucket_of(offset, count):
    half = count // 2
    upper = (offset > 0).astype(np.int64) * half
    distance = np.abs(offset)
    exact = half // 2
    scaled = np.log(np.maximum(distance, 1) / exact) / np.log(FAR / exact) * (half - exact)
    larger = np.minimum(exact + scaled.astype(np.int64), half - 1)
    return (upper + np.where(distance < exact, distance, larger)).astype(np.int32)


class Place:
    def __init__(self, ndp, nmp):
        self.dp, self.mp = lax.axis_index("dp"), lax.axis_index("mp")
        self.x, self.c = self.mp // 2, self.mp % 2
        self.z, self.y = self.dp // 2, self.dp % 2
        self.nz = ndp // 2
        self.nmp = nmp

    def at(self, x=None, c=None, z=None, y=None):
        x = self.x if x is None else x
        c = self.c if c is None else c
        z = self.z if z is None else z
        y = self.y if y is None else y
        return (z * 2 + y, x * 2 + c)

    def greet(self):
        bar = pltpu.get_barrier_semaphore()

        def tell(who):
            pl.semaphore_signal(bar, inc=1, device_id=who, device_id_type=MESH)

        tell(self.at(c=1 - self.c))
        tell(self.at(x=1 - self.x))
        tell(self.at(x=1 - self.x, c=1 - self.c))
        tell(self.at(y=1 - self.y))

        def tell_z(k, carry):
            tell(self.at(z=lax.rem(self.z + k, self.nz)))
            return carry

        lax.fori_loop(1, self.nz, tell_z, 0)
        pl.semaphore_wait(bar, 4 + self.nz - 1)


def remote(src, dst, ssem, rsem, who):
    return pltpu.make_async_remote_copy(
        src_ref=src, dst_ref=dst, send_sem=ssem, recv_sem=rsem, device_id=who, device_id_type=MESH
    )


def loop(lo, hi, fn):
    def step(k, carry):
        fn(k)
        return carry

    lax.fori_loop(lo, hi, step, 0)


class Gather:
    def __init__(self, here, pack, order, W, ssem, rsem):
        self.h, self.order = here, order
        self.W = W.at[pack]
        self.ss, self.rs = ssem.at[pack], rsem.at[pack]

    def zi(self, k):
        return lax.rem(self.h.z + k, self.h.nz)

    def send(self, src, kind, idx, who, sidx=None):
        sidx = idx if sidx is None else sidx
        return remote(src, src, self.ss.at[kind, sidx], self.rs.at[kind, idx], who)

    def first_to(self, k):
        h = self.h
        if self.order == "xzy":
            return self.send(self.W.at[h.x, h.c, h.z, h.y], 0, 0, h.at(x=1 - h.x))
        z = self.zi(k)
        return self.send(self.W.at[h.x, h.c, h.z, h.y], 0, h.z, h.at(z=z), z)

    def first_from(self, k):
        h = self.h
        if self.order == "xzy":
            return self.send(self.W.at[1 - h.x, h.c, h.z, h.y], 0, 0, h.at(x=1 - h.x))
        z = self.zi(k)
        return self.send(self.W.at[h.x, h.c, z, h.y], 0, z, h.at(z=z), z)

    def second_to(self, k):
        h, z = self.h, self.zi(k)
        if self.order == "xzy":
            return self.send(self.W.at[:, h.c, h.z, h.y], 1, h.z, h.at(z=z), z)
        peer = h.at(x=1 - h.x) if self.order == "zxy" else h.at(y=1 - h.y)
        return self.send(self.W.at[h.x, h.c, z, h.y], 1, z, peer)

    def second_from(self, k):
        h, z = self.h, self.zi(k)
        if self.order == "xzy":
            return self.send(self.W.at[:, h.c, z, h.y], 1, z, h.at(z=z), z)
        if self.order == "zxy":
            return self.send(self.W.at[1 - h.x, h.c, z, h.y], 1, z, h.at(x=1 - h.x))
        return self.send(self.W.at[h.x, h.c, z, 1 - h.y], 1, z, h.at(y=1 - h.y))

    def third_to(self, half, k):
        h, z = self.h, self.zi(k)
        if self.order == "zyx":
            y = h.y if half == 0 else 1 - h.y
            return self.send(self.W.at[h.x, h.c, z, y], 2 + half, z, h.at(x=1 - h.x))
        x = h.x if half == 0 else 1 - h.x
        return self.send(self.W.at[x, h.c, z, h.y], 2 + half, z, h.at(y=1 - h.y))

    def third_from(self, half, k):
        h, z = self.h, self.zi(k)
        if self.order == "zyx":
            y = h.y if half == 0 else 1 - h.y
            return self.send(self.W.at[1 - h.x, h.c, z, y], 2 + half, z, h.at(x=1 - h.x))
        x = h.x if half == 0 else 1 - h.x
        return self.send(self.W.at[x, h.c, z, 1 - h.y], 2 + half, z, h.at(y=1 - h.y))

    def sib(self, half, k, c):
        h, z = self.h, self.zi(k)
        if self.order == "zyx":
            x = h.x if half == 0 else 1 - h.x
            block = self.W.at[x, c, z, :]
        else:
            y = h.y if half == 0 else 1 - h.y
            block = self.W.at[:, c, z, y]
        return self.send(block, 4 + half, z, h.at(c=1 - h.c))

    def start_first(self):
        if self.order == "xzy":
            self.first_to(0).start()
        else:
            loop(1, self.h.nz, lambda k: self.first_to(k).start())

    def after_first(self):
        nz = self.h.nz
        if self.order == "xzy":
            self.first_from(0).wait_recv()
            loop(1, nz, lambda k: self.second_to(k).start())
            self.third_to(0, 0).start()
            self.third_to(1, 0).start()
            self.sib(0, 0, self.h.c).start()
        else:

            def on(k):
                pl.when(k > 0)(lambda: self.first_from(k).wait_recv())
                self.second_to(k).start()
                self.third_to(0, k).start()

            loop(0, nz, on)

    def after_second(self):
        nz = self.h.nz
        if self.order == "xzy":

            def on(k):
                self.second_from(k).wait_recv()
                self.third_to(0, k).start()
                self.third_to(1, k).start()
                self.sib(0, k, self.h.c).start()

            loop(1, nz, on)
        else:

            def on(k):
                self.second_from(k).wait_recv()
                self.third_to(1, k).start()
                self.sib(0, k, self.h.c).start()

            loop(0, nz, on)

    def after_third(self):
        def on(k):
            self.third_from(0, k).wait_recv()
            self.third_from(1, k).wait_recv()
            self.sib(1, k, self.h.c).start()

        loop(0, self.h.nz, on)

    def finish(self):
        nz = self.h.nz

        def on(k):
            for half in (0, 1):
                self.sib(half, k, 1 - self.h.c).wait_recv()
                self.sib(half, k, self.h.c).wait_send()
                self.third_to(half, k).wait_send()

        loop(0, nz, on)
        if self.order == "xzy":
            self.first_to(0).wait_send()
            loop(1, nz, lambda k: self.second_to(k).wait_send())
        else:
            loop(1, nz, lambda k: self.first_to(k).wait_send())
            loop(0, nz, lambda k: self.second_to(k).wait_send())


class Swap:
    def __init__(self, here, src, dst, ssem, rsem, lsem, back):
        self.h, self.src, self.dst, self.ss, self.rs, self.ls, self.back = here, src, dst, ssem, rsem, lsem, back
        self.share = (dst if back else src).shape[0] // here.nmp

    def views(self, sender, receiver):
        src, dst = self.src, self.dst
        if self.back:
            return src.at[:, receiver], dst.at[pl.ds(sender * self.share, self.share)]
        return src.at[pl.ds(receiver * self.share, self.share)], dst.at[:, sender]

    def to(self, k):
        other = lax.rem(self.h.mp + k, self.h.nmp)
        src, dst = self.views(self.h.mp, other)
        return remote(src, dst, self.ss.at[k], self.rs.at[k], (self.h.dp, other))

    def come(self, k):
        other = lax.rem(self.h.mp + self.h.nmp - k, self.h.nmp)
        src, dst = self.views(other, self.h.mp)
        return remote(dst, dst, self.ss.at[k], self.rs.at[k], (self.h.dp, other))

    def local(self):
        src, dst = self.views(self.h.mp, self.h.mp)
        return pltpu.make_async_copy(src, dst, self.ls.at[0])

    def start(self):
        for k in range(1, self.h.nmp):
            self.to(k).start()
        self.local().start()

    def finish(self):
        for k in range(1, self.h.nmp):
            self.come(k).wait_recv()
            self.to(k).wait_send()
        self.local().wait()


def gather_kernel(ndp, nmp, own, tok, cot, bias, W, X, DY, BT, ssem, rsem, tsem, bsem, lsem):
    h = Place(ndp, nmp)
    h.greet()
    for p in range(3):
        pltpu.make_async_copy(own.at[p], W.at[p, h.x, h.c, h.z, h.y], lsem.at[p]).start()
    sx = Swap(h, tok, X, tsem.at[0], tsem.at[1], tsem.at[4], False)
    sd = Swap(h, cot, DY, tsem.at[2], tsem.at[3], tsem.at[5], False)
    for p in range(3):
        pltpu.make_async_copy(own.at[p], W.at[p, h.x, h.c, h.z, h.y], lsem.at[p]).wait()
    A = Gather(h, 0, "xzy", W, ssem, rsem)
    B = Gather(h, 1, "zxy", W, ssem, rsem)
    C = Gather(h, 2, "zyx", W, ssem, rsem)
    A.start_first()
    bts = []
    for k in range(1, nmp):
        other = lax.rem(h.mp + k, nmp)
        bts.append(remote(bias, BT.at[h.mp], bsem.at[0, k], bsem.at[1, k], (h.dp, other)))
        bts[-1].start()
    own_bias = pltpu.make_async_copy(bias, BT.at[h.mp], lsem.at[3])
    own_bias.start()
    sx.start()
    A.after_first()
    A.after_second()
    B.start_first()
    A.after_third()
    C.start_first()
    B.after_first()
    C.after_first()
    B.after_second()
    C.after_second()
    sx.finish()
    sd.start()
    A.finish()
    B.after_third()
    C.after_third()
    B.finish()
    C.finish()
    sd.finish()
    own_bias.wait()
    for k in range(1, nmp):
        other = lax.rem(h.mp + nmp - k, nmp)
        remote(bias, BT.at[other], bsem.at[0, k], bsem.at[1, k], (h.dp, other)).wait_recv()
        bts[k - 1].wait_send()


def gather_all(own, tok, cot, bias, ndp, nmp):
    n, rows, width = own.shape
    pairs, positions, _ = tok.shape
    nz = ndp // 2
    share = pairs // nmp
    any_ = pl.BlockSpec(memory_space=pl.ANY)
    dma = pltpu.SemaphoreType.DMA
    return pl.pallas_call(
        functools.partial(gather_kernel, ndp, nmp),
        out_shape=(
            jax.ShapeDtypeStruct((n, nmp // 2, 2, nz, 2, rows, width), BF),
            jax.ShapeDtypeStruct((share, nmp, positions, width), BF),
            jax.ShapeDtypeStruct((share, nmp, positions, width), BF),
            jax.ShapeDtypeStruct((nmp,) + bias.shape, F32),
        ),
        in_specs=[any_] * 4,
        out_specs=(any_,) * 4,
        scratch_shapes=[dma((n, 6, nz)), dma((n, 6, nz)), dma((6, nmp)), dma((2, nmp)), dma((4,))],
        compiler_params=pltpu.CompilerParams(collective_id=0, has_side_effects=True),
    )(own, tok, cot, bias)


class Scatter:
    def __init__(self, here, pack, G, mine, R0, R1, R2, R3, out, ssem, rsem, lsem):
        self.h, self.p = here, pack
        self.G, self.mine = G.at[pack], mine.at[pack]
        self.R0, self.R1, self.R2, self.R3, self.out = R0.at[pack], R1.at[pack], R2.at[pack], R3.at[pack], out
        self.ss, self.rs, self.ls = ssem.at[pack], rsem.at[pack], lsem.at[pack]

    def zi(self, k):
        return lax.rem(self.h.z + k, self.h.nz)

    def sib(self, x):
        h = self.h
        return remote(self.G.at[x, 1 - h.c], self.R0.at[x], self.ss.at[0, x], self.rs.at[0, x], h.at(c=1 - h.c))

    def local(self, x):
        return pltpu.make_async_copy(self.G.at[x, self.h.c], self.mine.at[x], self.ls.at[x])

    def ysend(self, k):
        h, z = self.h, self.zi(k)
        return remote(self.mine.at[:, z, 1 - h.y], self.R1.at[:, z], self.ss.at[1, z], self.rs.at[1, z], h.at(y=1 - h.y))

    def zsend(self, k):
        h, z = self.h, self.zi(k)
        return remote(self.R1.at[:, z], self.R2.at[h.z], self.ss.at[2, z], self.rs.at[2, h.z], h.at(z=z))

    def zcome(self, k):
        h, z = self.h, self.zi(k)
        return remote(self.R2.at[z], self.R2.at[z], self.ss.at[2, z], self.rs.at[2, z], h.at(z=z))

    def xsend(self):
        h = self.h
        return remote(self.R1.at[1 - h.x, h.z], self.R3, self.ss.at[3, 0], self.rs.at[3, 0], h.at(x=1 - h.x))

    def start(self):
        for x in range(2):
            self.local(x).start()
            self.sib(x).start()

    def after_sib(self):
        h = self.h
        for x in range(2):
            self.local(x).wait()
            self.sib(x).wait_recv()

        def on(k):
            z = self.zi(k)
            for y in (1 - h.y, h.y):
                for x in range(2):
                    self.mine[x, z, y] = (self.mine[x, z, y].astype(F32) + self.R0[x, z, y].astype(F32)).astype(BF)
                if y is not h.y:
                    self.ysend(k).start()

        loop(0, h.nz, on)

    def after_y(self):
        h = self.h

        def on(kk):
            k = lax.rem(kk + 1, h.nz)
            z = self.zi(k)
            self.ysend(k).wait_recv()
            for x in range(2):
                self.R1[x, z] = (self.mine[x, z, h.y].astype(F32) + self.R1[x, z].astype(F32)).astype(BF)
            pl.when(k > 0)(lambda: self.zsend(k).start())

        loop(0, h.nz, on)

    def after_z(self):
        h = self.h
        loop(1, h.nz, lambda k: self.zcome(k).wait_recv())

        def total(x):
            def add(k, acc):
                return acc + self.R2[self.zi(k), x].astype(F32)

            return lax.fori_loop(1, h.nz, add, self.R1[x, h.z].astype(F32))

        self.R1[1 - h.x, h.z] = total(1 - h.x).astype(BF)
        self.xsend().start()
        self.out[self.p] = total(h.x)

    def finish(self):
        h = self.h
        self.xsend().wait()
        self.out[self.p] += self.R3[...].astype(F32)
        for x in range(2):
            self.sib(x).wait_send()
        loop(0, h.nz, lambda k: self.ysend(k).wait_send())
        loop(1, h.nz, lambda k: self.zsend(k).wait_send())


def scatter_kernel(ndp, nmp, n, G, lay, ing, out, L, I, mine, R0, R1, R2, R3, ssem, rsem, lsem, tsem):
    h = Place(ndp, nmp)
    h.greet()
    packs = [Scatter(h, p, G, mine, R0, R1, R2, R3, out, ssem, rsem, lsem) for p in range(n)]
    sl = Swap(h, lay, L, tsem.at[0], tsem.at[1], tsem.at[4], True)
    si = Swap(h, ing, I, tsem.at[2], tsem.at[3], tsem.at[5], True)
    for s in packs:
        s.start()
    sl.start()
    for s in packs:
        s.after_sib()
    for s in packs:
        s.after_y()
    si.start()
    for s in packs:
        s.after_z()
    for s in packs:
        s.finish()
    sl.finish()
    si.finish()


def scatter_all(G, lay, ing, ndp, nmp):
    n, rows, width = G.shape[0], G.shape[-2], G.shape[-1]
    nz = ndp // 2
    share, _, positions, _ = lay.shape
    any_ = pl.BlockSpec(memory_space=pl.ANY)
    dma = pltpu.SemaphoreType.DMA
    back = jax.ShapeDtypeStruct((share * nmp, positions, width), BF)
    return pl.pallas_call(
        functools.partial(scatter_kernel, ndp, nmp, n),
        out_shape=(jax.ShapeDtypeStruct((n, rows, width), F32), back, back),
        in_specs=[any_] * 3,
        out_specs=(pl.BlockSpec(memory_space=pltpu.VMEM), any_, any_),
        scratch_shapes=[
            pltpu.VMEM((n, 2, nz, 2, rows, width), BF),
            pltpu.VMEM((n, 2, nz, 2, rows, width), BF),
            pltpu.VMEM((n, 2, nz, rows, width), BF),
            pltpu.VMEM((n, nz, 2, rows, width), BF),
            pltpu.VMEM((n, rows, width), BF),
            dma((n, 4, max(nz, 2))),
            dma((n, 4, max(nz, 2))),
            dma((n, 2)),
            dma((6, nmp)),
        ],
        compiler_params=pltpu.CompilerParams(collective_id=1, has_side_effects=True, vmem_limit_bytes=56 * MIB),
    )(G, lay, ing)


def dot(a, b, ca=1, cb=0):
    return lax.dot_general(a, b, (((ca,), (cb,)), ((), ())), preferred_element_type=F32)


def body(tokens, cotangent, lengths, gain_attn, gain_ff, bias_table, w_query, w_key, w_value, w_out_attn, w_in_ff, w_out_ff):
    ndp, nmp = lax.axis_size("dp"), lax.axis_size("mp")
    pairs, positions, width = tokens.shape
    seq = positions * nmp
    share = pairs // nmp
    buckets, heads_mp = bias_table.shape
    heads = heads_mp * nmp
    part = w_query.shape[1]
    dh = part // heads_mp
    rows = w_query.shape[0]
    padded = -(-rows // 16) * 16
    n = share * seq

    own = jnp.stack(
        [
            jnp.concatenate([w_query, w_key, w_value, w_out_attn.T], axis=1).astype(BF),
            w_in_ff.astype(BF),
            w_out_ff.T.astype(BF),
        ]
    )
    own = jnp.pad(own, ((0, 0), (0, padded - rows), (0, 0)))
    bias_own = jnp.zeros((8, 128), F32).at[:heads_mp, :buckets].set(bias_table.T)
    W, X, DY, BT = gather_all(own, tokens, cotangent, bias_own, ndp, nmp)
    W = W.reshape(3, nmp, ndp, padded, width)[:, :, :, :rows].reshape(3, nmp, width, width)
    A, B, C = W[0], W[1], W[2]
    table = BT[:, :heads_mp, :buckets].reshape(heads, buckets)
    lens = lax.dynamic_slice_in_dim(lengths, lax.axis_index("mp") * share, share)

    x = X.reshape(n, width).astype(F32)
    dy_low = DY.reshape(n, width)
    dy = dy_low.astype(F32)
    codes = bucket_of(np.arange(seq)[None, :] - np.arange(seq)[:, None], buckets)
    onehot = jnp.asarray(codes)[None] == jnp.arange(buckets, dtype=jnp.int32)[:, None, None]
    biases = jnp.einsum("hb,bij->hij", table, onehot.astype(F32), precision=HIGHEST)

    r1 = lax.rsqrt(jnp.mean(x * x, axis=-1, keepdims=True) + EPS)
    n1 = (x * r1 * gain_attn).astype(BF)
    qkv = [dot(n1, A[m][:, : 3 * part]).astype(BF) for m in range(nmp)]

    def cut(i):
        return jnp.stack([q[:, i * part : (i + 1) * part] for q in qkv], 1).reshape(share, seq, heads, dh)

    q, k, v = cut(0), cut(1), cut(2)
    s = jnp.einsum("pqhd,pkhd->phqk", q, k, preferred_element_type=F32) + biases[None]
    live = jnp.arange(seq)[None, :] < lens[:, None]
    s = jnp.where(live[:, None, None, :], s, -1e30)
    prob = jax.nn.softmax(s, axis=-1)
    plow = prob.astype(BF)
    o = jnp.einsum("phqk,pkhd->pqhd", plow, v, preferred_element_type=F32).astype(BF)
    om = o.reshape(n, nmp, part)
    att = sum(dot(om[:, m], A[m][:, 3 * part :], 1, 1) for m in range(nmp))
    h = x + att
    r2 = lax.rsqrt(jnp.mean(h * h, axis=-1, keepdims=True) + EPS)
    n2 = (h * r2 * gain_ff).astype(BF)
    ff = 0.0
    gn2 = 0.0
    g_in, g_out = [], []
    for m in range(nmp):
        a = dot(n2, B[m])
        u, back = jax.vjp(jax.nn.gelu, a)
        u = u.astype(BF)
        ff = ff + dot(u, C[m], 1, 1)
        g_out.append(dot(dy_low, u, 0, 0).astype(BF))
        ga = back(dot(dy_low, C[m]))[0].astype(BF)
        g_in.append(dot(n2, ga, 0, 0).astype(BF))
        gn2 = gn2 + dot(ga, B[m], 1, 1)
    layer = (h + ff).astype(BF)
    nh = h * r2
    gain_ff_part = jnp.sum(gn2 * nh, axis=0)
    e = gn2 * gain_ff
    gh = dy + r2 * (e - nh * jnp.mean(e * nh, axis=-1, keepdims=True))
    gh_low = gh.astype(BF)
    do = [dot(gh_low, A[m][:, 3 * part :]).astype(BF) for m in range(nmp)]
    do4 = jnp.stack(do, 1).reshape(share, seq, heads, dh)
    dP = jnp.einsum("pqhd,pkhd->phqk", do4, v, preferred_element_type=F32)
    gv = jnp.einsum("phqk,pqhd->pkhd", plow, do4, preferred_element_type=F32).astype(BF)
    gs = (prob * (dP - jnp.sum(prob * dP, axis=-1, keepdims=True))).astype(BF)
    gq = jnp.einsum("phqk,pkhd->pqhd", gs, k, preferred_element_type=F32).astype(BF)
    gk = jnp.einsum("phqk,pqhd->pkhd", gs, q, preferred_element_type=F32).astype(BF)
    gb = jnp.einsum("hij,bij->bh", jnp.sum(gs.astype(F32), 0), onehot.astype(F32), precision=HIGHEST)
    g_attn = []
    gn1 = 0.0
    for m in range(nmp):
        gm = jnp.concatenate([g.reshape(n, nmp, part)[:, m] for g in (gq, gk, gv)], 1)
        g_attn.append(jnp.concatenate([dot(n1, gm, 0, 0), dot(gh_low, om[:, m], 0, 0)], 1).astype(BF))
        gn1 = gn1 + dot(gm, A[m][:, : 3 * part], 1, 1)
    nx = x * r1
    gain_attn_part = jnp.sum(gn1 * nx, axis=0)
    e1 = gn1 * gain_attn
    ing = (gh + r1 * (e1 - nx * jnp.mean(e1 * nx, axis=-1, keepdims=True))).astype(BF)

    G = jnp.stack([jnp.stack(g_attn), jnp.stack(g_in), jnp.stack(g_out)]).reshape(3, nmp, ndp, rows, width)
    G = jnp.pad(G, ((0, 0), (0, 0), (0, 0), (0, padded - rows), (0, 0)))
    G = G.reshape(3, nmp // 2, 2, ndp // 2, 2, padded, width)
    S, layer_out, input_grad = scatter_all(
        G, layer.reshape(share, nmp, positions, width), ing.reshape(share, nmp, positions, width), ndp, nmp
    )
    S = S[:, :rows]
    sa = S[0]
    gga, ggf, gball = lax.psum((gain_attn_part, gain_ff_part, gb), ("dp", "mp"))
    gbt = lax.dynamic_slice_in_dim(gball, lax.axis_index("mp") * heads_mp, heads_mp, 1)
    return (
        layer_out,
        input_grad,
        gga,
        ggf,
        gbt,
        sa[:, :part],
        sa[:, part : 2 * part],
        sa[:, 2 * part : 3 * part],
        sa[:, 3 * part :].T,
        S[1],
        S[2].T,
    )


def solution(mesh):
    act = P("dp", "mp", None)
    rows, cols = P("dp", "mp"), P("mp", "dp")
    return jax.shard_map(
        body,
        mesh=mesh,
        in_specs=(act, act, P("dp"), P(), P(), P(None, "mp"), rows, rows, rows, cols, rows, cols),
        out_specs=(act, act, P(), P(), P(None, "mp"), rows, rows, rows, cols, rows, cols),
        check_vma=False,
    )
```

time: 1100 us -> 676 us (0.61)
  waiting for transfers between devices: 528 us -> 0 us
  Pallas kernels: 0 us -> 237 us
  blocking collectives: 148 us -> 41.7 us
  local copies, waits for them, and re-layouts: 61.8 us -> 119 us
  matrix products: 260 us -> 204 us
  between operations: 16.4 us -> 2.19 us
  starting transfers between devices: 11.1 us -> 0 us
    pallas_call x0 -> x2, Pallas kernels: none -> 237 us  [the longest x1 120 us: scatter_all(): pl.pallas_call(functools.partial(scatter_kernel, ndp, nmp, n), out_shape=...]
    unnamed x18 -> x0, waiting for transfers between devices: 191 us -> none
    all_gather x6 -> x0, waiting for transfers between devices: 153 us -> none  [the longest x2 72 us: gather_grads(): return lax.all_gather(x, 'mp', axis=1, tiled=True)]
    reduce_scatter x4 -> x0, waiting for transfers between devices: 151 us -> none  [the longest x2 93.5 us: sum_rows(): lax.psum_scatter(x.astype(jnp.bfloat16), 'mp', scatter_dimension=1, tiled...]
    all_gather x4 -> x0, blocking collectives: 108 us -> none  [the longest x1 27.6 us: body(): lax.all_gather(w_value.astype(bfloat), 'dp', axis=0, tiled=True)]
    dot_general x69 -> x55, matrix products: 256 us -> 184 us  [the longest x48 88.3 us: dot(): lax.dot_general(a, b, (((ca,), (cb,)), ((), ())), preferred_element_type=...]
    all_to_all x2 -> x0, waiting for transfers between devices: 32.3 us -> none  [sent_and_summed(): lax.all_to_all(in_blocks(array, dim, length), axis, 0, 0, tiled=True)]
    another operation x0 -> x11, other arithmetic: none -> 28.4 us  [the longest x1 11.4 us: body(): jnp.stack([jnp.stack(g_attn), jnp.stack(g_in), jnp.stack(g_out)])]
  transfers between devices with their start and end apart: 16 -> 0, of which waited for: 12 -> 0; matrix products, arithmetic and copies ran while one was open for 13% -> 0% of each run, Pallas kernels for 0% -> 0%
where the time goes in v1:
time: 676 us; the launch traced here: 667 us
  Pallas kernels  237 us (35%)
  matrix products  204 us (30%)
  local copies, waits for them, and re-layouts  119 us (18%)
  other arithmetic  63.1 us (9%)
  blocking collectives  41.7 us (6%)
    pallas_call x1, Pallas kernels, scatter_all(): pl.pallas_call(functools.partial(scatter_kernel, ndp, nmp, n), out_shape=...  120 us
    pallas_call x1, Pallas kernels, gather_all(): pl.pallas_call(functools.partial(gather_kernel, ndp, nmp), out_shape=(jax...  117 us
    dot_general x48, matrix products, dot(): lax.dot_general(a, b, (((ca,), (cb,)), ((), ())), preferred_element_type=...  88.3 us
    psum x1, blocking collectives, body(): gga, ggf, gball = lax.psum((gain_attn_part, gain_ff_part, gb), ('dp', 'mp'))  41.7 us
    reduce_sum x1, other arithmetic, body(): jnp.sum(gs.astype(F32), 0)  27.8 us
    sub x1, matrix products, body(): prob = jax.nn.softmax(s, axis=-1)  20.3 us
    dot_general x1, matrix products, body(): jnp.einsum('hij,bij->bh', jnp.sum(gs.astype(F32), 0), onehot.astype(F32),...  20.2 us
    dot_general x1, matrix products, body(): dP = jnp.einsum('pqhd,pkhd->phqk', do4, v, preferred_element_type=F32)  20 us

profile of v1, /device:TPU:1, one launch (start us, length us, event | category | flops | bytes accessed | tf_op | source)
XLA Modules:
  0.0 666.9 jit_solution(9119827079688177893)
XLA Ops:
  8.4 116.8 %shard_map.212 = (bf16[3,2,2,4,2,96,768]{6,5,4,3,2,1,0:T(8,128)(2,1)}, bf16[2,4,128,768]{3,2,1,0:T(8,128)(2,1)}, bf16[2,4,128,768]{3,2,1,0:T(8,128)(2,1)}, f32[4,8,128]{2,1,0:T(8,128)}) custom-call(bf16[3,96,768]{2,1,0:T(8,128)(2,1)} %pad_maximum_fusion.19.own, bf16[8,128,768]{2,1,0:T(8,128)(2,1)} %tok.1, bf16[8,128,768]{2,1,0:T(8,128)(2,1)} %cot.1, ...), custom_call_target="tpu_custom_call" | custom-call | tf_op jit(solution)/shard_map/pallas_call | solution.py:304
  125.3 11.8 %fusion.154 = (bf16[1,2,2,4,2,96,768]{6,5,4,3,2,1,0:T(8,128)(2,1)}, bf16[1,2,2,4,2,96,768]{6,5,4,3,2,1,0:T(8,128)(2,1)}, bf16[1,2,2,4,2,96,768]{6,5,4,3,2,1,0:T(8,128)(2,1)}) fusion(bf16[3,2,2,4,2,96,768]{6,5,4,3,2,1,0:T(8,128)(2,1)} %get-tuple-element.31), kind=kLoop, calls=%fused_computation.264 | loop fusion | bytes 28311552 | tf_op jit(solution)/shard_map/slice | solution.py:487
  138.0 3.2 slice_bitcast_fusion.11
  161.2 14.2 %fusion.2 = f32[12,512,512]{2,0,1:T(8,128)} fusion(f32[12,32,1]{1,0,2:T(8,128)S(1)} %reshape.369, s32[512,512]{1,0:T(8,128)} %constant.72.clone), kind=kOutput, calls=%fused_computation.3 | convolution fusion | flops 1216348160 | bytes 13633024 | tf_op jit(solution)/shard_map/hb,bij->hij/dot_general | solution.py:496
  175.5 17.8 %copy.66 = f32[12,512,512]{1,2,0:T(8,128)} copy(f32[12,512,512]{2,0,1:T(8,128)} %fusion.2) | data formatting | bytes 25165824 | tf_op jit(solution)/shard_map/hb,bij->hij/dot_general | solution.py:496
  193.3 20.3 %fusion.155 = (f32[2,12,512]{2,1,0:T(8,128)S(1)}, f32[2,12,512,512]{2,3,1,0:T(8,128)}) fusion(f32[12,512,512]{1,2,0:T(8,128)} %copy.66, pred[2,512]{1,0:T(4,128)(4,1)S(1)} %iota_compare_fusion.5, bf16[2,512,12,64]{1,0,3,2:T(2,128)(2,1)S(1)} %reshape.356, bf16[2,512,12,64]{1,0,3,2:T(2,128)(2,1)S(1)} %reshape.357), kind=kOutput, calls=%fused_computation.265 | convolution fusion | flops 830472704 | bytes 40944640 | tf_op jit(solution)/shard_map/sub | solution.py:509
  213.6 11.0 %fusion.64 = bf16[2,512,12,64]{1,3,2,0:T(8,128)(2,1)S(1)} fusion(bf16[2,512,12,64]{1,0,3,2:T(2,128)(2,1)} %reshape.360, f32[2,12,512,512]{2,3,1,0:T(8,128)} %get-tuple-element.118, f32[2,12,512]{2,1,0:T(8,128)S(1)} %get-tuple-element.117), kind=kOutput, calls=%fused_computation.109 | convolution fusion | flops 818675712 | bytes 28360704 | tf_op jit(solution)/shard_map/phqk,pkhd->pqhd/dot_general | solution.py:511
  237.6 3.5 fusion.42
  245.6 3.9 fusion.35
  259.1 3.7 fusion.28
  266.2 3.1 fusion.114
  275.0 3.5 fusion.21
  283.8 3.6 fusion.108
  287.4 5.1 add_convert_fusion
  311.5 4.2 reshape.362
  315.8 13.7 %fusion.61 = bf16[2,512,12,64]{1,3,2,0:T(8,128)(2,1)} fusion(bf16[2,512,12,64]{1,0,3,2:T(2,128)(2,1)} %reshape.362, f32[2,12,512,512]{2,3,1,0:T(8,128)} %get-tuple-element.118, f32[2,12,512]{2,1,0:T(8,128)S(1)} %get-tuple-element.117), kind=kOutput, calls=%fused_computation.108 | convolution fusion | flops 818675712 | bytes 28360704 | tf_op jit(solution)/shard_map/phqk,pqhd->pkhd/dot_general | solution.py:538
  329.5 4.2 copy.80
  333.7 3.8 reshape.365
  339.9 20.0 %multiply_reduce_fusion = (f32[2,12,512]{2,1,0:T(8,128)}, f32[2,12,512,512]{2,3,1,0:T(8,128)}) fusion(f32[2,12,512,512]{2,3,1,0:T(8,128)} %get-tuple-element.118, f32[2,12,512]{2,1,0:T(8,128)} %copy-done.56, bf16[2,512,12,64]{1,0,3,2:T(2,128)(2,1)} %reshape.360, bf16[2,512,12,64]{1,0,3,2:T(2,128)(2,1)} %reshape.362), kind=kOutput, calls=%fused_computation.6 | convolution fusion | flops 824168448 | bytes 53575680 | tf_op jit(solution)/shard_map/pqhd,pkhd->phqk/dot_general | solution.py:537
  359.9 27.8 %convert_reduce_fusion = (f32[12,512,512]{1,2,0:T(8,128)}, bf16[2,12,512,512]{2,3,1,0:T(8,128)(2,1)}) fusion(f32[2,12,512,512]{2,3,1,0:T(8,128)} %get-tuple-element.123, f32[2,12,512]{2,1,0:T(8,128)} %get-tuple-element.122, f32[2,12,512,512]{2,3,1,0:T(8,128)} %get-tuple-element.118, f32[2,12,512]{2,1,0:T(8,128)} %copy-done.56), kind=kLoop, calls=%fused_computation.4 | loop fusion | flops 34603008 | bytes 75595776 | tf_op jit(solution)/shard_map/reduce_sum | solution.py:542
  387.7 9.7 %fusion.68 = bf16[2,512,12,64]{1,3,2,0:T(8,128)(2,1)} fusion(bf16[2,12,512,512]{2,3,1,0:T(8,128)(2,1)} %get-tuple-element.78, bf16[2,512,12,64]{1,0,3,2:T(2,128)(2,1)S(1)} %copy-done.8), kind=kOutput, calls=%fused_computation.111 | convolution fusion | flops 806092800 | bytes 15728640 | tf_op jit(solution)/shard_map/phqk,pqhd->pkhd/dot_general | solution.py:541
  397.4 6.5 fusion.67
  406.7 3.8 reshape.363
  410.5 4.2 copy.77
  414.7 4.0 reshape.364
  422.4 3.2 fusion.130
  431.8 6.6 copy.81
  438.4 11.4 %pad_maximum_fusion.G = bf16[3,2,2,4,2,96,768]{6,5,4,3,2,1,0:T(8,128)(2,1)} fusion(bf16[1,2,2,4,2,96,768]{6,5,4,3,2,1,0:T(8,128)(2,1)} %bitcast.294, bf16[1,2,2,4,2,96,768]{6,5,4,3,2,1,0:T(8,128)(2,1)} %bitcast.295, bf16[1,2,2,4,2,96,768]{6,5,4,3,2,1,0:T(8,128)(2,1)} %bitcast.297), kind=kLoop, calls=%fused_computation.12 | loop fusion | flops 14155776 | bytes 28311552 | tf_op jit(solution)/shard_map/stack | solution.py:554
  459.7 119.9 %shard_map.213 = (f32[3,96,768]{2,1,0:T(8,128)}, bf16[8,128,768]{2,1,0:T(8,128)(2,1)}, bf16[8,128,768]{2,1,0:T(8,128)(2,1)}) custom-call(bf16[3,2,2,4,2,96,768]{6,5,4,3,2,1,0:T(8,128)(2,1)} %pad_maximum_fusion.G, bf16[2,4,128,768]{3,2,1,0:T(8,128)(2,1)} %bitcast.318, bf16[2,4,128,768]{3,2,1,0:T(8,128)(2,1)} %bitcast.327), custom_call_target="tpu_custom_call" | custom-call | tf_op jit(solution)/shard_map/pallas_call | solution.py:439
  583.2 18.5 %copy.82 = f32[12,512,512]{2,0,1:T(8,128)} copy(f32[12,512,512]{1,2,0:T(8,128)} %get-tuple-element.77) | data formatting | bytes 25165824 | tf_op jit(solution)/shard_map/reduce_sum | solution.py:542
  601.7 20.2 %fusion.107 = f32[32,12]{0,1:T(8,128)S(1)} fusion(f32[12,512,512]{2,0,1:T(8,128)} %copy.82, s32[512,512]{1,0:T(8,128)S(1)} %copy-done.17), kind=kOutput, calls=%fused_computation.172 | convolution fusion | flops 1216348160 | bytes 13633024 | tf_op jit(solution)/shard_map/hij,bij->bh/dot_general | solution.py:542
  621.9 41.7 %all-reduce.1 = (f32[768]{0:T(1024)}, f32[768]{0:T(1024)}, f32[32,12]{0,1:T(8,128)S(1)}) all-reduce(f32[768]{0:T(1024)S(1)} %get-tuple-element.72, f32[768]{0:T(1024)S(1)} %copy-done.62, f32[32,12]{0,1:T(8,128)S(1)} %fusion.107), channel_id=1, replica_groups=mesh['dp'=8,'mp'=4] {'dp','mp'}, use_global_device_ids=true, to_apply=%region_8.9 | all-reduce | flops 1920 | bytes 15360 | tf_op jit(solution)/shard_map/psum | solution.py:562
  (228 shorter events, 119.6 us)
Async XLA Ops:
  125.3 11.9 %copy-start = (bf16[2,4,128,768]{3,2,1,0:T(8,128)(2,1)S(1)}, bf16[2,4,128,768]{3,2,1,0:T(8,128)(2,1)}, u32[]{:S(2)}) copy-start(bf16[2,4,128,768]{3,2,1,0:T(8,128)(2,1)} %get-tuple-element.30) | copy-start | bytes 4718596
  125.3 12.3 %copy-start.63 = (f32[4,8,128]{2,1,0:T(8,128)S(1)}, f32[4,8,128]{2,1,0:T(8,128)}, u32[]{:S(2)}) copy-start(f32[4,8,128]{2,1,0:T(8,128)} %get-tuple-element.32) | copy-start | bytes 49156
  125.3 12.3 %copy-start.60 = (f32[768]{0:T(1024)S(1)}, f32[768]{0:T(1024)}, u32[]{:S(2)}) copy-start(f32[768]{0:T(1024)} %param.18) | copy-start | bytes 9220
  137.5 3.7 copy-start.57
  138.0 9.7 %copy-start.29 = (bf16[1024,768]{1,0:T(8,128)(2,1)}, bf16[1024,768]{1,0:T(8,128)(2,1)S(1)}, u32[]{:S(2)}) copy-start(bf16[1024,768]{1,0:T(8,128)(2,1)S(1)} %fusion.47) | copy-start | bytes 4718596
  141.3 4.3 copy-start.18
  141.3 6.4 copy-start.20
  151.3 42.0 %copy-start.7 = (bf16[2,512,12,64]{1,0,3,2:T(2,128)(2,1)}, bf16[2,512,12,64]{1,0,3,2:T(2,128)(2,1)S(1)}, u32[]{:S(2)}) copy-start(bf16[2,512,12,64]{1,0,3,2:T(2,128)(2,1)S(1)} %reshape.357) | copy-start | bytes 4718596
  161.2 32.0 %copy-start.3 = (bf16[2,512,12,64]{1,0,3,2:T(2,128)(2,1)}, bf16[2,512,12,64]{1,0,3,2:T(2,128)(2,1)S(1)}, u32[]{:S(2)}) copy-start(bf16[2,512,12,64]{1,0,3,2:T(2,128)(2,1)S(1)} %reshape.356) | copy-start | bytes 4718596
  213.6 102.2 %copy-start.56 = (f32[2,12,512]{2,1,0:T(8,128)}, f32[2,12,512]{2,1,0:T(8,128)S(1)}, u32[]{:S(2)}) copy-start(f32[2,12,512]{2,1,0:T(8,128)S(1)} %get-tuple-element.117) | copy-start | bytes 147460
  227.6 3.1 copy-start.9
  227.6 3.1 copy-start.24
  230.7 3.8 slice-start.2
  234.5 3.0 slice-start
  287.4 5.1 copy-start.65
  292.5 3.3 copy-start.38
  359.9 27.8 %copy-start.8 = (bf16[2,512,12,64]{1,0,3,2:T(2,128)(2,1)S(1)}, bf16[2,512,12,64]{1,0,3,2:T(2,128)(2,1)}, u32[]{:S(2)}) copy-start(bf16[2,512,12,64]{1,0,3,2:T(2,128)(2,1)} %copy-done.7) | copy-start | bytes 4718596
  387.7 9.7 %copy-start.4 = (bf16[2,512,12,64]{1,0,3,2:T(2,128)(2,1)S(1)}, bf16[2,512,12,64]{1,0,3,2:T(2,128)(2,1)}, u32[]{:S(2)}) copy-start(bf16[2,512,12,64]{1,0,3,2:T(2,128)(2,1)} %copy-done.3) | copy-start | bytes 4718596
  420.4 5.2 copy-start.33
  420.4 6.3 copy-start.48
  420.4 7.4 %copy-start.50 = (bf16[1024,192]{0,1:T(8,128)(2,1)}, bf16[1024,192]{0,1:T(8,128)(2,1)S(1)}, u32[]{:S(2)}) copy-start(bf16[1024,192]{0,1:T(8,128)(2,1)S(1)} %get-tuple-element.93) | copy-start | bytes 1179652
  420.7 4.9 copy-start.35
  420.7 6.0 copy-start.52
  420.7 7.1 %copy-start.54 = (bf16[1024,192]{0,1:T(8,128)(2,1)}, bf16[1024,192]{0,1:T(8,128)(2,1)S(1)}, u32[]{:S(2)}) copy-start(bf16[1024,192]{0,1:T(8,128)(2,1)S(1)} %get-tuple-element.89) | copy-start | bytes 1179652
  438.4 11.4 %copy-start.22 = (bf16[768,768]{1,0:T(8,128)(2,1)S(1)}, bf16[768,768]{1,0:T(8,128)(2,1)}, u32[]{:S(2)}) copy-start(bf16[768,768]{1,0:T(8,128)(2,1)} %copy-done.20) | copy-start | bytes 3538948
  438.4 11.4 %copy-start.46 = (bf16[1024,192]{0,1:T(8,128)(2,1)S(1)}, bf16[1024,192]{0,1:T(8,128)(2,1)}, u32[]{:S(2)}) copy-start(bf16[1024,192]{0,1:T(8,128)(2,1)} %get-tuple-element.97) | copy-start | bytes 1179652
  438.4 11.4 %copy-start.51 = (bf16[1024,192]{0,1:T(8,128)(2,1)S(1)}, bf16[1024,192]{0,1:T(8,128)(2,1)}, u32[]{:S(2)}) copy-start(bf16[1024,192]{0,1:T(8,128)(2,1)} %copy-done.50) | copy-start | bytes 1179652
  438.4 11.4 %copy-start.55 = (bf16[1024,192]{0,1:T(8,128)(2,1)S(1)}, bf16[1024,192]{0,1:T(8,128)(2,1)}, u32[]{:S(2)}) copy-start(bf16[1024,192]{0,1:T(8,128)(2,1)} %copy-done.54) | copy-start | bytes 1179652
  583.2 18.5 %copy-start.17 = (s32[512,512]{1,0:T(8,128)S(1)}, s32[512,512]{1,0:T(8,128)}, u32[]{:S(2)}) copy-start(s32[512,512]{1,0:T(8,128)} %constant.72.clone) | copy-start | bytes 3145732
  601.7 20.2 %copy-start.62 = (f32[768]{0:T(1024)S(1)}, f32[768]{0:T(1024)}, u32[]{:S(2)}) copy-start(f32[768]{0:T(1024)} %get-tuple-element.70) | copy-start | bytes 9220
  601.7 62.5 %copy-start.32 = (bf16[8,128,768]{2,1,0:T(8,128)(2,1)S(1)}, bf16[8,128,768]{2,1,0:T(8,128)(2,1)}, u32[]{:S(2)}) copy-start(bf16[8,128,768]{2,1,0:T(8,128)(2,1)} %get-tuple-element.138) | copy-start | bytes 4718596
  621.9 43.4 %copy-start.31 = (bf16[8,128,768]{2,1,0:T(8,128)(2,1)S(1)}, bf16[8,128,768]{2,1,0:T(8,128)(2,1)}, u32[]{:S(2)}) copy-start(bf16[8,128,768]{2,1,0:T(8,128)(2,1)} %get-tuple-element.139) | copy-start | bytes 4718596
  (38 other events, 73.4 us)

commit v2 on v0

v2 whole, which is shorter than its diff:
```python
import functools
import math

import jax
import jax.numpy as jnp
import numpy as np
from jax import lax
from jax.experimental import pallas as pl
from jax.experimental.pallas import tpu as pltpu
from jax.sharding import PartitionSpec as P

BF = jnp.bfloat16
F32 = jnp.float32
MESH = pl.DeviceIdType.MESH
EPS = 1e-06
FAR = 128
HIGHEST = lax.Precision.HIGHEST
MIB = 2**20


def bucket_of(offset, count):
    half = count // 2
    upper = (offset > 0).astype(np.int64) * half
    distance = np.abs(offset)
    exact = half // 2
    scaled = np.log(np.maximum(distance, 1) / exact) / np.log(FAR / exact) * (half - exact)
    larger = np.minimum(exact + scaled.astype(np.int64), half - 1)
    return (upper + np.where(distance < exact, distance, larger)).astype(np.int32)


class Place:
    def __init__(self, ndp, nmp, fine):
        self.dp, self.mp = lax.axis_index("dp"), lax.axis_index("mp")
        self.x, self.c = self.mp // 2, self.mp % 2
        self.fine = fine
        self.z, self.y = self.dp // fine // 2, self.dp // fine % 2
        self.nz = ndp // fine // 2
        self.nmp = nmp

    def at(self, x=None, c=None, z=None, y=None):
        x = self.x if x is None else x
        c = self.c if c is None else c
        z = self.z if z is None else z
        y = self.y if y is None else y
        return ((z * 2 + y) * self.fine + self.dp % self.fine, x * 2 + c)

    def zi(self, k):
        return lax.rem(self.z + k, self.nz)

    def greet(self):
        bar = pltpu.get_barrier_semaphore()

        def tell(who):
            pl.semaphore_signal(bar, inc=1, device_id=who, device_id_type=MESH)

        tell(self.at(c=1 - self.c))
        tell(self.at(x=1 - self.x))
        tell(self.at(x=1 - self.x, c=1 - self.c))
        tell(self.at(y=1 - self.y))
        loop(1, self.nz, lambda k: tell(self.at(z=self.zi(k))))

    def met(self):
        pl.semaphore_wait(pltpu.get_barrier_semaphore(), 4 + self.nz - 1)


def remote(src, dst, ssem, rsem, who):
    return pltpu.make_async_remote_copy(
        src_ref=src, dst_ref=dst, send_sem=ssem, recv_sem=rsem, device_id=who, device_id_type=MESH
    )


def loop(lo, hi, fn):
    def step(k, carry):
        fn(k)
        return carry

    lax.fori_loop(lo, hi, step, 0)


class Gather:
    def __init__(self, here, pack, order, W, ssem, rsem):
        self.h, self.order, self.nz = here, order, here.nz
        self.W = W.at[pack]
        self.ss, self.rs = ssem.at[pack], rsem.at[pack]

    def send(self, src, kind, idx, who, sidx=None):
        sidx = idx if sidx is None else sidx
        return remote(src, src, self.ss.at[kind, sidx], self.rs.at[kind, idx], who)

    def first(self, k, mine=True):
        h = self.h
        if self.order == "xzy":
            x = h.x if mine else 1 - h.x
            return self.send(self.W.at[x, h.c, h.z, h.y], 0, 0, h.at(x=1 - h.x))
        z = h.zi(k)
        own = h.z if mine else z
        return self.send(self.W.at[h.x, h.c, own, h.y], 0, own, h.at(z=z), z)

    def second(self, k, mine=True):
        h, z = self.h, self.h.zi(k)
        if self.order == "xzy":
            own = h.z if mine else z
            return self.send(self.W.at[:, h.c, own, h.y], 1, own, h.at(z=z), z)
        if self.order == "zxy":
            x = h.x if mine else 1 - h.x
            return self.send(self.W.at[x, h.c, z, h.y], 1, z, h.at(x=1 - h.x))
        y = h.y if mine else 1 - h.y
        return self.send(self.W.at[h.x, h.c, z, y], 1, z, h.at(y=1 - h.y))

    def third(self, half, k, mine=True):
        h, z = self.h, self.h.zi(k)
        x, y = h.x, h.y
        if self.order == "zyx":
            y = y if half == 0 else 1 - y
            x = x if mine else 1 - x
            return self.send(self.W.at[x, h.c, z, y], 2 + half, z, h.at(x=1 - h.x))
        x = x if half == 0 else 1 - x
        y = y if mine else 1 - y
        return self.send(self.W.at[x, h.c, z, y], 2 + half, z, h.at(y=1 - h.y))

    def sib(self, half, k, mine=True):
        h, z = self.h, self.h.zi(k)
        c = h.c if mine else 1 - h.c
        if self.order == "zyx":
            block = self.W.at[h.x if half == 0 else 1 - h.x, c, z]
        else:
            block = self.W.at[:, c, z, h.y if half == 0 else 1 - h.y]
        return self.send(block, 4 + half, z, h.at(c=1 - h.c))

    def sib_wait(self, half):
        loop(0, self.nz, lambda k: self.sib(half, k, False).wait_recv())

    def sent(self):
        def on(k):
            for half in (0, 1):
                self.sib(half, k).wait_send()
                self.third(half, k).wait_send()

        loop(0, self.nz, on)
        if self.order == "xzy":
            self.first(0).wait_send()
            loop(1, self.nz, lambda k: self.second(k).wait_send())
        else:
            loop(1, self.nz, lambda k: self.first(k).wait_send())
            loop(0, self.nz, lambda k: self.second(k).wait_send())


class Swap:
    def __init__(self, here, whole, flat, sems, back):
        self.h, self.whole, self.flat, self.sems, self.back = here, whole, flat, sems, back
        self.positions = whole.shape[1]
        self.share = whole.shape[0] // here.nmp

    def views(self, s, outer, inner):
        at = pl.multiple_of((s * self.h.nmp + inner) * self.positions, self.positions)
        return self.whole.at[outer * self.share + s], self.flat.at[pl.ds(at, self.positions)]

    def copy(self, s, k, mine):
        h = self.h
        other = lax.rem(h.mp + (k if mine else h.nmp - k), h.nmp)
        sender, receiver = (h.mp, other) if mine else (other, h.mp)
        if self.back:
            dst, src = self.views(s, sender, receiver)
        else:
            src, dst = self.views(s, receiver, sender)
        if not mine:
            src = dst
        return remote(src, dst, self.sems.at[0, k, s], self.sems.at[1, k, s], (h.dp, other))

    def local(self, s):
        whole, flat = self.views(s, self.h.mp, self.h.mp)
        src, dst = (flat, whole) if self.back else (whole, flat)
        return pltpu.make_async_copy(src, dst, self.sems.at[0, 0, s])

    def start(self):
        for k in range(1, self.h.nmp):
            for s in range(self.share):
                self.copy(s, k, True).start()
        for s in range(self.share):
            self.local(s).start()

    def come(self):
        for k in range(1, self.h.nmp):
            for s in range(self.share):
                self.copy(s, k, False).wait_recv()
        for s in range(self.share):
            self.local(s).wait()

    def sent(self):
        for k in range(1, self.h.nmp):
            for s in range(self.share):
                self.copy(s, k, True).wait_send()


def dot(a, b, ca=1, cb=0, precision=None):
    return lax.dot_general(a, b, (((ca,), (cb,)), ((), ())), preferred_element_type=F32, precision=precision)


def tile_rows(i, size):
    return pl.ds(pl.multiple_of(i * size, size), size)


TILE = 256


def rsq(v):
    return lax.rsqrt(jnp.mean(v * v, axis=-1, keepdims=True) + EPS)


def toeplitz(offsets, ST):
    heads, span = ST.shape[0], ST.shape[2]
    for h in range(heads):
        row = jnp.broadcast_to(offsets[h : h + 1, :], (128, offsets.shape[1]))
        ST[h] = pltpu.roll(row, 0, 1, stride=1, stride_axis=0)[:, :span]


def biased(s, ST, h, i0, dead):
    blocks = s.shape[0] // 128
    width = s.shape[1]
    pieces = []
    for j in range(blocks):
        c0 = 128 * (blocks - 1 - j) + i0
        piece = s[128 * j : 128 * (j + 1)] + ST[h, :, c0 : c0 + width]
        pieces.append(piece if j < blocks // 2 else piece + dead)
    return jnp.concatenate(pieces, 0)


def attend(QV, ST, h, part, dh, seq, dead, base, OV, LV):
    q0, k0, v0 = h * dh, part + h * dh, 2 * part + h * dh
    rows = pl.ds(base, seq)
    keys = QV[rows, k0 : k0 + dh]
    values_t = QV[rows, v0 : v0 + dh].T
    queries = QV[rows, q0 : q0 + dh]
    for i0 in range(0, seq, TILE):
        s = biased(dot(keys, queries[i0 : i0 + TILE], 1, 1), ST, h, i0, dead)
        top = jnp.max(s, axis=0, keepdims=True)
        e = jnp.exp(s - top)
        total = jnp.sum(e, axis=0, keepdims=True)
        out = dot(values_t, e.astype(BF)) * (1.0 / total)
        at = pl.ds(pl.multiple_of(base + i0, TILE), TILE)
        OV[at, h * dh : (h + 1) * dh] = out.astype(BF).T
        LV[h : h + 1, at] = top + jnp.log(total)


def forward_kernel(cfg, tok, cot, wq, wk, wv, wo, wi, wf, table, onehot, gain, lens, *refs):
    W, X, DY, OFF, H, QKV, O, LSE = refs[:8]
    OWN, OFFV, XV, N1, AV, QV, OV, LV, HV, ST = refs[8:18]
    ssem, rsem, tsem, dsem, bsem, lsem, asem, osem = refs[18:]
    ndp, nmp, fine, seq, heads_mp = cfg
    h = Place(ndp, nmp, fine)
    h.greet()
    rows, part = wq.shape
    n, width = XV.shape
    dh = part // heads_mp
    share = n // seq
    OWN[0, :, :part] = wq[...].astype(BF)
    OWN[0, :, part : 2 * part] = wk[...].astype(BF)
    OWN[0, :, 2 * part : 3 * part] = wv[...].astype(BF)
    OWN[0, :, 3 * part :] = wo[...].T.astype(BF)
    OWN[1] = wi[...].astype(BF)
    OWN[2] = wf[...].T.astype(BF)

    def own(p):
        return pltpu.make_async_copy(OWN.at[p], W.at[p, h.x, h.c, h.z, h.y], lsem.at[p])

    for p in range(3):
        own(p).start()
    OFFV[h.mp] = jnp.zeros_like(OFFV[0])
    OFFV[h.mp, :heads_mp] = dot(table[...], onehot[...], 0, 0, HIGHEST)

    def offs(k, mine=True):
        other = lax.rem(h.mp + (k if mine else nmp - k), nmp)
        at = OFFV.at[h.mp if mine else other]
        return remote(at, at, bsem.at[0, k], bsem.at[1, k], (h.dp, other))

    A = Gather(h, 0, "zyx", W, ssem, rsem)
    B = Gather(h, 1, "xzy", W, ssem, rsem)
    C = Gather(h, 2, "zxy", W, ssem, rsem)
    sx = Swap(h, tok, X, tsem, False)
    sd = Swap(h, cot, DY, dsem, False)
    nz = h.nz
    for p in range(3):
        own(p).wait()
    h.met()
    loop(1, nz, lambda k: A.first(k).start())
    A.second(0).start()
    sx.start()
    B.first(0).start()
    for k in range(1, nmp):
        offs(k).start()

    def a_second(k):
        A.first(k, False).wait_recv()
        A.second(k).start()

    loop(1, nz, a_second)
    loop(1, nz, lambda k: C.first(k).start())
    B.first(0, False).wait_recv()
    loop(1, nz, lambda k: B.second(k).start())

    def a_sib(k):
        A.second(k, False).wait_recv()
        A.sib(0, k).start()

    loop(0, nz, a_sib)
    sx.come()
    load_x = pltpu.make_async_copy(X, XV, lsem.at[0])
    load_x.start()

    def a_third(k):
        A.third(0, k).start()
        A.third(1, k).start()

    loop(0, nz, a_third)
    B.third(0, 0).start()
    B.third(1, 0).start()
    B.sib(0, 0).start()
    A.sib_wait(0)

    def group(i):
        return lax.rem(2 * h.x + i, nmp)

    def load_a(i):
        m = group(i)
        return pltpu.make_async_copy(W.at[0, m // 2, m % 2], AV.at[lax.rem(i, 2)], asem.at[lax.rem(i, 2)])

    def store(i):
        m, slot = group(i), lax.rem(i, 2)
        return (
            pltpu.make_async_copy(QV.at[slot], QKV.at[m], osem.at[0, slot]),
            pltpu.make_async_copy(OV.at[slot], O.at[m], osem.at[1, slot]),
            pltpu.make_async_copy(LV.at[slot], LSE.at[m], osem.at[2, slot]),
        )

    load_a(0).start()
    for k in range(1, nmp):
        offs(k, False).wait_recv()
    load_x.wait()

    def norm(t):
        r = tile_rows(t, TILE)
        x = XV[r, :].astype(F32)
        N1[r, :] = (x * rsq(x) * gain[...].reshape(1, width)).astype(BF)
        HV[r, :] = x

    loop(0, n // TILE, norm)

    def tick_b_second():
        def on(k):
            B.second(k, False).wait_recv()
            B.third(0, k).start()
            B.third(1, k).start()
            B.sib(0, k).start()

        loop(1, nz, on)

    def tick_a_third():
        def on(k):
            A.third(0, k, False).wait_recv()
            A.third(1, k, False).wait_recv()
            A.sib(1, k).start()

        loop(0, nz, on)

    def tick_c_first():
        C.second(0).start()
        C.third(0, 0).start()

        def on(k):
            C.first(k, False).wait_recv()
            C.second(k).start()
            C.third(0, k).start()

        loop(1, nz, on)

    def tick_c_second():
        def on(k):
            C.second(k, False).wait_recv()
            C.third(1, k).start()
            C.sib(0, k).start()

        loop(0, nz, on)

    def tick_third(T):
        def on(k):
            T.third(0, k, False).wait_recv()
            T.third(1, k, False).wait_recv()
            T.sib(1, k).start()

        loop(0, nz, on)

    ticks = {
        (0, 1, 2): tick_c_first,
        (1, 0, 1): tick_b_second,
        (1, 1, 2): tick_a_third,
        (2, 0, 0): sd.start,
        (3, 0, 0): tick_c_second,
    }

    def step(i):
        slot = lax.rem(i, 2)
        m = group(i)

        @pl.when(i == 2)
        def _():
            A.sib_wait(1)
            load_a(2).start()

        load_a(i).wait()
        pl.when((i == 0) | (i == 2))(lambda: load_a(i + 1).start())

        @pl.when(i >= 2)
        def _():
            for cp in store(i - 2):
                cp.wait()

        toeplitz(OFFV.at[m], ST)

        def project(t):
            r = tile_rows(t, TILE)
            w = AV[slot, :, :, :, : 3 * part].reshape(width, 3 * part)
            QV[slot, r, :] = dot(N1[r, :], w).astype(BF)

        loop(0, n // TILE, project)

        def pair(p):
            base = pl.multiple_of(p * seq, seq)
            off = jnp.where(lens[h.mp * share + p] < seq, -1e30, 0.0).astype(F32)
            for head in range(heads_mp):
                for (ti, tp, th), fn in ticks.items():
                    if th == head:
                        pl.when((i == ti) & (p == tp))(fn)
                attend(QV.at[slot], ST, head, part, dh, seq, off, base, OV.at[slot], LV.at[slot])

        loop(0, share, pair)

        def join(t):
            r = tile_rows(t, TILE)
            w = AV[slot, :, :, :, 3 * part :].reshape(width, part)
            HV[r, :] += dot(OV[slot, r, :], w, 1, 1)

        loop(0, n // TILE, join)
        for cp in store(i):
            cp.start()

    loop(0, nmp, step)
    out = [pltpu.make_async_copy(HV, H, lsem.at[1]), pltpu.make_async_copy(OFFV, OFF, lsem.at[2])]
    for cp in out:
        cp.start()
    tick_third(B)
    tick_third(C)
    for T in (B, C):
        T.sib_wait(0)
        T.sib_wait(1)
    for T in (A, B, C):
        T.sent()
    sx.sent()
    sd.come()
    sd.sent()
    for k in range(1, nmp):
        offs(k).wait_send()
    for i in (nmp - 2, nmp - 1):
        for cp in store(i):
            cp.wait()
    for cp in out:
        cp.wait()


def forward(tok, cot, ws, table, onehot, gain, lens, ndp, nmp, fine):
    pairs, positions, width = tok.shape
    rows, part = ws[0].shape
    hid = ws[4].shape[1]
    heads_mp = table.shape[1]
    seq = positions * nmp
    share = pairs // nmp
    n = share * seq
    nz = ndp // fine // 2
    any_ = pl.BlockSpec(memory_space=pl.ANY)
    vm = pl.BlockSpec(memory_space=pltpu.VMEM)
    dma = pltpu.SemaphoreType.DMA
    sds = jax.ShapeDtypeStruct
    return pl.pallas_call(
        functools.partial(forward_kernel, (ndp, nmp, fine, seq, heads_mp)),
        out_shape=(
            sds((3, nmp // 2, 2, nz, 2, rows, hid), BF),
            sds((n, width), BF),
            sds((n, width), BF),
            sds((nmp, 8, 2 * seq), F32),
            sds((n, width), F32),
            sds((nmp, n, 3 * part), BF),
            sds((nmp, n, part), BF),
            sds((nmp, 8, n), F32),
        ),
        in_specs=[any_, any_] + [vm] * 9 + [pl.BlockSpec(memory_space=pltpu.SMEM)],
        out_specs=(any_,) * 8,
        scratch_shapes=[
            pltpu.VMEM((3, rows, hid), BF),
            pltpu.VMEM((nmp, 8, 2 * seq), F32),
            pltpu.VMEM((n, width), BF),
            pltpu.VMEM((n, width), BF),
            pltpu.VMEM((2, nz, 2, rows, hid), BF),
            pltpu.VMEM((2, n, 3 * part), BF),
            pltpu.VMEM((2, n, part), BF),
            pltpu.VMEM((2, 8, n), F32),
            pltpu.VMEM((n, width), F32),
            pltpu.VMEM((heads_mp, 128, 2 * seq - 128), F32),
            dma((3, 6, nz)),
            dma((3, 6, nz)),
            dma((2, nmp, share)),
            dma((2, nmp, share)),
            dma((2, nmp)),
            dma((4,)),
            dma((2,)),
            dma((3, 2)),
        ],
        compiler_params=pltpu.CompilerParams(collective_id=0, has_side_effects=True, vmem_limit_bytes=56 * MIB),
    )(tok, cot, *ws, table, onehot, gain, lens)


GELU_C = float(np.sqrt(2.0 / np.pi))


def gelu_both(a):
    a2 = a * a
    t = jnp.tanh(a * (GELU_C + (GELU_C * 0.044715) * a2))
    half = 0.5 + 0.5 * t
    slope = half + (0.5 * a) * (1.0 - t * t) * (GELU_C + (3.0 * GELU_C * 0.044715) * a2)
    return a * half, slope


class Scatter:
    def __init__(self, here, pack, bufs, sems):
        self.h, self.p, self.nz = here, pack, here.nz
        self.MINE, self.R0, self.R1, self.R2, self.R3, self.ACC = [b.at[pack] for b in bufs]
        self.sems = [s.at[pack] for s in sems]
        self.rows = self.R3.shape[0]

    def slot(self, m):
        return jnp.where(m % 2 == self.h.c, m // 2, 2)

    def block(self, z, y):
        return pl.ds(pl.multiple_of((z * 2 + y) * self.rows, self.rows), self.rows)

    def sib(self, x):
        return remote(self.MINE.at[2], self.R0.at[x], self.sems[0].at[x], self.sems[1].at[x], self.h.at(c=1 - self.h.c))

    def ysend(self, x, k):
        h, z = self.h, self.h.zi(k)
        src = self.MINE.at[x, self.block(z, 1 - h.y)]
        return remote(src, self.R1.at[x, z], self.sems[2].at[x, z], self.sems[3].at[x, z], h.at(y=1 - h.y))

    def zsend(self, x, k):
        h, z = self.h, self.h.zi(k)
        return remote(self.R1.at[x, z], self.R2.at[x, h.z], self.sems[4].at[x, z], self.sems[5].at[x, h.z], h.at(z=z))

    def zcome(self, x, k):
        h, z = self.h, self.h.zi(k)
        return remote(self.R2.at[x, z], self.R2.at[x, z], self.sems[4].at[x, z], self.sems[5].at[x, z], h.at(z=z))

    def xsend(self):
        h = self.h
        return remote(self.R1.at[1 - h.x, h.z], self.R3, self.sems[6].at[0], self.sems[7].at[0], h.at(x=1 - h.x))

    def after_group(self, m):
        pl.when(m % 2 != self.h.c)(lambda: self.sib(m // 2).start())

    def before_group(self, m):
        pl.when(m == 3 - self.h.c)(lambda: self.sib(0).wait_send())

    def after_sib(self, x):
        self.sib(x).wait_recv()

        def on(k):
            r = self.block(self.h.zi(k), 1 - self.h.y)
            self.MINE[x, r] = (self.MINE[x, r].astype(F32) + self.R0[x, r].astype(F32)).astype(BF)
            self.ysend(x, k).start()

        loop(0, self.nz, on)

    def after_y(self, x):
        def on(kk):
            k = lax.rem(kk + 1, self.nz)
            z = self.h.zi(k)
            r = self.block(z, self.h.y)
            self.ysend(x, k).wait_recv()
            total = self.MINE[x, r].astype(F32) + self.R0[x, r].astype(F32) + self.R1[x, z].astype(F32)
            self.R1[x, z] = total.astype(BF)
            pl.when(k > 0)(lambda: self.zsend(x, k).start())

        loop(0, self.nz, on)

    def after_z(self, x):
        h = self.h
        loop(1, self.nz, lambda k: self.zcome(x, k).wait_recv())

        def add(k, acc):
            return acc + self.R2[x, h.zi(k)].astype(F32)

        total = lax.fori_loop(1, self.nz, add, self.R1[x, h.z].astype(F32))

        @pl.when(h.x != x)
        def _():
            self.R1[x, h.z] = total.astype(BF)
            self.xsend().start()

        @pl.when(h.x == x)
        def _():
            self.ACC[...] = total

    def result(self):
        self.xsend().wait_recv()
        return self.ACC[...] + self.R3[...].astype(F32)

    def sent(self):
        self.xsend().wait_send()
        self.sib(1).wait_send()
        for x in range(2):
            loop(0, self.nz, lambda k: self.ysend(x, k).wait_send())
            loop(1, self.nz, lambda k: self.zsend(x, k).wait_send())


def attend_back(QV, ST, DO, LV, GQKV, D, h, part, dh, seq, dead, base):
    rows = pl.ds(base, seq)
    q0, k0, v0 = h * dh, part + h * dh, 2 * part + h * dh
    queries = QV[rows, q0 : q0 + dh]
    keys = QV[rows, k0 : k0 + dh]
    values = QV[rows, v0 : v0 + dh]
    keys_t = keys.T
    d_o = DO[rows, h * dh : (h + 1) * dh]
    blocks = seq // 128
    gv = gk = 0.0
    for i0 in range(0, seq, TILE):
        q, do = queries[i0 : i0 + TILE], d_o[i0 : i0 + TILE]
        s = biased(dot(keys, q, 1, 1), ST, h, i0, dead)
        at = pl.ds(pl.multiple_of(base + i0, TILE), TILE)
        prob = jnp.exp(s - LV[h : h + 1, at])
        dprob = dot(values, do, 1, 1)
        weighted = prob * dprob
        delta = jnp.sum(weighted, axis=0, keepdims=True)
        gs = (weighted - prob * delta).astype(BF)
        gv += dot(prob.astype(BF), do)
        gk += dot(gs, q)
        gq = dot(keys_t, gs)
        GQKV[at, q0 : q0 + dh] = gq.astype(BF).T
        for j in range(blocks):
            c0 = 128 * (blocks - 1 - j) + i0
            D[h, :, c0 : c0 + TILE] += gs[128 * j : 128 * (j + 1)].astype(F32)
    GQKV[rows, k0 : k0 + dh] = gk.astype(BF)
    GQKV[rows, v0 : v0 + dh] = gv.astype(BF)


def backward_kernel(cfg, H, X, DY, W, QKV, O, LSE, OFF, gain1, gain2, onehot, lens, *refs):
    L, I, GQ, GK, GV, GO, GI, GF, SMALL = refs[:9]
    HV, XV, DYV, N2, N2T, DYT, U, GA, FF, GN, BV, CV, QV, OV, LV, OFFV, ST, D = refs[9:27]
    bufs, SR, SZ = refs[27:33], refs[33], refs[34]
    lsem, wsem, qsem, tsem, dsem, ssmall, rsmall = refs[35:42]
    sems = refs[42:50]
    ndp, nmp, fine, seq, heads_mp = cfg
    h = Place(ndp, nmp, fine)
    h.greet()
    n, width = HV.shape
    part = OV.shape[2]
    hid = U.shape[1]
    dh = part // heads_mp
    share = n // seq
    tiles = n // TILE
    GQKV, DO = U, GA
    packs = [Scatter(h, p, bufs, sems) for p in range(3)]
    PA, PI, PO = packs
    MINE = bufs[0]

    loads = [pltpu.make_async_copy(a, b, lsem.at[i]) for i, (a, b) in enumerate(((H, HV), (DY, DYV), (X, XV), (OFF, OFFV)))]
    for cp in loads:
        cp.start()

    def load_ff(m):
        slot = lax.rem(m, 2)
        return (
            pltpu.make_async_copy(W.at[1, m // 2, m % 2], BV.at[slot], wsem.at[0, slot]),
            pltpu.make_async_copy(W.at[2, m // 2, m % 2], CV.at[slot], wsem.at[1, slot]),
        )

    def load_attn(m):
        slot = lax.rem(m, 2)
        return (
            pltpu.make_async_copy(W.at[0, m // 2, m % 2], BV.at[slot], wsem.at[0, slot]),
            pltpu.make_async_copy(QKV.at[m], QV.at[slot], qsem.at[0, slot]),
            pltpu.make_async_copy(O.at[m], OV.at[slot], qsem.at[1, slot]),
            pltpu.make_async_copy(LSE.at[m], LV.at[slot], qsem.at[2, slot]),
        )

    def go(copies):
        for cp in copies:
            cp.start()

    def done(copies):
        for cp in copies:
            cp.wait()

    go(load_ff(0))
    SMALL[...] = jnp.zeros_like(SMALL)
    done(loads[:2])

    def prep(t):
        r = tile_rows(t, TILE)
        hid_in = HV[r, :]
        n2 = (hid_in * rsq(hid_in) * gain2[...].reshape(1, width)).astype(BF)
        N2[r, :] = n2
        N2T[:, r] = n2.T
        DYT[:, r] = DYV[r, :].T
        FF[r, :] = hid_in
        GN[r, :] = jnp.zeros((TILE, width), F32)

    loop(0, tiles, prep)

    def ff_group(m):
        slot = lax.rem(m, 2)
        done(load_ff(m))
        pl.when(m + 1 < nmp)(lambda: go(load_ff(m + 1)))

        def rowwise(t):
            r = tile_rows(t, TILE)
            b = BV[slot].reshape(width, hid)
            c = CV[slot].reshape(width, hid)
            a = dot(N2[r, :], b)
            gu = dot(DYV[r, :], c)
            u, slope = gelu_both(a)
            u = u.astype(BF)
            ga = (gu * slope).astype(BF)
            U[r, :] = u
            GA[r, :] = ga
            FF[r, :] += dot(u, c, 1, 1)
            GN[r, :] += dot(ga, b, 1, 1)

        loop(0, tiles, rowwise)

        @pl.when(m == 0)
        def _():
            h.met()

        @pl.when(m == 2)
        def _():
            PI.after_sib(0)
            PO.after_sib(0)

        PI.before_group(m)
        PO.before_group(m)
        to = PI.slot(m)

        def grads(t):
            r = tile_rows(t, TILE)
            MINE[1, to, r, :] = dot(N2T[r, :], GA[...]).astype(BF)
            MINE[2, to, r, :] = dot(DYT[r, :], U[...]).astype(BF)

        loop(0, width // TILE, grads)
        PI.after_group(m)
        PO.after_group(m)

    loop(0, nmp, ff_group)
    go(load_attn(0))
    done(loads[2:])

    def mid(t):
        r = tile_rows(t, TILE)
        hid_in = HV[r, :]
        r2 = rsq(hid_in)
        nh = hid_in * r2
        g = GN[r, :]
        SMALL[1:2, :] += jnp.sum(g * nh, axis=0, keepdims=True)
        e = g * gain2[...].reshape(1, width)
        gh = DYV[r, :].astype(F32) + r2 * (e - nh * jnp.mean(e * nh, axis=-1, keepdims=True))
        DYV[r, :] = FF[r, :].astype(BF)
        HV[r, :] = gh
        low = gh.astype(BF)
        N2[r, :] = low
        DYT[:, r] = low.T
        x = XV[r, :].astype(F32)
        N2T[:, r] = (x * rsq(x) * gain1[...].reshape(1, width)).astype(BF).T
        GN[r, :] = jnp.zeros((TILE, width), F32)

    loop(0, tiles, mid)
    sl = Swap(h, L, DYV, tsem, True)
    si = Swap(h, I, XV, dsem, True)

    ticks = {
        (0, 0, 0): lambda: PI.after_sib(1) or PO.after_sib(1) or sl.start(),
        (0, 1, 0): lambda: PI.after_y(0),
        (0, 1, 1): lambda: PO.after_y(0),
        (2, 0, 0): lambda: PI.after_y(1),
        (2, 0, 1): lambda: PO.after_y(1),
        (2, 0, 2): lambda: PA.after_sib(0),
        (2, 1, 0): lambda: PI.after_z(0) or PO.after_z(0),
        (3, 1, 0): lambda: PA.after_y(0),
    }

    def attn_group(m):
        slot = lax.rem(m, 2)
        done(load_attn(m))
        pl.when(m + 1 < nmp)(lambda: go(load_attn(m + 1)))
        toeplitz(OFFV.at[m], ST)
        D[...] = jnp.zeros_like(D)

        def project(t):
            r = tile_rows(t, TILE)
            w = BV[slot, :, :, :, 3 * part :].reshape(width, part)
            DO[r, :part] = dot(N2[r, :], w).astype(BF)

        loop(0, tiles, project)

        def pair(p):
            base = pl.multiple_of(p * seq, seq)
            off = jnp.where(lens[h.mp * share + p] < seq, -1e30, 0.0).astype(F32)
            for head in range(heads_mp):
                for (tm, tp, th), fn in ticks.items():
                    if th == head:
                        pl.when((m == tm) & (p == tp))(fn)
                attend_back(QV.at[slot], ST, DO, LV.at[slot], GQKV, D, head, part, dh, seq, off, base)

        loop(0, share, pair)
        PA.before_group(m)
        to = PA.slot(m)

        def grads(t):
            r = tile_rows(t, TILE)
            MINE[0, to, r, : 3 * part] = dot(N2T[r, :], GQKV[:, : 3 * part]).astype(BF)
            MINE[0, to, r, 3 * part :] = dot(DYT[r, :], OV[slot]).astype(BF)

        loop(0, width // TILE, grads)
        PA.after_group(m)

        def join(t):
            r = tile_rows(t, TILE)
            w = BV[slot, :, :, :, : 3 * part].reshape(width, 3 * part)
            GN[r, :] += dot(GQKV[r, : 3 * part], w, 1, 1)

        loop(0, tiles, join)
        sums = []
        for head in range(heads_mp):
            wide = jnp.concatenate([D[head], jnp.zeros((128, 128), F32)], 1)
            span = wide.shape[1]
            half = 64
            while half:
                wide = wide[:half] + pltpu.roll(wide[half:], span - half, 1)
                half //= 2
            sums.append(wide)
        sums = jnp.concatenate(sums + [jnp.zeros((8 - heads_mp, span), F32)], 0)
        at = pl.ds(pl.multiple_of(m * 128, 128), 128)
        SMALL[8:16, at] = dot(sums, onehot[...], 1, 1, HIGHEST)

    loop(0, nmp, attn_group)
    PA.after_sib(1)

    def last(t):
        r = tile_rows(t, TILE)
        x = XV[r, :].astype(F32)
        r1 = rsq(x)
        nx = x * r1
        g = GN[r, :]
        SMALL[0:1, :] += jnp.sum(g * nx, axis=0, keepdims=True)
        e = g * gain1[...].reshape(1, width)
        XV[r, :] = (HV[r, :] + r1 * (e - nx * jnp.mean(e * nx, axis=-1, keepdims=True))).astype(BF)

    loop(0, tiles, last)
    si.start()
    PI.after_z(1)
    PO.after_z(1)
    for i, who in enumerate((h.at(c=1 - h.c), h.at(x=1 - h.x), h.at(y=1 - h.y))):
        cp = remote(SMALL, SR.at[i], ssmall.at[i], rsmall.at[i], who)
        cp.start()
        cp.wait()
        SMALL[...] += SR[i]
    SZ[h.z] = SMALL[...]

    def zsmall(k, mine):
        z = h.zi(k)
        at = SZ.at[h.z if mine else z]
        return remote(at, at, ssmall.at[3 + z], rsmall.at[3 + (h.z if mine else z)], h.at(z=z))

    loop(1, h.nz, lambda k: zsmall(k, True).start())
    PA.after_y(1)
    loop(1, h.nz, lambda k: zsmall(k, False).wait_recv())
    SMALL[...] = lax.fori_loop(1, h.nz, lambda z, acc: acc + SZ[z], SZ[0])
    PA.after_z(0)
    GI[...] = PI.result()
    GF[...] = PO.result().T
    PA.after_z(1)
    ga = PA.result()
    GQ[...] = ga[:, :part]
    GK[...] = ga[:, part : 2 * part]
    GV[...] = ga[:, 2 * part : 3 * part]
    GO[...] = ga[:, 3 * part :].T
    for P_ in packs:
        P_.sent()
    loop(1, h.nz, lambda k: zsmall(k, True).wait_send())
    sl.come()
    sl.sent()
    si.come()
    si.sent()


def backward(H, X, DY, W, QKV, O, LSE, OFF, gain1, gain2, onehot, lens, shards, positions, ndp, nmp, fine, heads_mp):
    n, width = H.shape
    _, _, _, nz, _, rows, hid = W.shape
    part = O.shape[2]
    seq = positions * nmp
    share = n // seq
    any_ = pl.BlockSpec(memory_space=pl.ANY)
    vm = pl.BlockSpec(memory_space=pltpu.VMEM)
    dma = pltpu.SemaphoreType.DMA
    sds = jax.ShapeDtypeStruct
    bf = lambda *s: pltpu.VMEM(s, BF)
    fl = lambda *s: pltpu.VMEM(s, F32)
    act = sds((share * nmp, positions, width), BF)
    return pl.pallas_call(
        functools.partial(backward_kernel, (ndp, nmp, fine, seq, heads_mp)),
        out_shape=(act, act) + tuple(sds(s, F32) for s in shards) + (sds((16, width), F32),),
        in_specs=[any_] * 8 + [vm] * 3 + [pl.BlockSpec(memory_space=pltpu.SMEM)],
        out_specs=(any_, any_) + (vm,) * 7,
        scratch_shapes=[
            fl(n, width),
            bf(n, width),
            bf(n, width),
            bf(n, width),
            bf(width, n),
            bf(width, n),
            bf(n, hid),
            bf(n, hid),
            fl(n, width),
            fl(n, width),
            bf(2, nz, 2, rows, hid),
            bf(2, nz, 2, rows, hid),
            bf(2, n, 3 * part),
            bf(2, n, part),
            fl(2, 8, n),
            fl(nmp, 8, 2 * seq),
            fl(heads_mp, 128, 2 * seq - 128),
            fl(heads_mp, 128, 2 * seq - 128),
            bf(3, 3, width, hid),
            bf(3, 2, width, hid),
            bf(3, 2, nz, rows, hid),
            bf(3, 2, nz, rows, hid),
            bf(3, rows, hid),
            fl(3, rows, hid),
            fl(3, 16, width),
            fl(nz, 16, width),
            dma((4,)),
            dma((2, 2)),
            dma((3, 2)),
            dma((2, nmp, share)),
            dma((2, nmp, share)),
            dma((3 + nz,)),
            dma((3 + nz,)),
            dma((3, 2)),
            dma((3, 2)),
            dma((3, 2, nz)),
            dma((3, 2, nz)),
            dma((3, 2, nz)),
            dma((3, 2, nz)),
            dma((3, 1)),
            dma((3, 1)),
        ],
        compiler_params=pltpu.CompilerParams(collective_id=1, has_side_effects=True, vmem_limit_bytes=62 * MIB),
    )(H, X, DY, W, QKV, O, LSE, OFF, gain1, gain2, onehot, lens)


def body(tokens, cotangent, lengths, gain_attn, gain_ff, bias_table, w_query, w_key, w_value, w_out_attn, w_in_ff, w_out_ff):
    ndp, nmp = lax.axis_size("dp"), lax.axis_size("mp")
    positions = tokens.shape[1]
    seq = positions * nmp
    buckets, heads_mp = bias_table.shape
    fine = 16 // math.gcd(w_query.shape[0], 16)
    groups = [list(range(g, g + fine)) for g in range(0, ndp, fine)]

    def join(a, dim):
        return a if fine == 1 else lax.all_gather(a, "dp", axis=dim, tiled=True, axis_index_groups=groups)

    def split(a, dim):
        if fine == 1:
            return a
        return lax.psum_scatter(a, "dp", scatter_dimension=dim, tiled=True, axis_index_groups=groups)

    dims = (0, 0, 0, 1, 0, 1)
    ws = tuple(join(w, d) for w, d in zip((w_query, w_key, w_value, w_out_attn, w_in_ff, w_out_ff), dims))
    place = np.arange(2 * seq)
    place = np.where(place < 2 * seq - 128, seq - 128 - place, seq - 128 + 2 * seq - place)
    onehot = (bucket_of(place, buckets)[None] == np.arange(128)[:, None]).astype(np.float32)
    W, X, DY, OFF, H, QKV, O, LSE = forward(
        tokens, cotangent, ws, bias_table, onehot[:buckets], gain_attn, lengths, ndp, nmp, fine
    )
    layer, ing, *grads, small = backward(
        H, X, DY, W, QKV, O, LSE, OFF, gain_attn, gain_ff, onehot, lengths, [w.shape for w in ws],
        positions, ndp, nmp, fine, heads_mp,
    )
    if fine > 1:
        small = lax.psum(small, "dp", axis_index_groups=groups)
    gb = lax.dynamic_slice(small, (8, lax.axis_index("mp") * 128), (heads_mp, buckets)).T
    return (layer, ing, small[0], small[1], gb) + tuple(split(g, d) for g, d in zip(grads, dims))


def solution(mesh):
    act = P("dp", "mp", None)
    rows, cols = P("dp", "mp"), P("mp", "dp")
    return jax.shard_map(
        body,
        mesh=mesh,
        in_specs=(act, act, P("dp"), P(), P(), P(None, "mp"), rows, rows, rows, cols, rows, cols),
        out_specs=(act, act, P(), P(), P(None, "mp"), rows, rows, rows, cols, rows, cols),
        check_vma=False,
    )
```

time: 1100 us -> 278 us (0.25)
  the two profiles are of different devices: /device:TPU:1 before, /device:TPU:26 now
where the time goes in v2:
time: 278 us
  Pallas kernels  262 us (94%)
  local copies, waits for them, and re-layouts  15.1 us (5%)
    pallas_call x1, Pallas kernels, backward(): pl.pallas_call(functools.partial(backward_kernel, (ndp, nmp, fine, seq, h...  166 us
    pallas_call x1, Pallas kernels, forward(): pl.pallas_call(functools.partial(forward_kernel, (ndp, nmp, fine, seq, he...  96.5 us
    unnamed x22, local copies, waits for them, and re-layouts  12.3 us

profile of v2, /device:TPU:26, one launch (start us, length us, event | category | flops | bytes accessed | tf_op | source)
XLA Modules:
  0.0 278.0 jit_solution(14147581988566045689)
XLA Ops:
  0.6 1.9 copy.25.wf
  2.5 1.4 copy.26.table
  3.9 96.5 %shard_map.221 = (bf16[3,2,2,4,2,96,768]{6,5,4,3,2,1,0:T(8,128)(2,1)}, bf16[1024,768]{1,0:T(8,128)(2,1)}, bf16[1024,768]{1,0:T(8,128)(2,1)}, f32[4,8,1024]{2,1,0...) custom-call(bf16[8,128,768]{2,1,0:T(8,128)(2,1)} %tok.1, ...), custom_call_target="tpu_custom_call" | custom-call | tf_op jit(solution)/shard_map/pallas_call | solution.py:482
  100.4 165.7 %shard_map.222 = (bf16[8,128,768]{2,1,0:T(8,128)(2,1)}, bf16[8,128,768]{2,1,0:T(8,128)(2,1)}, f32[96,192]{1,0:T(8,128)}, f32[96,192]{1,0:T(8,128)}, f32[96,192]{...) custom-call(f32[1024,768]{1,0:T(8,128)} %get-tuple-element.28.H, ...), custom_call_target="tpu_custom_call" | custom-call | tf_op jit(solution)/shard_map/pallas_call | solution.py:914
  266.1 1.9 copy.27
  268.0 1.3 dynamic-slice_bitcast_fusion
  269.3 1.4 slice_reduce_fusion
  270.8 0.0 copy-start
  270.8 2.8 copy.35
  273.5 0.0 copy-done
  273.5 0.0 copy-start.5
  273.5 0.0 copy-start.4
  273.5 0.0 copy-start.3
  273.6 0.0 copy-start.2
  273.6 0.0 copy-start.1
  273.6 1.1 copy.36
  274.7 0.0 copy-done.5
  274.7 0.6 copy.37
  275.4 0.0 copy-done.4
  275.4 0.6 copy.38
  276.0 0.0 copy-done.3
  276.0 0.6 copy.39
  276.7 0.0 copy-done.2
  276.7 0.6 copy.40
  277.3 0.0 copy-done.1
  277.3 0.7 copy.41
Async XLA Ops:
  270.8 2.8 copy-start
  273.5 1.2 copy-start.5
  273.5 1.8 copy-start.4
  273.5 2.5 copy-start.3
  273.6 3.1 %copy-start.2 = (f32[192,96]{1,0:T(8,128)S(1)}, f32[192,96]{1,0:T(8,128)}, u32[]{:S(2)}) copy-start(f32[192,96]{1,0:T(8,128)} %get-tuple-element.77) | copy-start | bytes 221188
  273.6 3.7 %copy-start.1 = (f32[96,768]{1,0:T(8,128)S(1)}, f32[96,768]{1,0:T(8,128)}, u32[]{:S(2)}) copy-start(f32[96,768]{1,0:T(8,128)} %get-tuple-element.78) | copy-start | bytes 884740

commit v3 on v0

v3 whole, which is shorter than its diff:
```python
import functools
import math

import jax
import jax.numpy as jnp
import numpy as np
from jax import lax
from jax.experimental import pallas as pl
from jax.experimental.pallas import tpu as pltpu
from jax.sharding import PartitionSpec as P

BF = jnp.bfloat16
F32 = jnp.float32
MESH = pl.DeviceIdType.MESH
EPS = 1e-06
FAR = 128
HIGHEST = lax.Precision.HIGHEST
MIB = 2**20


def bucket_of(offset, count):
    half = count // 2
    upper = (offset > 0).astype(np.int64) * half
    distance = np.abs(offset)
    exact = half // 2
    scaled = np.log(np.maximum(distance, 1) / exact) / np.log(FAR / exact) * (half - exact)
    larger = np.minimum(exact + scaled.astype(np.int64), half - 1)
    return (upper + np.where(distance < exact, distance, larger)).astype(np.int32)

PLAN = {
    ("start", 0): ("C.Y0", "A.X0",),
    ("start", 1): ("A.plane2",),
    ("start", 2): ("B.Y0",),
    ("start", 3): ("B.Zs", "dy",),
    ("attend", 0): ("A.z2y",),
    ("attend", 2): ("A.ds", "C.Zs", "B.zy",),
    ("attend", 3): ("B.Xs",),
    ("attend", 4): ("C.zy", "B.ys", "C.Xs",),
    ("attend", 7): ("B.xd", "C.ys", "C.DX",),
    ("ff", 3): ("C.xd",),
    ("ff", 4): ("B.ds",),
    ("ff", 9): ("C.ds",),
    ("ff", 11): ("PO.sw0",),
    ("ff", 19): ("PO.yw0",),
    ("ff", 21): ("PO.sw1", "PI.xs0",),
    ("back", 0): ("lay", "PO.yw1", "PO.st1",),
    ("back", 1): ("PO.st0",),
    ("back", 2): ("PI.xs1", "PI.xw0", "PO.yt0",),
    ("back", 3): ("PA.st0", "PO.yt1",),
    ("back", 4): ("PI.xy0", "PA.st1", "PA.yt0",),
    ("back", 6): ("PI.xw1", "PO.zt0", "PA.yt1",),
    ("back", 7): ("PI.xy1", "PA.sw0",),
    ("end", 1): ("PA.yw0",),
    ("end", 3): ("PO.zw1", "PA.sw1",),
    ("end", 4): ("PI.zo1",),
    ("end", 5): ("PI.zo0", "PA.zw0", "PA.zt1", "PO.zt1", "PA.zt0", "PA.yw1", "PO.zw0", "PA.zw1",),
}
MODES = {"A": "plane", "B": "zxy", "C": "half"}
X_FIRST = {"PA": False, "PI": True, "PO": False}
A_BY_HOPS = True


class Place:
    def __init__(self, ndp, nmp, fine, rows):
        self.dp, self.mp = lax.axis_index("dp"), lax.axis_index("mp")
        self.x, self.c = self.mp // 2, self.mp % 2
        self.fine = fine
        self.z, self.y = self.dp // fine // 2, self.dp // fine % 2
        self.nz = ndp // fine // 2
        self.nmp, self.rows = nmp, rows

    def at(self, x=None, c=None, z=None, y=None):
        x = self.x if x is None else x
        c = self.c if c is None else c
        z = self.z if z is None else z
        y = self.y if y is None else y
        return ((z * 2 + y) * self.fine + self.dp % self.fine, x * 2 + c)

    def zi(self, k):
        return lax.rem(self.z + k, self.nz)

    def block(self, z, y, count=1):
        return pl.ds(pl.multiple_of((z * 2 + y) * self.rows, self.rows), count * self.rows)

    def greet(self):
        bar = pltpu.get_barrier_semaphore()

        def tell(who):
            pl.semaphore_signal(bar, inc=1, device_id=who, device_id_type=MESH)

        tell(self.at(c=1 - self.c))
        tell(self.at(x=1 - self.x))
        tell(self.at(x=1 - self.x, c=1 - self.c))
        tell(self.at(y=1 - self.y))
        loop(1, self.nz, lambda k: tell(self.at(z=self.zi(k))))

    def met(self):
        pl.semaphore_wait(pltpu.get_barrier_semaphore(), 4 + self.nz - 1)


def remote(src, dst, ssem, rsem, who):
    return pltpu.make_async_remote_copy(
        src_ref=src, dst_ref=dst, send_sem=ssem, recv_sem=rsem, device_id=who, device_id_type=MESH
    )


def loop(lo, hi, fn):
    def step(k, carry):
        fn(k)
        return carry

    lax.fori_loop(lo, hi, step, 0)


class Gather:
    def __init__(self, here, pack, mode, W, ssem, rsem):
        self.h, self.nz, self.mode = here, here.nz, mode
        self.W = W.at[pack]
        self.ss, self.rs = ssem.at[pack], rsem.at[pack]

    def at(self, x, c, z, y):
        return self.W.at[x, c, self.h.block(z, y)]

    def send(self, src, kind, idx, who, skind=None, sidx=None):
        skind = kind if skind is None else skind
        sidx = idx if sidx is None else sidx
        return remote(src, src, self.ss.at[skind, sidx], self.rs.at[kind, idx], who)

    def hop(self, b, step):
        h = self.h
        return self.send(self.at(h.x, h.c, b, h.y), 0, b, h.at(z=h.z + step), 0 if step > 0 else 7)

    def z(self, z, mine=True):
        h = self.h
        b = h.z if mine else z
        return self.send(self.at(h.x, h.c, b, h.y), 0, b, h.at(z=z), sidx=z)

    def y(self, z, mine=True):
        h = self.h
        return self.send(self.at(h.x, h.c, z, h.y if mine else 1 - h.y), 1, z, h.at(y=1 - h.y))

    def x(self, z, mine=True):
        h = self.h
        return self.send(self.at(h.x if mine else 1 - h.x, h.c, z, h.y), 2, z, h.at(x=1 - h.x))

    def diag_by_x(self, z):
        h = self.h
        return self.send(self.at(h.x, h.c, z, 1 - h.y), 3, z, h.at(x=1 - h.x))

    def diag_by_y(self, z):
        h = self.h
        return self.send(self.at(1 - h.x, h.c, z, h.y), 3, z, h.at(y=1 - h.y))

    def diag(self, z):
        h = self.h
        return self.send(self.at(1 - h.x, h.c, z, 1 - h.y), 3, z, h.at(x=1 - h.x))

    def z2(self, z, mine=True):
        h = self.h
        b = h.z if mine else z
        return self.send(self.at(1 - h.x, h.c, b, h.y), 4, b, h.at(z=z), sidx=z)

    def sib(self, half, z, mine=True):
        h = self.h
        block = self.W.at[h.x if half == 0 else 1 - h.x, h.c if mine else 1 - h.c, h.block(z, 0, 2)]
        return self.send(block, 5 + half, z, h.at(c=1 - h.c))

    def sib_wait(self, half):
        self.all(lambda z: self.sib(half, z, False).wait_recv())

    def all(self, fn):
        loop(0, self.nz, lambda k: fn(self.h.zi(k)))

    def others(self, fn):
        loop(1, self.nz, lambda k: fn(self.h.zi(k)))

    def by_x(self, z, fn):
        if self.mode == "half":
            pl.when(z % 2 == 0)(fn)

    def by_y(self, z, fn):
        if self.mode == "half":
            pl.when(z % 2 == 1)(fn)
        else:
            fn()

    def hops(self):
        h = self.h
        for step in (1, -1):
            pl.when((h.z + step >= 0) & (h.z + step < self.nz))(lambda: self.hop(h.z, step).start())
        self.y(h.z).start()

    def hops_on(self):
        h = self.h

        def on(d):
            for step in (1, -1):
                b = h.z - step * d

                @pl.when((b >= 0) & (b < self.nz))
                def _():
                    self.z(b, False).wait_recv()
                    pl.when((h.z + step >= 0) & (h.z + step < self.nz))(lambda: self.hop(b, step).start())
                    self.y(b).start()

        loop(1, self.nz, on)

    def hops_sent(self):
        h = self.h

        def on(b):
            pl.when((b <= h.z) & (h.z + 1 < self.nz))(lambda: self.hop(b, 1).wait_send())
            pl.when((b >= h.z) & (h.z >= 1))(lambda: self.hop(b, -1).wait_send())

        loop(0, self.nz, on)

    def steps(self):
        h = self.h

        def zy(z):
            self.z(z, False).wait_recv()
            self.y(z).start()

        def ys(z):
            self.y(z, False).wait_recv()
            self.sib(0, z).start()

        def z2y(z):
            self.z2(z, False).wait_recv()
            self.diag_by_y(z).start()

        def xd(z):
            self.x(z, False).wait_recv()
            self.by_y(z, lambda: self.diag_by_y(z).start())

        def ds(z):
            self.diag(z).wait_recv()
            self.sib(1, z).start()

        def plane2():
            self.x(h.z, False).wait_recv()
            self.others(lambda z: self.z2(z).start())
            self.diag_by_y(h.z).start()

        return {
            "Zs": lambda: self.others(lambda z: self.z(z).start()),
            "Y0": lambda: self.y(h.z).start(),
            "zy": lambda: self.others(zy),
            "ys": lambda: self.all(ys),
            "X0": lambda: self.x(h.z).start(),
            "plane2": plane2,
            "z2y": lambda: self.others(z2y),
            "Xs": lambda: self.all(lambda z: self.x(z).start()),
            "DX": lambda: self.all(lambda z: self.by_x(z, lambda: self.diag_by_x(z).start())),
            "xd": lambda: self.all(xd),
            "ds": lambda: self.all(ds),
        }

    def sent(self):
        self.all(lambda z: self.y(z).wait_send())
        self.all(lambda z: self.sib(0, z).wait_send())
        self.all(lambda z: self.sib(1, z).wait_send())
        if self.mode == "plane":
            self.x(self.h.z).wait_send()
            self.others(lambda z: self.z2(z).wait_send())
            self.all(lambda z: self.diag_by_y(z).wait_send())
        else:
            self.all(lambda z: self.x(z).wait_send())
            self.all(lambda z: self.by_x(z, lambda: self.diag_by_x(z).wait_send()))
            self.all(lambda z: self.by_y(z, lambda: self.diag_by_y(z).wait_send()))


class Swap:
    def __init__(self, here, whole, flat, sems, back):
        self.h, self.whole, self.flat, self.sems, self.back = here, whole, flat, sems, back
        self.positions = whole.shape[1]
        self.share = whole.shape[0] // here.nmp

    def views(self, s, outer, inner):
        at = pl.multiple_of((s * self.h.nmp + inner) * self.positions, self.positions)
        return self.whole.at[outer * self.share + s], self.flat.at[pl.ds(at, self.positions)]

    def copy(self, s, k, mine):
        h = self.h
        other = lax.rem(h.mp + (k if mine else h.nmp - k), h.nmp)
        sender, receiver = (h.mp, other) if mine else (other, h.mp)
        if self.back:
            dst, src = self.views(s, sender, receiver)
        else:
            src, dst = self.views(s, receiver, sender)
        if not mine:
            src = dst
        return remote(src, dst, self.sems.at[0, k, s], self.sems.at[1, k, s], (h.dp, other))

    def local(self, s):
        whole, flat = self.views(s, self.h.mp, self.h.mp)
        src, dst = (flat, whole) if self.back else (whole, flat)
        return pltpu.make_async_copy(src, dst, self.sems.at[0, 0, s])

    def start(self, s):
        for k in range(1, self.h.nmp):
            self.copy(s, k, True).start()
        self.local(s).start()

    def start_all(self):
        for s in range(self.share):
            self.start(s)

    def come(self):
        for s in range(self.share):
            for k in range(1, self.h.nmp):
                self.copy(s, k, False).wait_recv()
            self.local(s).wait()

    def sent(self):
        for s in range(self.share):
            for k in range(1, self.h.nmp):
                self.copy(s, k, True).wait_send()


class Scatter:
    def __init__(self, here, pack, x_first, mine, bufs, RES, sems):
        self.h, self.nz, self.x_first = here, here.nz, x_first
        self.MINE, self.SENT = mine
        self.R0, self.R1, self.R2, self.R3 = [b.at[pack] for b in bufs]
        self.RES = RES.at[pack]
        self.sems = [s.at[pack] for s in sems]
        self.block = here.block

    def half(self, own):
        return self.h.x if own else 1 - self.h.x

    def put(self, m, columns, value):
        @pl.when(m % 2 == self.h.c)
        def _():
            self.MINE[m // 2, :, columns] = value

        @pl.when(m % 2 != self.h.c)
        def _():
            self.SENT[:, columns] = value

    def two(self, x, r):
        return self.MINE[x, r].astype(F32) + self.R0[x, r].astype(F32)

    def sib(self, x):
        return remote(self.SENT, self.R0.at[x], self.sems[0].at[x], self.sems[1].at[x], self.h.at(c=1 - self.h.c))

    def ysend(self, x, z):
        h = self.h
        src = self.MINE.at[x, self.block(z, 1 - h.y)]
        return remote(src, self.R1.at[x, z], self.sems[2].at[x, z], self.sems[3].at[x, z], h.at(y=1 - h.y))

    def zsend(self, x, z):
        h = self.h
        return remote(self.R1.at[x, z], self.R2.at[x, h.z], self.sems[4].at[x, z], self.sems[5].at[x, h.z], h.at(z=z))

    def zcome(self, x, z):
        h = self.h
        return remote(self.R2.at[x, z], self.R2.at[x, z], self.sems[4].at[x, z], self.sems[5].at[x, z], h.at(z=z))

    def xsend(self):
        h = self.h
        return remote(self.R1.at[1 - h.x, h.z], self.R3, self.sems[6].at[0], self.sems[7].at[0], h.at(x=1 - h.x))

    def xall(self, z, y_is_own, mine=True):
        h = self.h
        i = 2 if y_is_own else 4
        to = h.x if mine else 1 - h.x
        src = self.MINE.at[1 - h.x, self.block(z, h.y if y_is_own else 1 - h.y)]
        dst = (self.R1 if y_is_own else self.R2).at[to, z]
        return remote(src, dst, self.sems[i].at[1 - h.x, z], self.sems[i + 1].at[to, z], h.at(x=1 - h.x))

    def after_group(self, m):
        pl.when(m % 2 != self.h.c)(lambda: self.sib(m // 2).start())

    def before_group(self, m, i):
        pl.when((m % 2 != self.h.c) & (i >= 2))(lambda: self.sib(1 - m // 2).wait_send())

    def sib_sent(self, own):
        self.sib(self.half(own)).wait_send()

    def each(self, fn):
        loop(1, self.nz + 1, lambda k: fn(self.h.zi(k)))

    def others(self, fn):
        loop(1, self.nz, lambda k: fn(self.h.zi(k)))

    def after_sib(self, own):
        x = self.half(own)
        self.sib(x).wait_recv()

        def on(z):
            r = self.block(z, 1 - self.h.y)
            self.MINE[x, r] = self.two(x, r).astype(BF)
            self.ysend(x, z).start()

        self.each(on)

    def after_y(self, own):
        x = self.half(own)

        def on(z):
            self.ysend(x, z).wait_recv()
            total = self.two(x, self.block(z, self.h.y)) + self.R1[x, z].astype(F32)
            self.R1[x, z] = total.astype(BF)
            pl.when(z != self.h.z)(lambda: self.zsend(x, z).start())

        self.each(on)

    def after_z(self, own):
        h, x = self.h, self.half(own)
        self.others(lambda z: self.zcome(x, z).wait_recv())

        def add(k, acc):
            return acc + self.R2[x, h.zi(k)].astype(F32)

        total = lax.fori_loop(1, self.nz, add, self.R1[x, h.z].astype(F32))
        if own:
            self.RES[...] = total
        else:
            self.R1[x, h.z] = total.astype(BF)
            self.xsend().start()

    def to_x(self):
        x = self.half(False)
        self.sib(x).wait_recv()

        def on(z):
            for y_is_own in (True, False):
                r = self.block(z, self.h.y if y_is_own else 1 - self.h.y)
                self.MINE[x, r] = self.two(x, r).astype(BF)
                self.xall(z, y_is_own).start()

        self.each(on)

    def after_x(self):
        x = self.half(True)
        self.sib(x).wait_recv()

        def on(z):
            r = self.block(z, 1 - self.h.y)
            self.xall(z, False, False).wait_recv()
            self.MINE[x, r] = (self.two(x, r) + self.R2[1 - x, z].astype(F32)).astype(BF)
            self.ysend(x, z).start()

        self.each(on)

    def after_x_and_y(self):
        x = self.half(True)

        def on(z):
            self.xall(z, True, False).wait_recv()
            self.ysend(x, z).wait_recv()
            total = self.two(x, self.block(z, self.h.y)) + self.R1[x, z].astype(F32) + self.R1[1 - x, z].astype(F32)
            self.R1[x, z] = total.astype(BF)
            pl.when(z != self.h.z)(lambda: self.zsend(x, z).start())

        self.each(on)

    def steps(self):
        out = {}
        if self.x_first:
            fns = {"xs": self.to_x, "xw": self.after_x, "xy": self.after_x_and_y, "zo": lambda: self.after_z(True)}
        else:
            fns = {}
            for tag, own in (("w", True), ("t", False)):
                fns["s" + tag] = functools.partial(self.after_sib, own)
                fns["y" + tag] = functools.partial(self.after_y, own)
                fns["z" + tag] = functools.partial(self.after_z, own)
        for name, fn in fns.items():
            for c in (0, 1):
                out[name + str(c)] = functools.partial(self.on_core, c, fn)
        return out

    def on_core(self, c, fn):
        pl.when(self.h.c == c)(fn)

    def result(self):
        if not self.x_first:
            self.xsend().wait_recv()
            self.RES[...] += self.R3[...].astype(F32)

    def sent(self):
        own, other = self.half(True), self.half(False)
        for x in (own,) if self.x_first else (own, other):
            self.each(lambda z: self.ysend(x, z).wait_send())
            self.others(lambda z: self.zsend(x, z).wait_send())
        if self.x_first:
            self.each(lambda z: self.xall(z, True).wait_send())
            self.each(lambda z: self.xall(z, False).wait_send())
        else:
            self.xsend().wait_send()


def dot(a, b, ca=1, cb=0, precision=None):
    return lax.dot_general(a, b, (((ca,), (cb,)), ((), ())), preferred_element_type=F32, precision=precision)


def tile_rows(i, size):
    return pl.ds(pl.multiple_of(i * size, size), size)


TILE = 256


def rsq(v):
    return lax.rsqrt(jnp.mean(v * v, axis=-1, keepdims=True) + EPS)


def toeplitz(offsets, ST):
    heads, span = ST.shape[0], ST.shape[2]
    for h in range(heads):
        row = jnp.broadcast_to(offsets[h : h + 1, :], (128, offsets.shape[1]))
        ST[h] = pltpu.roll(row, 0, 1, stride=1, stride_axis=0)[:, :span]


def biased(s, ST, h, dead):
    blocks = s.shape[0] // 128
    pieces = []
    for j in range(blocks):
        c0 = 128 * (blocks - 1 - j)
        piece = s[128 * j : 128 * (j + 1)] + ST[h, :, c0 : c0 + s.shape[1]]
        pieces.append(piece if j < blocks // 2 else piece + dead)
    return jnp.concatenate(pieces, 0)


def attend(QV, ST, h, part, dh, seq, dead, base, OV, LV):
    q0, k0, v0 = h * dh, part + h * dh, 2 * part + h * dh
    rows = pl.ds(base, seq)
    queries, keys, values = QV[rows, q0 : q0 + dh], QV[rows, k0 : k0 + dh], QV[rows, v0 : v0 + dh]
    s = biased(dot(keys, queries, 1, 1), ST, h, dead)
    top = jnp.max(s, axis=0, keepdims=True)
    e = jnp.exp(s - top)
    total = jnp.sum(e, axis=0, keepdims=True)
    prob = (e * (1.0 / total)).astype(BF)
    OV[rows, h * dh : (h + 1) * dh] = dot(prob, values, 0, 0).astype(BF)
    LV[h : h + 1, rows] = top + jnp.log(total)


GELU_C = float(np.sqrt(2.0 / np.pi))


def gelu_both(a):
    a2 = a * a
    t = jnp.tanh(a * (GELU_C + (GELU_C * 0.044715) * a2))
    half = 0.5 + 0.5 * t
    slope = half + (0.5 * a) * (1.0 - t * t) * (GELU_C + (3.0 * GELU_C * 0.044715) * a2)
    return a * half, slope


def attend_back(QV, ST, DO, LV, GQKV, D, h, part, dh, seq, dead, base):
    rows = pl.ds(base, seq)
    q0, k0, v0 = h * dh, part + h * dh, 2 * part + h * dh
    queries, keys, values = QV[rows, q0 : q0 + dh], QV[rows, k0 : k0 + dh], QV[rows, v0 : v0 + dh]
    d_o = DO[rows, h * dh : (h + 1) * dh]
    s = biased(dot(keys, queries, 1, 1), ST, h, dead)
    prob = jnp.exp(s - LV[h : h + 1, rows])
    dprob = dot(values, d_o, 1, 1)
    weighted = prob * dprob
    delta = jnp.sum(weighted, axis=0, keepdims=True)
    gs = (weighted - prob * delta).astype(BF)
    GQKV[rows, v0 : v0 + dh] = dot(prob.astype(BF), d_o).astype(BF)
    GQKV[rows, k0 : k0 + dh] = dot(gs, queries).astype(BF)
    GQKV[rows, q0 : q0 + dh] = dot(keys.T, gs).astype(BF).T
    blocks = seq // 128
    for d in range(1 - blocks, blocks):
        c0 = 128 * (blocks - 1 - d)
        acc = D[h, :, c0 : c0 + 128]
        for j in range(max(0, d), min(blocks, blocks + d)):
            acc += gs[128 * j : 128 * (j + 1), 128 * (j - d) : 128 * (j - d + 1)].astype(F32)
        D[h, :, c0 : c0 + 128] = acc


def layer_kernel(cfg, tok, cot, wq, wk, wv, wo, wi, wf_t, table_t, onehot, gain1, gain2, lens, *refs):
    ndp, nmp, fine, seq, heads_mp = cfg
    L, I, RES, SMALL, W, QKV, O, LSE = refs[:8]
    OWN, OFFV, XV, DYV, N2, N2T, DYT, U, GA, HV, FF, GN, BV, CV, QV, OV, LV, ST, D = refs[8:27]
    FFMINE, SENT = refs[27:29]
    bufs, SR, SZ = refs[29:33], refs[33], refs[34]
    ssem, rsem, xsem, dysem, lsem, isem, bsem, osem, wsem, qsem, ssmall, rsmall, csem = refs[35:48]
    sems = refs[48:56]
    rows, part = wq.shape
    h = Place(ndp, nmp, fine, rows)
    h.greet()
    n, width = XV.shape
    hid = U.shape[1]
    dh = part // heads_mp
    share = n // seq
    tiles = n // TILE
    nz = h.nz

    def gain(ref):
        return ref[...].reshape(1, width)

    def go(copies):
        for cp in copies:
            cp.start()

    def done(copies):
        for cp in copies:
            cp.wait()

    def run(section, at, static=None, period=1):
        for (name, slot), steps in PLAN.items():
            if name == section and (slot == at if static is None else slot % period in static):

                def fn(steps=steps):
                    for step in steps:
                        ACTIONS[step]()

                if static is None:
                    fn()
                else:
                    pl.when(at == slot)(fn)

    OWN[0, :, :part] = wq[...].astype(BF)
    OWN[0, :, part : 2 * part] = wk[...].astype(BF)
    OWN[0, :, 2 * part : 3 * part] = wv[...].astype(BF)
    OWN[0, :, 3 * part :] = wo[...].T.astype(BF)
    OWN[1] = wi[...].astype(BF)
    OWN[2] = wf_t[...].astype(BF)
    own = [pltpu.make_async_copy(OWN.at[p], W.at[p, h.x, h.c, h.block(h.z, h.y)], csem.at[p]) for p in range(3)]
    go(own)
    OFFV[h.mp] = jnp.zeros_like(OFFV[0])
    OFFV[h.mp, :heads_mp] = dot(table_t[...], onehot[: table_t.shape[1], :], 1, 0, HIGHEST)

    def offs(k, mine=True):
        other = lax.rem(h.mp + (k if mine else nmp - k), nmp)
        at = OFFV.at[h.mp if mine else other]
        return remote(at, at, bsem.at[0, k], bsem.at[1, k], (h.dp, other))

    A, B, C = [Gather(h, p, MODES[name], W, ssem, rsem) for p, name in enumerate("ABC")]
    mines = (CV, SENT.at[0]), (FFMINE.at[0], SENT.at[0]), (FFMINE.at[1], SENT.at[1])
    PA, PI, PO = [
        Scatter(h, p, X_FIRST[name], mines[p], bufs, RES, sems) for p, name in enumerate(("PA", "PI", "PO"))
    ]
    sx = Swap(h, tok, XV, xsem, False)
    sd = Swap(h, cot, DYV, dysem, False)
    sl = Swap(h, L, DYV, lsem, True)
    si = Swap(h, I, XV, isem, True)

    ACTIONS = {"dy": sd.start_all, "lay": sl.start_all}
    for name, part_of in (("A", A), ("B", B), ("C", C), ("PA", PA), ("PI", PI), ("PO", PO)):
        ACTIONS.update({name + "." + step: fn for step, fn in part_of.steps().items()})

    done(own)
    h.met()
    if A_BY_HOPS:
        A.hops()
    else:
        ACTIONS["A.Zs"]()
        ACTIONS["A.Y0"]()
    sx.start_all()
    for k in range(1, nmp):
        offs(k).start()
    run("start", 0)
    if A_BY_HOPS:
        A.hops_on()
    else:
        ACTIONS["A.zy"]()
    run("start", 1)
    ACTIONS["A.ys"]()
    run("start", 2)
    sx.come()
    run("start", 3)
    A.sib_wait(0)

    def group(i):
        return lax.rem(2 * h.x + i, nmp)

    def load(p, i, m, V, sem):
        slot = lax.rem(i, 2)
        return pltpu.make_async_copy(W.at[p, m // 2, m % 2], V.at[slot], sem.at[slot])

    def load_a(i):
        return load(0, i, group(i), BV, wsem.at[0])

    def store(i):
        m, slot = group(i), lax.rem(i, 2)
        return (
            pltpu.make_async_copy(QV.at[slot], QKV.at[m], osem.at[0, slot]),
            pltpu.make_async_copy(OV.at[slot], O.at[m], osem.at[1, slot]),
            pltpu.make_async_copy(LV.at[slot], LSE.at[m], osem.at[2, slot]),
        )

    load_a(0).start()
    for k in range(1, nmp):
        offs(k, False).wait_recv()

    def norm(t):
        r = tile_rows(t, TILE)
        x = XV[r, :].astype(F32)
        N2[r, :] = (x * rsq(x) * gain(gain1)).astype(BF)
        HV[r, :] = x

    loop(0, tiles, norm)

    def attn_group(i):
        slot = lax.rem(i, 2)
        m = group(i)

        @pl.when(i == 2)
        def _():
            A.sib_wait(1)
            load_a(2).start()

        load_a(i).wait()
        pl.when((i == 0) | (i == 2))(lambda: load_a(i + 1).start())
        pl.when(i >= 2)(lambda: done(store(i - 2)))
        toeplitz(OFFV.at[m], ST)

        QV[slot] = dot(N2[...], BV[slot, :, : 3 * part]).astype(BF)

        def pair(p):
            base = pl.multiple_of(p * seq, seq)
            off = jnp.where(lens[h.mp * share + p] < seq, -1e30, 0.0).astype(F32)
            run("attend", i * share + p, range(1))
            for head in range(heads_mp):
                attend(QV.at[slot], ST, head, part, dh, seq, off, base, OV.at[slot], LV.at[slot])

        loop(0, share, pair)

        HV[...] += dot(OV[slot], BV[slot, :, 3 * part :], 1, 1)
        go(store(i))

    loop(0, nmp, attn_group)

    run("between", 0)

    def load_ff(i):
        m = group(i)
        return load(1, i, m, BV, wsem.at[0]), load(2, i, m, CV, wsem.at[1])

    sd.come()
    SMALL[...] = jnp.zeros_like(SMALL)

    def prep(t):
        r = tile_rows(t, TILE)
        hidden = HV[r, :]
        n2 = (hidden * rsq(hidden) * gain(gain2)).astype(BF)
        N2[r, :] = n2
        N2T[:, r] = n2.T
        DYT[:, r] = DYV[r, :].T
        FF[r, :] = hidden
        GN[r, :] = jnp.zeros((TILE, width), F32)

    loop(0, tiles, prep)
    run("between", 1)
    B.sib_wait(0)
    C.sib_wait(0)
    go(load_ff(0))

    steps = tiles + 2

    def ff_group(i):
        slot = lax.rem(i, 2)
        m = group(i)
        done(load_ff(i))
        pl.when((i == 0) | (i == 2))(lambda: go(load_ff(i + 1)))

        def rowwise(t):
            run("ff", i * steps + t, range(tiles), steps)
            r = tile_rows(t, TILE)
            b = BV[slot]
            c = CV[slot]
            a = dot(N2[r, :], b)
            gu = dot(DYV[r, :], c)
            u, slope = gelu_both(a)
            u = u.astype(BF)
            ga = (gu * slope).astype(BF)
            U[r, :] = u
            GA[r, :] = ga
            FF[r, :] += dot(u, c, 1, 1)
            GN[r, :] += dot(ga, b, 1, 1)

        loop(0, tiles, rowwise)
        PI.before_group(m, i)
        PO.before_group(m, i)

        run("ff", i * steps + tiles, (tiles,), steps)
        PI.put(m, slice(None), dot(N2T[...], GA[...]).astype(BF))
        run("ff", i * steps + tiles + 1, (tiles + 1,), steps)
        PO.put(m, slice(None), dot(DYT[...], U[...]).astype(BF))
        PI.after_group(m)
        PO.after_group(m)

        @pl.when(i == 1)
        def _():
            run("between", 2)
            B.sib_wait(1)
            C.sib_wait(1)
            go(load_ff(2))

    loop(0, nmp, ff_group)

    def back_group(i):
        return lax.rem(2 * (1 - h.x) + i, nmp)

    def load_attn(i):
        m, slot = back_group(i), lax.rem(i, 2)
        return (
            load(0, i, m, BV, wsem.at[0]),
            pltpu.make_async_copy(QKV.at[m], QV.at[slot], qsem.at[0, slot]),
            pltpu.make_async_copy(O.at[m], OV.at[slot], qsem.at[1, slot]),
            pltpu.make_async_copy(LSE.at[m], LV.at[slot], qsem.at[2, slot]),
        )

    for i in (nmp - 2, nmp - 1):
        done(store(i))
    go(load_attn(0))
    run("between", 3)

    def mid(t):
        r = tile_rows(t, TILE)
        hidden = HV[r, :]
        r2 = rsq(hidden)
        nh = hidden * r2
        g = GN[r, :]
        SMALL[1:2, :] += jnp.sum(g * nh, axis=0, keepdims=True)
        e = g * gain(gain2)
        gh = DYV[r, :].astype(F32) + r2 * (e - nh * jnp.mean(e * nh, axis=-1, keepdims=True))
        DYV[r, :] = FF[r, :].astype(BF)
        HV[r, :] = gh
        low = gh.astype(BF)
        N2[r, :] = low
        DYT[:, r] = low.T
        x = XV[r, :].astype(F32)
        N2T[:, r] = (x * rsq(x) * gain(gain1)).astype(BF).T
        GN[r, :] = jnp.zeros((TILE, width), F32)
        U[r, 3 * part :] = jnp.zeros((TILE, hid - 3 * part), BF)

    loop(0, tiles, mid)

    GQKV, DO = U, GA
    wide = -(-3 * part // 128) * 128

    def last(p, t):
        r = pl.ds(pl.multiple_of(p * seq + t * TILE, TILE), TILE)
        x = XV[r, :].astype(F32)
        r1 = rsq(x)
        nx = x * r1
        g = GN[r, :]
        SMALL[0:1, :] += jnp.sum(g * nx, axis=0, keepdims=True)
        e = g * gain(gain1)
        XV[r, :] = (HV[r, :] + r1 * (e - nx * jnp.mean(e * nx, axis=-1, keepdims=True))).astype(BF)


    def attn_back_group(i):
        slot = lax.rem(i, 2)
        m = back_group(i)
        done(load_attn(i))
        pl.when(i + 1 < nmp)(lambda: go(load_attn(i + 1)))
        toeplitz(OFFV.at[m], ST)
        D[...] = jnp.zeros_like(D)

        DO[:, :part] = dot(N2[...], BV[slot, :, 3 * part :]).astype(BF)

        def join(p):
            r = tile_rows(p, seq)
            GN[r, :] += dot(GQKV[r, :wide], BV[slot, :, :wide], 1, 1)

            @pl.when(i == nmp - 1)
            def _():
                loop(0, seq // TILE, functools.partial(last, p))
                si.start(p)

        def pair(p):
            pl.when(p > 0)(lambda: join(p - 1))
            base = pl.multiple_of(p * seq, seq)
            off = jnp.where(lens[h.mp * share + p] < seq, -1e30, 0.0).astype(F32)
            run("back", i * share + p, range(1))
            for head in range(heads_mp):
                attend_back(QV.at[slot], ST, DO, LV.at[slot], GQKV, D, head, part, dh, seq, off, base)

        loop(0, share, pair)
        PA.before_group(m, i)
        pl.when((m % 2 != h.c) & (i < 2))(lambda: PI.sib_sent(False))

        PA.put(m, slice(0, 3 * part), dot(N2T[...], GQKV[:, : 3 * part]).astype(BF))
        PA.put(m, slice(3 * part, hid), dot(DYT[...], OV[slot]).astype(BF))
        PA.after_group(m)
        join(share - 1)
        sums = []
        for head in range(heads_mp):
            strip = jnp.concatenate([D[head], jnp.zeros((128, 128), F32)], 1)
            span = strip.shape[1]
            half = 64
            while half:
                strip = strip[:half] + pltpu.roll(strip[half:], span - half, 1)
                half //= 2
            sums.append(strip)
        sums = jnp.concatenate(sums + [jnp.zeros((8 - heads_mp, span), F32)], 0)
        at = pl.ds(pl.multiple_of(m * 128, 128), 128)
        SMALL[8:16, at] = dot(sums, onehot[...], 1, 1, HIGHEST)

    loop(0, nmp, attn_back_group)
    run("end", 0)

    small = [
        remote(SMALL, SR.at[i], ssmall.at[i], rsmall.at[i], who)
        for i, who in enumerate((h.at(c=1 - h.c), h.at(x=1 - h.x), h.at(y=1 - h.y)))
    ]

    def small_step(i):
        small[i].wait()
        SMALL[...] += SR[i]

    small[0].start()
    run("end", 1)
    small_step(0)
    small[1].start()
    run("end", 2)
    small_step(1)
    small[2].start()
    run("end", 3)
    small_step(2)
    SZ[h.z] = SMALL[...]

    def small_z(k, mine):
        z = h.zi(k)
        b = h.z if mine else z
        return remote(SZ.at[b], SZ.at[b], ssmall.at[3 + z], rsmall.at[3 + b], h.at(z=z))

    loop(1, nz, lambda k: small_z(k, True).start())
    run("end", 4)
    loop(1, nz, lambda k: small_z(k, False).wait_recv())
    SMALL[...] = lax.fori_loop(1, nz, lambda z, acc: acc + SZ[z], SZ[0])
    run("end", 5)
    for T in (PA, PI, PO):
        T.result()
        T.sent()
    PA.sib_sent(True)
    PO.sib_sent(False)
    loop(1, nz, lambda k: small_z(k, True).wait_send())
    if A_BY_HOPS:
        A.hops_sent()
    else:
        A.others(lambda z: A.z(z).wait_send())
    for T in (B, C):
        T.others(lambda z: T.z(z).wait_send())
    for T in (A, B, C):
        T.sent()
    for k in range(1, nmp):
        offs(k).wait_send()
    sx.sent()
    sd.sent()
    sl.come()
    sl.sent()
    si.come()
    si.sent()


def layer(tok, cot, ws, table_t, onehot, gain1, gain2, lens, ndp, nmp, fine):
    pairs, positions, width = tok.shape
    rows, part = ws[0].shape
    hid = ws[4].shape[1]
    heads_mp = table_t.shape[0]
    seq = positions * nmp
    share = pairs // nmp
    n = share * seq
    nz = ndp // fine // 2
    any_ = pl.BlockSpec(memory_space=pl.ANY)
    vm = pl.BlockSpec(memory_space=pltpu.VMEM)
    dma = pltpu.SemaphoreType.DMA
    sds = jax.ShapeDtypeStruct
    bf = lambda *s: pltpu.VMEM(s, BF)
    fl = lambda *s: pltpu.VMEM(s, F32)
    act = sds((pairs, positions, width), BF)
    return pl.pallas_call(
        functools.partial(layer_kernel, (ndp, nmp, fine, seq, heads_mp)),
        out_shape=(act, act)
        + (
            sds((3, rows, hid), F32),
            sds((16, width), F32),
            sds((3, nmp // 2, 2, width, hid), BF),
            sds((nmp, n, 3 * part), BF),
            sds((nmp, n, part), BF),
            sds((nmp, 8, n), F32),
        ),
        in_specs=[any_, any_] + [vm] * 10 + [pl.BlockSpec(memory_space=pltpu.SMEM)],
        out_specs=(any_, any_) + (vm,) * 2 + (any_,) * 4,
        scratch_shapes=[
            bf(3, rows, hid),
            fl(nmp, 8, 2 * seq),
            bf(n, width),
            bf(n, width),
            bf(n, width),
            bf(width, n),
            bf(width, n),
            bf(n, hid),
            bf(n, hid),
            fl(n, width),
            fl(n, width),
            fl(n, width),
            bf(2, width, hid),
            bf(2, width, hid),
            bf(2, n, 3 * part),
            bf(2, n, part),
            fl(2, 8, n),
            fl(heads_mp, 128, 2 * seq - 128),
            fl(heads_mp, 128, 2 * seq - 128),
            bf(2, 2, width, hid),
            bf(2, width, hid),
            bf(3, 2, width, hid),
            bf(3, 2, nz, rows, hid),
            bf(3, 2, nz, rows, hid),
            bf(3, rows, hid),
            fl(3, 16, width),
            fl(nz, 16, width),
            dma((3, 8, nz)),
            dma((3, 8, nz)),
        ]
        + [dma((2, nmp, share))] * 4
        + [dma((2, nmp)), dma((3, 2)), dma((2, 2)), dma((3, 2)), dma((3 + nz,)), dma((3 + nz,)), dma((3,))]
        + [dma((3, 2))] * 2
        + [dma((3, 2, nz))] * 4
        + [dma((3, 1))] * 2,
        compiler_params=pltpu.CompilerParams(collective_id=0, has_side_effects=True, vmem_limit_bytes=63 * MIB),
    )(tok, cot, *ws, table_t, onehot, gain1, gain2, lens)


def finish_kernel(heads_mp, L, I, RES, SMALL, L2, I2, GQ, GK, GV, GO, GI, GF, G1, G2, GB, buf, sem):
    come = [pltpu.make_async_copy(a, buf.at[i], sem.at[0, i]) for i, a in enumerate((L, I))]
    go = [pltpu.make_async_copy(buf.at[i], a, sem.at[1, i]) for i, a in enumerate((L2, I2))]
    for cp in come:
        cp.start()
    for before, after in zip(come, go):
        before.wait()
        after.start()
    part = GQ.shape[1]
    GQ[...] = RES[0, :, :part]
    GK[...] = RES[0, :, part : 2 * part]
    GV[...] = RES[0, :, 2 * part : 3 * part]
    GO[...] = RES[0, :, 3 * part :].T
    GI[...] = RES[1]
    GF[...] = RES[2]
    G1[...] = SMALL[0, :]
    G2[...] = SMALL[1, :]
    at = pl.ds(pl.multiple_of(lax.axis_index("mp") * 128, 128), 128)
    GB[...] = SMALL[8:16, at][:heads_mp, : GB.shape[1]]
    for cp in go:
        cp.wait()


def finish(L, I, RES, SMALL, part, heads_mp, buckets):
    _, rows, hid = RES.shape
    width = SMALL.shape[1]
    any_ = pl.BlockSpec(memory_space=pl.ANY)
    vm = pl.BlockSpec(memory_space=pltpu.VMEM)
    sds = jax.ShapeDtypeStruct
    f32 = [(rows, part)] * 3 + [(part, rows), (rows, hid), (rows, hid), (width,), (width,), (heads_mp, buckets)]
    return pl.pallas_call(
        functools.partial(finish_kernel, heads_mp),
        out_shape=(sds(L.shape, BF), sds(I.shape, BF)) + tuple(sds(s, F32) for s in f32),
        in_specs=[any_, any_, vm, vm],
        out_specs=(any_, any_) + (vm,) * len(f32),
        scratch_shapes=[pltpu.VMEM((2,) + L.shape, BF), pltpu.SemaphoreType.DMA((2, 2))],
    )(L, I, RES, SMALL)


def body(tokens, cotangent, lengths, gain_attn, gain_ff, bias_table, w_query, w_key, w_value, w_out_attn, w_in_ff, w_out_ff):
    ndp, nmp = lax.axis_size("dp"), lax.axis_size("mp")
    seq = tokens.shape[1] * nmp
    buckets, heads_mp = bias_table.shape
    fine = 16 // math.gcd(w_query.shape[0], 16)
    groups = [list(range(g, g + fine)) for g in range(0, ndp, fine)]

    def join(a, dim):
        return a if fine == 1 else lax.all_gather(a, "dp", axis=dim, tiled=True, axis_index_groups=groups)

    def split(a, dim):
        if fine == 1:
            return a
        return lax.psum_scatter(a, "dp", scatter_dimension=dim, tiled=True, axis_index_groups=groups)

    dims = (0, 0, 0, 1, 0, 0)
    ws = tuple(join(w, d) for w, d in zip((w_query, w_key, w_value, w_out_attn, w_in_ff, w_out_ff.T), dims))
    place = np.arange(2 * seq)
    place = np.where(place < 2 * seq - 128, seq - 128 - place, seq - 128 + 2 * seq - place)
    onehot = (bucket_of(place, buckets)[None] == np.arange(128)[:, None]).astype(np.float32)
    out, ing, res, small = layer(
        tokens, cotangent, ws, bias_table.T, onehot, gain_attn, gain_ff, lengths, ndp, nmp, fine
    )[:4]
    if fine > 1:
        small = lax.psum(small, "dp", axis_index_groups=groups)
    out, ing, *grads, g1, g2, gb = finish(out, ing, res, small, w_query.shape[1], heads_mp, buckets)
    gq, gk, gv, go, gi, gf = (split(g, d) for g, d in zip(grads, dims))
    return out, ing, g1, g2, gb.T, gq, gk, gv, go, gi, gf.T


def solution(mesh):
    act = P("dp", "mp", None)
    rows, cols = P("dp", "mp"), P("mp", "dp")
    return jax.shard_map(
        body,
        mesh=mesh,
        in_specs=(act, act, P("dp"), P(), P(), P(None, "mp"), rows, rows, rows, cols, rows, cols),
        out_specs=(act, act, P(), P(), P(None, "mp"), rows, rows, rows, cols, rows, cols),
        check_vma=False,
    )
```

time: 1100 us -> 227 us (0.21)
  waiting for transfers between devices: 528 us -> 0 us
  matrix products: 260 us -> 0 us
  Pallas kernels: 0 us -> 226 us
  blocking collectives: 148 us -> 0 us
  other arithmetic: 68.9 us -> 0 us
  local copies, waits for them, and re-layouts: 61.8 us -> 0 us
  between operations: 16.4 us -> 0.82 us
  starting transfers between devices: 11.1 us -> 0 us
    dot_general x69 -> x0, matrix products: 256 us -> none  [the longest x16 34.1 us: masked_scores(): jnp.einsum('qhd,khd->hqk', query, keys, preferred_element_type=jnp.float32)]
    pallas_call x0 -> x2, Pallas kernels: none -> 226 us  [the longest x1 221 us: layer(): pl.pallas_call(functools.partial(layer_kernel, (ndp, nmp, fine, seq, head...]
    unnamed x18 -> x0, waiting for transfers between devices: 191 us -> none
    all_gather x6 -> x0, waiting for transfers between devices: 153 us -> none  [the longest x2 72 us: gather_grads(): return lax.all_gather(x, 'mp', axis=1, tiled=True)]
    reduce_scatter x4 -> x0, waiting for transfers between devices: 151 us -> none  [the longest x2 93.5 us: sum_rows(): lax.psum_scatter(x.astype(jnp.bfloat16), 'mp', scatter_dimension=1, tiled...]
    all_gather x4 -> x0, blocking collectives: 108 us -> none  [the longest x1 27.6 us: body(): lax.all_gather(w_value.astype(bfloat), 'dp', axis=0, tiled=True)]
    psum x1 -> x0, blocking collectives: 39.8 us -> none  [body(): lax.psum((gain_attn_part, gain_ff_part, every_head), ('dp', 'mp'))]
    all_to_all x2 -> x0, waiting for transfers between devices: 32.3 us -> none  [sent_and_summed(): lax.all_to_all(in_blocks(array, dim, length), axis, 0, 0, tiled=True)]
  transfers between devices with their start and end apart: 16 -> 0, of which waited for: 12 -> 0; matrix products, arithmetic and copies ran while one was open for 13% -> 0% of each run, Pallas kernels for 0% -> 0%
where the time goes in v3:
time: 227 us
  Pallas kernels  226 us (100%)
    pallas_call x1, Pallas kernels, layer(): pl.pallas_call(functools.partial(layer_kernel, (ndp, nmp, fine, seq, head...  221 us
    pallas_call x1, Pallas kernels, finish(): pl.pallas_call(functools.partial(finish_kernel, heads_mp), out_shape=(sds...  5.22 us

profile of v3, /device:TPU:1, one launch (start us, length us, event | category | flops | bytes accessed | tf_op | source)
XLA Modules:
  0.0 226.7 jit_solution(18242590060570665499)
XLA Ops:
  0.6 220.6 %shard_map.212 = (bf16[8,128,768]{2,1,0:T(8,128)(2,1)}, bf16[8,128,768]{2,1,0:T(8,128)(2,1)}, f32[3,96,768]{2,1,0:T(8,128)}, f32[16,768]{1,0:T(8,128)}, bf16[3,2...) custom-call(bf16[8,128,768]{2,1,0:T(8,128)(2,1)} %tok.1, ...), custom_call_target="tpu_custom_call" | custom-call | tf_op jit(solution)/shard_map/pallas_call | solution.py:969
  221.3 5.2 %shard_map.213 = (bf16[8,128,768]{2,1,0:T(8,128)(2,1)}, bf16[8,128,768]{2,1,0:T(8,128)(2,1)}, f32[96,192]{1,0:T(8,128)}, f32[96,192]{1,0:T(8,128)}, f32[96,192]{...) custom-call(bf16[8,128,768]{2,1,0:T(8,128)(2,1)} %get-tuple-element., ...), custom_call_target="tpu_custom_call" | custom-call | tf_op jit(solution)/shard_map/pallas_call | solution.py:1052

commit v4 on v3

--- a/solution.py
+++ b/solution.py
@@ -28,34 +28,40 @@
     return (upper + np.where(distance < exact, distance, larger)).astype(np.int32)
 
 PLAN = {
-    ("start", 0): ("C.Y0", "A.X0",),
-    ("start", 1): ("A.plane2",),
-    ("start", 2): ("B.Y0",),
-    ("start", 3): ("B.Zs", "dy",),
-    ("attend", 0): ("A.z2y",),
-    ("attend", 2): ("A.ds", "C.Zs", "B.zy",),
-    ("attend", 3): ("B.Xs",),
-    ("attend", 4): ("C.zy", "B.ys", "C.Xs",),
-    ("attend", 7): ("B.xd", "C.ys", "C.DX",),
-    ("ff", 3): ("C.xd",),
-    ("ff", 4): ("B.ds",),
-    ("ff", 9): ("C.ds",),
+    ("start", 0): ("C.Y0",),
+    ("start", 1): ("A.Xs", "B.Zs", "B.Y0",),
+    ("start", 2): ("B.X0", "C.Zs",),
+    ("start", 3): ("A.DX",),
+    ("attend", 0): ("A.xd",),
+    ("attend", 1): ("dy", "B.zy",),
+    ("attend", 2): ("B.plane2",),
+    ("attend", 3): ("A.ds",),
+    ("attend", 4): ("C.zy",),
+    ("attend", 6): ("C.Xs",),
+    ("attend", 7): ("B.ys",),
+    ("between", 0): ("B.z2y", "C.ys",),
+    ("ff", 4): ("C.DX", "B.ds",),
+    ("ff", 5): ("C.xd",),
+    ("ff", 10): ("C.ds",),
     ("ff", 11): ("PO.sw0",),
-    ("ff", 19): ("PO.yw0",),
-    ("ff", 21): ("PO.sw1", "PI.xs0",),
-    ("back", 0): ("lay", "PO.yw1", "PO.st1",),
-    ("back", 1): ("PO.st0",),
-    ("back", 2): ("PI.xs1", "PI.xw0", "PO.yt0",),
-    ("back", 3): ("PA.st0", "PO.yt1",),
-    ("back", 4): ("PI.xy0", "PA.st1", "PA.yt0",),
-    ("back", 6): ("PI.xw1", "PO.zt0", "PA.yt1",),
-    ("back", 7): ("PI.xy1", "PA.sw0",),
-    ("end", 1): ("PA.yw0",),
-    ("end", 3): ("PO.zw1", "PA.sw1",),
-    ("end", 4): ("PI.zo1",),
-    ("end", 5): ("PI.zo0", "PA.zw0", "PA.zt1", "PO.zt1", "PA.zt0", "PA.yw1", "PO.zw0", "PA.zw1",),
+    ("ff", 19): ("PO.sw1",),
+    ("ff", 20): ("PO.yw0",),
+    ("between", 3): ("PI.xs0", "PO.st0",),
+    ("back", 0): ("PO.yw1", "PI.xs1",),
+    ("back", 1): ("PO.st1", "PO.yt0",),
+    ("back", 2): ("PO.yt1",),
+    ("back", 3): ("PO.zt0", "PI.xw0",),
+    ("back", 4): ("PI.xw1", "PA.st0", "lay",),
+    ("back", 5): ("PI.xy0", "PO.zw1", "PA.st1",),
+    ("back", 6): ("PA.yt0",),
+    ("back", 7): ("PA.sw0", "PI.xy1", "PA.yt1", "PI.zo0",),
+    ("end", 0): ("PO.zw0",),
+    ("end", 1): ("PO.zt1",),
+    ("end", 2): ("PI.zo1",),
+    ("end", 3): ("PA.yw0", "PA.zt1",),
+    ("end", 5): ("PA.zt0", "PA.zw0", "PA.sw1", "PA.yw1", "PA.zw1",),
 }
-MODES = {"A": "plane", "B": "zxy", "C": "half"}
+MODES = {"A": "half", "B": "plane", "C": "half"}
 X_FIRST = {"PA": False, "PI": True, "PO": False}
 A_BY_HOPS = True
 
@@ -121,19 +127,22 @@
     def at(self, x, c, z, y):
         return self.W.at[x, c, self.h.block(z, y)]
 
-    def send(self, src, kind, idx, who, skind=None, sidx=None):
+    def send(self, src, kind, idx, who, skind=None, sidx=0):
         skind = kind if skind is None else skind
-        sidx = idx if sidx is None else sidx
         return remote(src, src, self.ss.at[skind, sidx], self.rs.at[kind, idx], who)
 
+    def wait_sent(self, kind, blocks):
+        src = self.W.at[0, 0, self.h.block(0, 0, blocks)]
+        remote(src, src, self.ss.at[kind, 0], self.rs.at[kind, 0], self.h.at(c=1 - self.h.c)).wait_send()
+
     def hop(self, b, step):
         h = self.h
-        return self.send(self.at(h.x, h.c, b, h.y), 0, b, h.at(z=h.z + step), 0 if step > 0 else 7)
+        return self.send(self.at(h.x, h.c, b, h.y), 0, b, h.at(z=h.z + step), 0 if step > 0 else 7, b)
 
     def z(self, z, mine=True):
         h = self.h
         b = h.z if mine else z
-        return self.send(self.at(h.x, h.c, b, h.y), 0, b, h.at(z=z), sidx=z)
+        return self.send(self.at(h.x, h.c, b, h.y), 0, b, h.at(z=z))
 
     def y(self, z, mine=True):
         h = self.h
@@ -158,7 +167,7 @@
     def z2(self, z, mine=True):
         h = self.h
         b = h.z if mine else z
-        return self.send(self.at(1 - h.x, h.c, b, h.y), 4, b, h.at(z=z), sidx=z)
+        return self.send(self.at(1 - h.x, h.c, b, h.y), 4, b, h.at(z=z))
 
     def sib(self, half, z, mine=True):
         h = self.h
@@ -256,18 +265,19 @@
             "ds": lambda: self.all(ds),
         }
 
-    def sent(self):
-        self.all(lambda z: self.y(z).wait_send())
-        self.all(lambda z: self.sib(0, z).wait_send())
-        self.all(lambda z: self.sib(1, z).wait_send())
+    def sent(self, by_hops=False):
+        nz = self.nz
+        if by_hops:
+            self.hops_sent()
+        else:
+            self.wait_sent(0, nz - 1)
+        self.wait_sent(1, nz)
+        self.wait_sent(2, 1 if self.mode == "plane" else nz)
+        self.wait_sent(3, nz)
         if self.mode == "plane":
-            self.x(self.h.z).wait_send()
-            self.others(lambda z: self.z2(z).wait_send())
-            self.all(lambda z: self.diag_by_y(z).wait_send())
-        else:
-            self.all(lambda z: self.x(z).wait_send())
-            self.all(lambda z: self.by_x(z, lambda: self.diag_by_x(z).wait_send()))
-            self.all(lambda z: self.by_y(z, lambda: self.diag_by_y(z).wait_send()))
+            self.wait_sent(4, nz - 1)
+        self.wait_sent(5, 2 * nz)
+        self.wait_sent(6, 2 * nz)
 
 
 class Swap:
@@ -348,15 +358,15 @@
     def ysend(self, x, z):
         h = self.h
         src = self.MINE.at[x, self.block(z, 1 - h.y)]
-        return remote(src, self.R1.at[x, z], self.sems[2].at[x, z], self.sems[3].at[x, z], h.at(y=1 - h.y))
+        return remote(src, self.R1.at[x, z], self.sems[2].at[x, 0], self.sems[3].at[x, z], h.at(y=1 - h.y))
 
     def zsend(self, x, z):
         h = self.h
-        return remote(self.R1.at[x, z], self.R2.at[x, h.z], self.sems[4].at[x, z], self.sems[5].at[x, h.z], h.at(z=z))
+        return remote(self.R1.at[x, z], self.R2.at[x, h.z], self.sems[4].at[x, 0], self.sems[5].at[x, h.z], h.at(z=z))
 
     def zcome(self, x, z):
         h = self.h
-        return remote(self.R2.at[x, z], self.R2.at[x, z], self.sems[4].at[x, z], self.sems[5].at[x, z], h.at(z=z))
+        return remote(self.R2.at[x, z], self.R2.at[x, z], self.sems[4].at[x, 0], self.sems[5].at[x, z], h.at(z=z))
 
     def xsend(self):
         h = self.h
@@ -368,7 +378,7 @@
         to = h.x if mine else 1 - h.x
         src = self.MINE.at[1 - h.x, self.block(z, h.y if y_is_own else 1 - h.y)]
         dst = (self.R1 if y_is_own else self.R2).at[to, z]
-        return remote(src, dst, self.sems[i].at[1 - h.x, z], self.sems[i + 1].at[to, z], h.at(x=1 - h.x))
+        return remote(src, dst, self.sems[i].at[1 - h.x, 0], self.sems[i + 1].at[to, z], h.at(x=1 - h.x))
 
     def after_group(self, m):
         pl.when(m % 2 != self.h.c)(lambda: self.sib(m // 2).start())
@@ -480,15 +490,19 @@
             self.xsend().wait_recv()
             self.RES[...] += self.R3[...].astype(F32)
 
+    def wait_sent(self, i, x, blocks):
+        src = self.R1.at[x, pl.ds(0, blocks)]
+        remote(src, src, self.sems[i].at[x, 0], self.sems[i + 1].at[x, 0], self.h.at(c=1 - self.h.c)).wait_send()
+
     def sent(self):
         own, other = self.half(True), self.half(False)
-        for x in (own,) if self.x_first else (own, other):
-            self.each(lambda z: self.ysend(x, z).wait_send())
-            self.others(lambda z: self.zsend(x, z).wait_send())
+        self.wait_sent(2, own, self.nz)
+        self.wait_sent(4, own, self.nz - 1)
+        self.wait_sent(2, other, self.nz)
         if self.x_first:
-            self.each(lambda z: self.xall(z, True).wait_send())
-            self.each(lambda z: self.xall(z, False).wait_send())
+            self.wait_sent(4, other, self.nz)
         else:
+            self.wait_sent(4, other, self.nz - 1)
             self.xsend().wait_send()
 
 
@@ -548,7 +562,7 @@
     return a * half, slope
 
 
-def attend_back(QV, ST, DO, LV, GQKV, D, h, part, dh, seq, dead, base):
+def attend_back(QV, ST, DO, LV, DL, GQKV, D, h, part, dh, seq, dead, base):
     rows = pl.ds(base, seq)
     q0, k0, v0 = h * dh, part + h * dh, 2 * part + h * dh
     queries, keys, values = QV[rows, q0 : q0 + dh], QV[rows, k0 : k0 + dh], QV[rows, v0 : v0 + dh]
@@ -556,9 +570,7 @@
     s = biased(dot(keys, queries, 1, 1), ST, h, dead)
     prob = jnp.exp(s - LV[h : h + 1, rows])
     dprob = dot(values, d_o, 1, 1)
-    weighted = prob * dprob
-    delta = jnp.sum(weighted, axis=0, keepdims=True)
-    gs = (weighted - prob * delta).astype(BF)
+    gs = (prob * (dprob - DL[h : h + 1, rows])).astype(BF)
     GQKV[rows, v0 : v0 + dh] = dot(prob.astype(BF), d_o).astype(BF)
     GQKV[rows, k0 : k0 + dh] = dot(gs, queries).astype(BF)
     GQKV[rows, q0 : q0 + dh] = dot(keys.T, gs).astype(BF).T
@@ -574,11 +586,11 @@
 def layer_kernel(cfg, tok, cot, wq, wk, wv, wo, wi, wf_t, table_t, onehot, gain1, gain2, lens, *refs):
     ndp, nmp, fine, seq, heads_mp = cfg
     L, I, RES, SMALL, W, QKV, O, LSE = refs[:8]
-    OWN, OFFV, XV, DYV, N2, N2T, DYT, U, GA, HV, FF, GN, BV, CV, QV, OV, LV, ST, D = refs[8:27]
-    FFMINE, SENT = refs[27:29]
-    bufs, SR, SZ = refs[29:33], refs[33], refs[34]
-    ssem, rsem, xsem, dysem, lsem, isem, bsem, osem, wsem, qsem, ssmall, rsmall, csem = refs[35:48]
-    sems = refs[48:56]
+    OWN, OFFV, XV, DYV, N2, N2T, DYT, U, GA, HV, FF, GN, BV, CV, QV, OV, LV, DL, ST, D = refs[8:28]
+    FFMINE, SENT = refs[28:30]
+    bufs, SR, SZ = refs[30:34], refs[34], refs[35]
+    ssem, rsem, xsem, dysem, lsem, isem, bsem, osem, wsem, qsem, ssmall, rsmall, csem = refs[36:49]
+    sems = refs[49:57]
     rows, part = wq.shape
     h = Place(ndp, nmp, fine, rows)
     h.greet()
@@ -650,6 +662,7 @@
     else:
         ACTIONS["A.Zs"]()
         ACTIONS["A.Y0"]()
+    run("first", 0)
     sx.start_all()
     for k in range(1, nmp):
         offs(k).start()
@@ -663,6 +676,14 @@
     run("start", 2)
     sx.come()
     run("start", 3)
+
+    def norm(t):
+        r = tile_rows(t, TILE)
+        x = XV[r, :].astype(F32)
+        N2[r, :] = (x * rsq(x) * gain(gain1)).astype(BF)
+        HV[r, :] = x
+
+    loop(0, tiles, norm)
     A.sib_wait(0)
 
     def group(i):
@@ -687,14 +708,6 @@
     for k in range(1, nmp):
         offs(k, False).wait_recv()
 
-    def norm(t):
-        r = tile_rows(t, TILE)
-        x = XV[r, :].astype(F32)
-        N2[r, :] = (x * rsq(x) * gain(gain1)).astype(BF)
-        HV[r, :] = x
-
-    loop(0, tiles, norm)
-
     def attn_group(i):
         slot = lax.rem(i, 2)
         m = group(i)
@@ -704,10 +717,10 @@
             A.sib_wait(1)
             load_a(2).start()
 
+        toeplitz(OFFV.at[m], ST)
+        pl.when(i >= 2)(lambda: done(store(i - 2)))
         load_a(i).wait()
         pl.when((i == 0) | (i == 2))(lambda: load_a(i + 1).start())
-        pl.when(i >= 2)(lambda: done(store(i - 2)))
-        toeplitz(OFFV.at[m], ST)
 
         QV[slot] = dot(N2[...], BV[slot, :, : 3 * part]).astype(BF)
 
@@ -845,15 +858,19 @@
         XV[r, :] = (HV[r, :] + r1 * (e - nx * jnp.mean(e * nx, axis=-1, keepdims=True))).astype(BF)
 
 
+    head_of = (lax.broadcasted_iota(jnp.int32, (8, part), 1) // dh == lax.broadcasted_iota(jnp.int32, (8, part), 0)).astype(F32)
+
     def attn_back_group(i):
         slot = lax.rem(i, 2)
         m = back_group(i)
+        toeplitz(OFFV.at[m], ST)
+        D[...] = jnp.zeros_like(D)
         done(load_attn(i))
         pl.when(i + 1 < nmp)(lambda: go(load_attn(i + 1)))
-        toeplitz(OFFV.at[m], ST)
-        D[...] = jnp.zeros_like(D)
-
-        DO[:, :part] = dot(N2[...], BV[slot, :, 3 * part :]).astype(BF)
+
+        d_o = dot(N2[...], BV[slot, :, 3 * part :]).astype(BF)
+        DO[:, :part] = d_o
+        DL[...] = dot(head_of, OV[slot].astype(F32) * d_o.astype(F32), 1, 1, HIGHEST)
 
         def join(p):
             r = tile_rows(p, seq)
@@ -862,7 +879,7 @@
             @pl.when(i == nmp - 1)
             def _():
                 loop(0, seq // TILE, functools.partial(last, p))
-                si.start(p)
+                pl.when(p + 1 < share)(lambda: si.start(p))
 
         def pair(p):
             pl.when(p > 0)(lambda: join(p - 1))
@@ -870,7 +887,7 @@
             off = jnp.where(lens[h.mp * share + p] < seq, -1e30, 0.0).astype(F32)
             run("back", i * share + p, range(1))
             for head in range(heads_mp):
-                attend_back(QV.at[slot], ST, DO, LV.at[slot], GQKV, D, head, part, dh, seq, off, base)
+                attend_back(QV.at[slot], ST, DO, LV.at[slot], DL, GQKV, D, head, part, dh, seq, off, base)
 
         loop(0, share, pair)
         PA.before_group(m, i)
@@ -898,48 +915,70 @@
 
     small = [
         remote(SMALL, SR.at[i], ssmall.at[i], rsmall.at[i], who)
-        for i, who in enumerate((h.at(c=1 - h.c), h.at(x=1 - h.x), h.at(y=1 - h.y)))
+        for i, who in enumerate((h.at(c=1 - h.c), h.at(x=1 - h.x), h.at(y=1 - h.y), h.at(c=1 - h.c)))
     ]
+
+    def small_z(k, mine):
+        z = h.zi(k)
+        b = h.z if mine else z
+        return remote(SZ.at[b], SZ.at[b], ssmall.at[4 + z], rsmall.at[4 + b], h.at(z=z))
 
     def small_step(i):
         small[i].wait()
         SMALL[...] += SR[i]
 
+    def on_core_0(fn):
+        pl.when(h.c == 0)(fn)
+
     small[0].start()
+    small_step(0)
+    on_core_0(lambda: small[1].start())
+    si.start(share - 1)
     run("end", 1)
-    small_step(0)
-    small[1].start()
+
+    @on_core_0
+    def _():
+        small_step(1)
+        small[2].start()
+
     run("end", 2)
-    small_step(1)
-    small[2].start()
+
+    @on_core_0
+    def _():
+        small_step(2)
+        SZ[h.z] = SMALL[...]
+        loop(1, nz, lambda k: small_z(k, True).start())
+
     run("end", 3)
-    small_step(2)
-    SZ[h.z] = SMALL[...]
-
-    def small_z(k, mine):
-        z = h.zi(k)
-        b = h.z if mine else z
-        return remote(SZ.at[b], SZ.at[b], ssmall.at[3 + z], rsmall.at[3 + b], h.at(z=z))
-
-    loop(1, nz, lambda k: small_z(k, True).start())
+
+    @on_core_0
+    def _():
+        loop(1, nz, lambda k: small_z(k, False).wait_recv())
+        SMALL[...] = lax.fori_loop(1, nz, lambda z, acc: acc + SZ[z], SZ[0])
+        small[3].start()
+
     run("end", 4)
-    loop(1, nz, lambda k: small_z(k, False).wait_recv())
-    SMALL[...] = lax.fori_loop(1, nz, lambda z, acc: acc + SZ[z], SZ[0])
+
+    @pl.when(h.c == 1)
+    def _():
+        small[3].wait_recv()
+        SMALL[...] = SR[3]
+
     run("end", 5)
     for T in (PA, PI, PO):
         T.result()
         T.sent()
     PA.sib_sent(True)
     PO.sib_sent(False)
-    loop(1, nz, lambda k: small_z(k, True).wait_send())
-    if A_BY_HOPS:
-        A.hops_sent()
-    else:
-        A.others(lambda z: A.z(z).wait_send())
-    for T in (B, C):
-        T.others(lambda z: T.z(z).wait_send())
-    for T in (A, B, C):
-        T.sent()
+
+    @on_core_0
+    def _():
+        loop(1, nz, lambda k: small_z(k, True).wait_send())
+        small[3].wait_send()
+
+    A.sent(A_BY_HOPS)
+    B.sent()
+    C.sent()
     for k in range(1, nmp):
         offs(k).wait_send()
     sx.sent()
@@ -997,6 +1036,7 @@
             bf(2, n, 3 * part),
             bf(2, n, part),
             fl(2, 8, n),
+            fl(8, n),
             fl(heads_mp, 128, 2 * seq - 128),
             fl(heads_mp, 128, 2 * seq - 128),
             bf(2, 2, width, hid),
@@ -1005,13 +1045,13 @@
             bf(3, 2, nz, rows, hid),
             bf(3, 2, nz, rows, hid),
             bf(3, rows, hid),
-            fl(3, 16, width),
+            fl(4, 16, width),
             fl(nz, 16, width),
             dma((3, 8, nz)),
             dma((3, 8, nz)),
         ]
         + [dma((2, nmp, share))] * 4
-        + [dma((2, nmp)), dma((3, 2)), dma((2, 2)), dma((3, 2)), dma((3 + nz,)), dma((3 + nz,)), dma((3,))]
+        + [dma((2, nmp)), dma((3, 2)), dma((2, 2)), dma((3, 2)), dma((4 + nz,)), dma((4 + nz,)), dma((3,))]
         + [dma((3, 2))] * 2
         + [dma((3, 2, nz))] * 4
         + [dma((3, 1))] * 2,
@@ -1019,14 +1059,19 @@
     )(tok, cot, *ws, table_t, onehot, gain1, gain2, lens)
 
 
-def finish_kernel(heads_mp, L, I, RES, SMALL, L2, I2, GQ, GK, GV, GO, GI, GF, G1, G2, GB, buf, sem):
-    come = [pltpu.make_async_copy(a, buf.at[i], sem.at[0, i]) for i, a in enumerate((L, I))]
+def finish_kernel(heads_mp, L, I, RES_, SMALL_, L2, I2, GQ, GK, GV, GO, GI, GF, G1, G2, GB, buf, RES, SMALL, sem):
+    come = [
+        pltpu.make_async_copy(a, b, sem.at[0, i])
+        for i, (a, b) in enumerate(((L, buf.at[0]), (I, buf.at[1]), (RES_, RES), (SMALL_, SMALL)))
+    ]
     go = [pltpu.make_async_copy(buf.at[i], a, sem.at[1, i]) for i, a in enumerate((L2, I2))]
     for cp in come:
         cp.start()
     for before, after in zip(come, go):
         before.wait()
         after.start()
+    come[2].wait()
+    come[3].wait()
     part = GQ.shape[1]
     GQ[...] = RES[0, :, :part]
     GK[...] = RES[0, :, part : 2 * part]
@@ -1052,9 +1097,14 @@
     return pl.pallas_call(
         functools.partial(finish_kernel, heads_mp),
         out_shape=(sds(L.shape, BF), sds(I.shape, BF)) + tuple(sds(s, F32) for s in f32),
-        in_specs=[any_, any_, vm, vm],
+        in_specs=[any_] * 4,
         out_specs=(any_, any_) + (vm,) * len(f32),
-        scratch_shapes=[pltpu.VMEM((2,) + L.shape, BF), pltpu.SemaphoreType.DMA((2, 2))],
+        scratch_shapes=[
+            pltpu.VMEM((2,) + L.shape, BF),
+            pltpu.VMEM(RES.shape, F32),
+            pltpu.VMEM(SMALL.shape, F32),
+            pltpu.SemaphoreType.DMA((2, 4)),
+        ],
     )(L, I, RES, SMALL)
 
 

time: 227 us -> 213 us (0.938)
  Pallas kernels: 226 us -> 212 us
    pallas_call x1, Pallas kernels: 221 us -> 208 us  [layer(): pl.pallas_call(functools.partial(layer_kernel, (ndp, nmp, fine, seq, head...]
where the time goes in v4:
time: 213 us; the launch traced here: 212 us
  Pallas kernels  212 us (100%)
    pallas_call x1, Pallas kernels, layer(): pl.pallas_call(functools.partial(layer_kernel, (ndp, nmp, fine, seq, head...  208 us

profile of v4, /device:TPU:1, one launch (start us, length us, event | category | flops | bytes accessed | tf_op | source)
XLA Modules:
  0.0 212.5 jit_solution(6369936302754403578)
XLA Ops:
  0.6 207.6 %shard_map.212 = (bf16[8,128,768]{2,1,0:T(8,128)(2,1)}, bf16[8,128,768]{2,1,0:T(8,128)(2,1)}, f32[3,96,768]{2,1,0:T(8,128)}, f32[16,768]{1,0:T(8,128)}, bf16[3,2...) custom-call(bf16[8,128,768]{2,1,0:T(8,128)(2,1)} %tok.1, ...), custom_call_target="tpu_custom_call" | custom-call | tf_op jit(solution)/shard_map/pallas_call | solution.py:1008
  208.2 4.1 %shard_map.213 = (bf16[8,128,768]{2,1,0:T(8,128)(2,1)}, bf16[8,128,768]{2,1,0:T(8,128)(2,1)}, f32[96,192]{1,0:T(8,128)}, f32[96,192]{1,0:T(8,128)}, f32[96,192]{...) custom-call(bf16[8,128,768]{2,1,0:T(8,128)(2,1)} %get-tuple-element., ...), custom_call_target="tpu_custom_call" | custom-call | tf_op jit(solution)/shard_map/pallas_call | solution.py:1097

commit v5 on v4

--- a/solution.py
+++ b/solution.py
@@ -28,40 +28,37 @@
     return (upper + np.where(distance < exact, distance, larger)).astype(np.int32)
 
 PLAN = {
-    ("start", 0): ("C.Y0",),
-    ("start", 1): ("A.Xs", "B.Zs", "B.Y0",),
-    ("start", 2): ("B.X0", "C.Zs",),
-    ("start", 3): ("A.DX",),
-    ("attend", 0): ("A.xd",),
-    ("attend", 1): ("dy", "B.zy",),
-    ("attend", 2): ("B.plane2",),
-    ("attend", 3): ("A.ds",),
-    ("attend", 4): ("C.zy",),
-    ("attend", 6): ("C.Xs",),
-    ("attend", 7): ("B.ys",),
-    ("between", 0): ("B.z2y", "C.ys",),
-    ("ff", 4): ("C.DX", "B.ds",),
-    ("ff", 5): ("C.xd",),
-    ("ff", 10): ("C.ds",),
-    ("ff", 11): ("PO.sw0",),
-    ("ff", 19): ("PO.sw1",),
-    ("ff", 20): ("PO.yw0",),
-    ("between", 3): ("PI.xs0", "PO.st0",),
-    ("back", 0): ("PO.yw1", "PI.xs1",),
-    ("back", 1): ("PO.st1", "PO.yt0",),
-    ("back", 2): ("PO.yt1",),
-    ("back", 3): ("PO.zt0", "PI.xw0",),
-    ("back", 4): ("PI.xw1", "PA.st0", "lay",),
-    ("back", 5): ("PI.xy0", "PO.zw1", "PA.st1",),
-    ("back", 6): ("PA.yt0",),
-    ("back", 7): ("PA.sw0", "PI.xy1", "PA.yt1", "PI.zo0",),
-    ("end", 0): ("PO.zw0",),
-    ("end", 1): ("PO.zt1",),
-    ("end", 2): ("PI.zo1",),
-    ("end", 3): ("PA.yw0", "PA.zt1",),
-    ("end", 5): ("PA.zt0", "PA.zw0", "PA.sw1", "PA.yw1", "PA.zw1",),
+    ("first", 0): ("B.Y0",),
+    ("start", 1): ("B.Zs", "A.Xs",),
+    ("start", 2): ("A.DX", "C.Zs",),
+    ("start", 3): ("C.Y0",),
+    ("attend", 0): ("C.X0",),
+    ("attend", 1): ("A.xd",),
+    ("attend", 2): ("B.zy", "dy", "A.ds",),
+    ("attend", 4): ("C.zy", "C.plane2",),
+    ("attend", 6): ("B.ys", "B.Xs",),
+    ("between", 0): ("C.ys",),
+    ("ff", 0): ("C.z2y",),
+    ("ff", 6): ("B.DX", "B.xd",),
+    ("ff", 8): ("C.ds",),
+    ("ff", 11): ("B.ds", "PO.sw0",),
+    ("ff", 15): ("PO.sw1",),
+    ("ff", 21): ("PO.yw1",),
+    ("ff", 23): ("PO.st0",),
+    ("between", 3): ("PI.xs0", "PO.yw0",),
+    ("back", 0): ("PO.st1",),
+    ("back", 1): ("PI.xs1", "PO.yt0", "lay",),
+    ("back", 2): ("PO.yt1", "PI.xw0", "PA.st0",),
+    ("back", 4): ("PA.st1", "PI.xy0",),
+    ("back", 5): ("PA.yt0", "PI.xw1", "PO.zt0",),
+    ("back", 6): ("PA.sw0", "PA.yt1",),
+    ("back", 7): ("PA.zt0", "PI.xy1",),
+    ("end", 0): ("PA.zt1", "PO.zt1", "PA.yw0",),
+    ("end", 3): ("PA.zw0", "PA.sw1", "PA.yw1",),
+    ("end", 4): ("PI.zo1", "PO.zw1", "PO.zw0",),
+    ("end", 5): ("PI.zo0", "PA.zw1",),
 }
-MODES = {"A": "half", "B": "plane", "C": "half"}
+MODES = {"A": "half", "B": "half", "C": "plane"}
 X_FIRST = {"PA": False, "PI": True, "PO": False}
 A_BY_HOPS = True
 

time: 213 us -> 202 us (0.948)
  Pallas kernels: 212 us -> 201 us
    pallas_call x1, Pallas kernels: 208 us -> 196 us  [layer(): pl.pallas_call(functools.partial(layer_kernel, (ndp, nmp, fine, seq, head...]
where the time goes in v5:
time: 202 us; the launch traced here: 201 us
  Pallas kernels  201 us (100%)
    pallas_call x1, Pallas kernels, layer(): pl.pallas_call(functools.partial(layer_kernel, (ndp, nmp, fine, seq, head...  196 us
    pallas_call x1, Pallas kernels, finish(): pl.pallas_call(functools.partial(finish_kernel, heads_mp), out_shape=(sds...  4.09 us

profile of v5, /device:TPU:1, one launch (start us, length us, event | category | flops | bytes accessed | tf_op | source)
XLA Modules:
  0.0 201.4 jit_solution(4118042313396364188)
XLA Ops:
  0.6 196.5 %shard_map.212 = (bf16[8,128,768]{2,1,0:T(8,128)(2,1)}, bf16[8,128,768]{2,1,0:T(8,128)(2,1)}, f32[3,96,768]{2,1,0:T(8,128)}, f32[16,768]{1,0:T(8,128)}, bf16[3,2...) custom-call(bf16[8,128,768]{2,1,0:T(8,128)(2,1)} %tok.1, ...), custom_call_target="tpu_custom_call" | custom-call | tf_op jit(solution)/shard_map/pallas_call | solution.py:1005
  197.1 4.1 %shard_map.213 = (bf16[8,128,768]{2,1,0:T(8,128)(2,1)}, bf16[8,128,768]{2,1,0:T(8,128)(2,1)}, f32[96,192]{1,0:T(8,128)}, f32[96,192]{1,0:T(8,128)}, f32[96,192]{...) custom-call(bf16[8,128,768]{2,1,0:T(8,128)(2,1)} %get-tuple-element., ...), custom_call_target="tpu_custom_call" | custom-call | tf_op jit(solution)/shard_map/pallas_call | solution.py:1094

commit v6 on v5

--- a/solution.py
+++ b/solution.py
@@ -928,51 +928,6 @@
         pl.when(h.c == 0)(fn)
 
     small[0].start()
-    small_step(0)
-    on_core_0(lambda: small[1].start())
-    si.start(share - 1)
-    run("end", 1)
-
-    @on_core_0
-    def _():
-        small_step(1)
-        small[2].start()
-
-    run("end", 2)
-
-    @on_core_0
-    def _():
-        small_step(2)
-        SZ[h.z] = SMALL[...]
-        loop(1, nz, lambda k: small_z(k, True).start())
-
-    run("end", 3)
-
-    @on_core_0
-    def _():
-        loop(1, nz, lambda k: small_z(k, False).wait_recv())
-        SMALL[...] = lax.fori_loop(1, nz, lambda z, acc: acc + SZ[z], SZ[0])
-        small[3].start()
-
-    run("end", 4)
-
-    @pl.when(h.c == 1)
-    def _():
-        small[3].wait_recv()
-        SMALL[...] = SR[3]
-
-    run("end", 5)
-    for T in (PA, PI, PO):
-        T.result()
-        T.sent()
-    PA.sib_sent(True)
-    PO.sib_sent(False)
-
-    @on_core_0
-    def _():
-        loop(1, nz, lambda k: small_z(k, True).wait_send())
-        small[3].wait_send()
-
     A.sent(A_BY_HOPS)
     B.sent()
     C.sent()
@@ -982,6 +937,51 @@
     sd.sent()
     sl.come()
     sl.sent()
+    small_step(0)
+    on_core_0(lambda: small[1].start())
+    si.start(share - 1)
+    run("end", 1)
+
+    @on_core_0
+    def _():
+        small_step(1)
+        small[2].start()
+
+    run("end", 2)
+
+    @on_core_0
+    def _():
+        small_step(2)
+        SZ[h.z] = SMALL[...]
+        loop(1, nz, lambda k: small_z(k, True).start())
+
+    run("end", 3)
+
+    @on_core_0
+    def _():
+        loop(1, nz, lambda k: small_z(k, False).wait_recv())
+        SMALL[...] = lax.fori_loop(1, nz, lambda z, acc: acc + SZ[z], SZ[0])
+        small[3].start()
+
+    run("end", 4)
+
+    @pl.when(h.c == 1)
+    def _():
+        small[3].wait_recv()
+        SMALL[...] = SR[3]
+
+    run("end", 5)
+    for T in (PA, PI, PO):
+        T.result()
+        T.sent()
+    PA.sib_sent(True)
+    PO.sib_sent(False)
+
+    @on_core_0
+    def _():
+        loop(1, nz, lambda k: small_z(k, True).wait_send())
+        small[3].wait_send()
+
     si.come()
     si.sent()
 

time: 202 us -> 202 us (level)
  no operation moved by 1% of the time
where the time goes in v6:
time: 202 us; the launch traced here: 201 us
  Pallas kernels  200 us (99%)
    pallas_call x1, Pallas kernels, layer(): pl.pallas_call(functools.partial(layer_kernel, (ndp, nmp, fine, seq, head...  196 us
    pallas_call x1, Pallas kernels, finish(): pl.pallas_call(functools.partial(finish_kernel, heads_mp), out_shape=(sds...  4.09 us

profile of v6, /device:TPU:1, one launch (start us, length us, event | category | flops | bytes accessed | tf_op | source)
XLA Modules:
  0.0 201.3 jit_solution(10955709329109957089)
XLA Ops:
  0.6 196.4 %shard_map.212 = (bf16[8,128,768]{2,1,0:T(8,128)(2,1)}, bf16[8,128,768]{2,1,0:T(8,128)(2,1)}, f32[3,96,768]{2,1,0:T(8,128)}, f32[16,768]{1,0:T(8,128)}, bf16[3,2...) custom-call(bf16[8,128,768]{2,1,0:T(8,128)(2,1)} %tok.1, ...), custom_call_target="tpu_custom_call" | custom-call | tf_op jit(solution)/shard_map/pallas_call | solution.py:1005
  197.0 4.1 %shard_map.213 = (bf16[8,128,768]{2,1,0:T(8,128)(2,1)}, bf16[8,128,768]{2,1,0:T(8,128)(2,1)}, f32[96,192]{1,0:T(8,128)}, f32[96,192]{1,0:T(8,128)}, f32[96,192]{...) custom-call(bf16[8,128,768]{2,1,0:T(8,128)(2,1)} %get-tuple-element., ...), custom_call_target="tpu_custom_call" | custom-call | tf_op jit(solution)/shard_map/pallas_call | solution.py:1094
